TPU v7x, 32 devices: a whole 2x2x4 slice. The times are simulated.
32 devices in a mesh: grp: 2 (over y), voc: 8 (over z, x), tok: 2 (over core).
Axes of the slice: x: 2, y: 2, z: 4, core: 2. Of those that a mesh axis runs over, the one named last changes fastest.
Arguments:
- target_hidden: bfloat16 [3072, 4096], P(('grp', 'tok'), 'voc'), parts along dimension 0, may hold values from -16 to 16
- draft_hidden: bfloat16 [3072, 896], P(('grp', 'tok'), 'voc'), parts along dimension 0, may hold values from -16 to 16
- target_head: bfloat16 [4096, 10240], P(None, 'voc'), may hold values from -1 to 1
- draft_head: bfloat16 [896, 10240], P('tok', 'voc'), may hold values from -1 to 1
Outputs:
- row_loss: float32 [3072], P(('grp', 'tok')), parts along dimension 0
- draft_grad: bfloat16 [1792, 10240], P(('grp', 'tok'), 'voc'), parts along dimension 0
There are 2 independent parts, one for each index of `grp`. A program takes and returns all parts, laid end to end along the dimension named above; an argument that names none is the same for every part. Nothing has to cross between parts.
All inputs are finite; a program needn't handle non-finite values.
Results may differ from a plain program's by a relative error of at most 0.0085.
Values may be sent and summed in bfloat16 or wider, within the bound.
No kernel may reach another device: no remote copies, remote signals or barrier semaphores. Data moves between devices by JAX's collectives and lax.ppermute only.
A program may use at most 128 MiB of HBM per device.

v0:
```python
import jax
import jax.numpy as jnp
from jax import lax
from jax.sharding import PartitionSpec as P


def body(target_hidden, draft_hidden, target_head, draft_head):
    rows = target_hidden.shape[0]
    vocab_local = target_head.shape[1]
    full = float(vocab_local * lax.axis_size("voc"))
    tokens_all = float(rows * lax.axis_size("tok"))
    draft_weights = lax.all_gather(draft_head, "tok", axis=0, tiled=True)
    target_logits = jnp.dot(
        lax.all_gather(target_hidden, "voc", axis=1, tiled=True),
        target_head,
        preferred_element_type=jnp.float32,
    )
    draft_features = lax.all_gather(draft_hidden, "voc", axis=1, tiled=True)
    draft_logits = jnp.dot(draft_features, draft_weights, preferred_element_type=jnp.float32)
    local_top_target = jnp.max(target_logits, axis=1)
    local_top_draft = jnp.max(draft_logits, axis=1)
    top_target, top_draft = lax.pmax((local_top_target, local_top_draft), "voc")
    target_exp = jnp.exp(target_logits - top_target[:, None])
    draft_exp = jnp.exp(draft_logits - top_draft[:, None])
    total_target, total_draft = lax.psum(
        (jnp.sum(target_exp, axis=1), jnp.sum(draft_exp, axis=1)), "voc"
    )
    target_prob = target_exp / total_target[:, None]
    draft_prob = draft_exp / total_draft[:, None]
    spread = full * (draft_prob - target_prob)
    root = jnp.sqrt(spread * spread + 1.0)
    slope = spread / root
    loss_part = jnp.sum(root - 1.0, axis=1) / (2.0 * full)
    inner_part = jnp.sum(draft_prob * slope, axis=1)
    row_loss, inner = lax.psum((loss_part, inner_part), "voc")
    logit_grad = (full * draft_prob * (slope - inner[:, None])).astype(jnp.bfloat16)
    summed = lax.dot_general(
        draft_features, logit_grad, (((0,), (0,)), ((), ())), preferred_element_type=jnp.float32
    )
    draft_grad = lax.psum_scatter(
        (summed / tokens_all).astype(jnp.bfloat16), "tok", scatter_dimension=0, tiled=True
    )
    return (row_loss, draft_grad)


def solution(mesh):
    return jax.shard_map(
        body,
        mesh=mesh,
        in_specs=(
            P(("grp", "tok"), "voc"),
            P(("grp", "tok"), "voc"),
            P(None, "voc"),
            P("tok", "voc"),
        ),
        out_specs=(P(("grp", "tok")), P(("grp", "tok"), "voc")),
        check_vma=False,
    )
```

profile of v0, /device:TPU:0, one launch (start us, length us, event | category | flops | bytes accessed | tf_op | source)
XLA Modules:
  0.0 276.8 jit_solution(4728855652593725857)
XLA Ops:
  7.2 0.0 all-gather.6.cloned.1.call-start
  7.2 0.7 all-gather.6.cloned.1.call-update
  7.9 0.0 all-gather.4.cloned.1.call-start
  7.9 0.7 all-gather.4.cloned.1.call-update
  8.6 0.0 all-gather.8.cloned.1.call-start
  8.7 0.7 all-gather.8.cloned.1.call-update
  9.4 0.0 reduce-scatter.4.cloned.1.call-start
  9.4 13.7 %all-gather.6.cloned.1.call-done = bf16[896,1280]{1,0:T(8,128)(2,1)} async-done(((bf16[448,1280]{1,0:T(8,128)(2,1)}), bf16[896,1280]{1,0:T(8,128)(2,1)}) %all-gather.6.cloned.1.call-update) | async-done | bytes 2293776 | tf_op jit(solution)/shard_map/all_gather | solution.py:12
  23.1 45.7 %all-gather.4.cloned.1.call-done = bf16[768,896]{0,1:T(8,128)(2,1)} async-done(((bf16[768,112]{0,1:T(8,128)(2,1)}), bf16[768,896]{0,1:T(8,128)(2,1)}) %all-gather.4.cloned.1.call-update) | async-done | bytes 1376272 | tf_op jit(solution)/shard_map/all_gather | solution.py:18
  68.8 6.3 %fusion.12 = (f32[768]{0:T(1024)S(1)}, f32[768,1280]{1,0:T(8,128)}) fusion(bf16[768,896]{0,1:T(8,128)(2,1)} %all-gather.4.cloned.1.call-done, bf16[896,1280]{1,0:T(8,128)(2,1)} %all-gather.6.cloned.1.call-done), kind=kOutput, calls=%fused_computation.19 | convolution fusion | flops 1762589952 | bytes 7605248 | tf_op jit(solution)/shard_map/dot_general | solution.py:19
  75.1 94.3 %all-gather.8.cloned.1.call-done = bf16[768,4096]{1,0:T(8,128)(2,1)} async-done(((bf16[768,512]{1,0:T(8,128)(2,1)}), bf16[768,4096]{1,0:T(8,128)(2,1)}) %all-gather.8.cloned.1.call-update) | async-done | bytes 6291472 | tf_op jit(solution)/shard_map/all_gather | solution.py:14
  169.4 14.8 %fusion.11 = (f32[768]{0:T(1024)S(1)}, f32[768,1280]{1,0:T(8,128)}) fusion(bf16[768,4096]{1,0:T(8,128)(2,1)} %all-gather.8.cloned.1.call-done, bf16[4096,1280]{1,0:T(8,128)(2,1)} %param.6), kind=kOutput, calls=%fused_computation.18 | convolution fusion | flops 8054045696 | bytes 20712448 | tf_op jit(solution)/shard_map/dot_general | solution.py:13
  184.2 18.8 %all-reduce.2 = (f32[768]{0:T(1024)S(1)}, f32[768]{0:T(1024)S(1)}) all-reduce(f32[768]{0:T(1024)S(1)} %get-tuple-element.15, f32[768]{0:T(1024)S(1)} %get-tuple-element.17), channel_id=1, replica_groups=mesh['grp'=2,'voc'=8,'tok'=2] {'voc'}, use_global_device_ids=true, to_apply=%region_5.0 | all-reduce | flops 1536 | bytes 12288 | tf_op jit(solution)/shard_map/pmax | solution.py:22
  203.0 4.6 %fusion.2 = (f32[768]{0:T(1024)S(1)}, f32[768]{0:T(1024)S(1)}) fusion(f32[768,1280]{1,0:T(8,128)} %get-tuple-element.18, f32[768]{0:T(1024)S(1)} %get-tuple-element.13, f32[768,1280]{1,0:T(8,128)} %get-tuple-element.16, f32[768]{0:T(1024)S(1)} %get-tuple-element.12), kind=kLoop, calls=%fused_computation.10 | loop fusion | flops 3930624 | bytes 7876608 | tf_op jit(solution)/shard_map/reduce_sum | solution.py:26
  207.6 17.9 %all-reduce.1 = (f32[768]{0:T(1024)S(1)}, f32[768]{0:T(1024)S(1)}) all-reduce(f32[768]{0:T(1024)S(1)} %get-tuple-element.20, f32[768]{0:T(1024)S(1)} %get-tuple-element.19), channel_id=1, replica_groups=mesh['grp'=2,'voc'=8,'tok'=2] {'voc'}, use_global_device_ids=true, to_apply=%region_7.0 | all-reduce | flops 1536 | bytes 12288 | tf_op jit(solution)/shard_map/psum | solution.py:25
  225.6 7.5 %multiply_reduce_fusion = (f32[768]{0:T(1024)S(1)}, f32[768]{0:T(1024)S(1)}, f32[768,1280]{1,0:T(8,128)}) fusion(f32[768]{0:T(1024)S(1)} %get-tuple-element.11, f32[768,1280]{1,0:T(8,128)} %get-tuple-element.18, f32[768]{0:T(1024)S(1)} %get-tuple-element.13, f32[768]{0:T(1024)S(1)} %get-tuple-element.10, f32[768,1280]{1,0:T(8,128)} %get-tuple-element.16, ...), kind=kLoop, calls=%fused_computation.2 | loop fusion | flops 12777984 | bytes 11814912 | tf_op jit(solution)/shard_map/reduce_sum | solution.py:34
  233.0 19.4 %all-reduce = (f32[768]{0:T(1024)}, f32[768]{0:T(1024)S(1)}) all-reduce(f32[768]{0:T(1024)S(1)} %broadcast_multiply_fusion, f32[768]{0:T(1024)S(1)} %get-tuple-element.6), channel_id=1, replica_groups=mesh['grp'=2,'voc'=8,'tok'=2] {'voc'}, use_global_device_ids=true, to_apply=%region_9.0 | all-reduce | flops 1536 | bytes 12288 | tf_op jit(solution)/shard_map/psum | solution.py:35
  252.4 8.0 %fusion.4 = bf16[896,1280]{0,1:T(8,128)(2,1)S(1)} fusion(bf16[768,896]{0,1:T(8,128)(2,1)} %all-gather.4.cloned.1.call-done, f32[768]{0:T(1024)S(1)} %get-tuple-element.9, f32[768,1280]{1,0:T(8,128)} %get-tuple-element.14, f32[768,1280]{1,0:T(8,128)} %get-tuple-element.18, f32[768]{0:T(1024)S(1)} %get-tuple-element.11, f32[768]{0:T(1024)S(1)} %get-tuple-element.13), kind=kOutput, calls=%fused_computation.12 | convolution fusion | flops 1772748800 | bytes 11543552 | tf_op jit(solution)/shard_map/dot_general | solution.py:37
  260.4 2.5 copy.8
  263.0 0.0 reduce-scatter.4.cloned.1.call-update
  263.0 7.2 %reduce-scatter.4.cloned.1.call-done = bf16[448,1280]{1,0:T(8,128)(2,1)} async-done(((bf16[896,1280]{1,0:T(8,128)(2,1)}), bf16[448,1280]{1,0:T(8,128)(2,1)}) %reduce-scatter.4.cloned.1.call-update) | async-done | bytes 1146896
  (1 shorter events, 0.0 us)
Async XLA Ops:
  7.2 16.0 %all-gather.6.cloned.1.call-start = ((), (), s32[]{:S(2)}) async-start(), calls=%async_computation.2 | async-start | bytes 3440640 | tf_op jit(solution)/shard_map/all_gather | solution.py:12
  7.9 60.9 %all-gather.4.cloned.1.call-start = ((), (), s32[]{:S(2)}) async-start(), calls=%async_computation.1 | async-start | bytes 1548288 | tf_op jit(solution)/shard_map/all_gather | solution.py:18
  8.6 160.8 %all-gather.8.cloned.1.call-start = ((), (), s32[]{:S(2)}) async-start(), calls=%async_computation.3 | async-start | bytes 7077888 | tf_op jit(solution)/shard_map/all_gather | solution.py:14
  9.4 260.8 %reduce-scatter.4.cloned.1.call-start = ((), (), s32[]{:S(2)}) async-start(), calls=%async_computation.4 | async-start | bytes 3440640
Sparse Core Ops, SparseCore 0:
  9.5 13.5 all-gather.5
  25.3 43.4 all-gather.3
  70.9 98.4 all-gather.7
  263.1 7.0 reduce-scatter.3
where the time goes:
time: 277 us
  waiting for transfers between devices  163 us (59%)
  blocking collectives  56.1 us (20%)
  matrix products  29 us (10%)
  between operations  13.8 us (5%)
  other arithmetic  12.1 us (4%)
    all_gather x1, waiting for transfers between devices, body(): lax.all_gather(target_hidden, 'voc', axis=1, tiled=True)  94.3 us
    all_gather x1, waiting for transfers between devices, body(): draft_features = lax.all_gather(draft_hidden, 'voc', axis=1, tiled=True)  45.7 us
    psum x1, blocking collectives, body(): row_loss, inner = lax.psum((loss_part, inner_part), 'voc')  19.4 us
    pmax x1, blocking collectives, body(): top_target, top_draft = lax.pmax((local_top_target, local_top_draft), 'voc')  18.8 us
    psum x1, blocking collectives, body(): lax.psum((jnp.sum(target_exp, axis=1), jnp.sum(draft_exp, axis=1)), 'voc')  17.9 us
    dot_general x1, matrix products, body(): jnp.dot(lax.all_gather(target_hidden, 'voc', axis=1, tiled=True), target_...  14.8 us
    all_gather x1, waiting for transfers between devices, body(): draft_weights = lax.all_gather(draft_head, 'tok', axis=0, tiled=True)  13.7 us
    unnamed x5, waiting for transfers between devices  9.31 us
  transfers between devices with their start and end apart: 4, of which 4 were waited for; matrix products, arithmetic and copies ran while one was open for 2% of the time, Pallas kernels for 0%

commit v1 on v0

v1 whole, which is shorter than its diff:
```python
import functools

import jax
import jax.numpy as jnp
from jax import lax
from jax.experimental import pallas as pl
from jax.experimental.pallas import tpu as pltpu
from jax.sharding import PartitionSpec as P

F32, BF16 = jnp.float32, jnp.bfloat16
VMEM_BYTES = 48 * 2**20
LANES = 128


def _eye(n):
    return lax.broadcasted_iota(jnp.int32, (n, n), 0) == lax.broadcasted_iota(jnp.int32, (n, n), 1)


def _to_row(eye, column):
    return jnp.sum(jnp.where(eye, column, 0.0), axis=0, keepdims=True)


def _to_column(eye, row):
    return jnp.sum(jnp.where(eye, row, 0.0), axis=1, keepdims=True)


def _dot(a, b):
    return jnp.dot(a, b, preferred_element_type=F32)


def _products(xs, wts, wds, feats):
    target = _dot(xs[0][:, :feats], wts[0][...])
    for x, w in zip(xs[1:], wts[1:], strict=True):
        target += _dot(x[:, :feats], w[...])
    draft = _dot(
        jnp.concatenate([x[:, feats:] for x in xs], axis=1),
        jnp.concatenate([w[...] for w in wds], axis=0),
    )
    return target, draft


def _near_kernel(feats, perm, x0, x1, x2, x3, w0, w1, w2, w3, d0, d1, d2, d3, acc_t, acc_d):
    target, draft = _products((x0, x1, x2, x3), (w0, w1, w2, w3), (d0, d1, d2, d3), feats)
    acc_t[...] = target
    acc_d[...] = draft


def _near(perm, own, p1, o, a, wt, wd, half, tile, feats):
    half_rows, width = p1.shape
    vocab = wt.shape[1]
    steps = half_rows // tile
    piece = lambda off: pl.BlockSpec((tile, width), lambda i, p: (i + off, 0))
    w_spec = lambda k: pl.BlockSpec((feats, vocab), lambda i, p: (p[k], 0))
    d_spec = lambda k: pl.BlockSpec((width - feats, vocab), lambda i, p: (p[k], 0))
    out = pl.BlockSpec((tile, vocab), lambda i, p: (i, 0))
    return pl.pallas_call(
        functools.partial(_near_kernel, feats),
        grid_spec=pltpu.PrefetchScalarGridSpec(
            num_scalar_prefetch=1,
            grid=(steps,),
            in_specs=[piece(half * steps), piece(0), piece(0), piece(0)]
            + [w_spec(k) for k in range(4)]
            + [d_spec(k) for k in range(4)],
            out_specs=[out, out],
        ),
        out_shape=[jax.ShapeDtypeStruct((half_rows, vocab), F32)] * 2,
        compiler_params=pltpu.CompilerParams(vmem_limit_bytes=VMEM_BYTES),
        cost_estimate=pl.CostEstimate(
            flops=2 * half_rows * 4 * width * vocab,
            bytes_accessed=8 * width * vocab + 8 * half_rows * vocab + 8 * half_rows * width,
            transcendentals=0,
        ),
        name="near_logits",
    )(perm, own, p1, o, a, *[wt] * 4, *[wd] * 4)


def _far_kernel(feats, chunk, first, perm, *refs):
    xs, wts, wds, (in_t, in_d) = refs[0:4], refs[4:8], refs[8:12], refs[12:14]
    refs = refs[14 if first else 16 :]
    stats_in = None if first else refs[0]
    e_t, e_d, stats = refs[0 if first else 1 :]
    j, steps = pl.program_id(0), pl.num_programs(0)
    rows, cols = in_t.shape
    target, draft = _products(xs, wts, wds, feats)
    here = pl.ds(pl.multiple_of(j * cols, cols), cols)
    e_t[:, here] = target + in_t[...]
    e_d[:, here] = draft + in_d[...]

    @pl.when(j == steps - 1)
    def _():
        eye = _eye(rows)
        if first:
            stats[...] = jnp.zeros_like(stats)
        else:
            stats[...] = stats_in[...]
        for kind, ref in enumerate((e_t, e_d)):
            logits = ref[...]
            top = jnp.max(logits, axis=1, keepdims=True)
            e = jnp.exp(logits - top)
            ref[...] = e
            row = 2 * chunk + kind
            stats[0, row : row + 1, :] = _to_row(eye, top)
            stats[1, row : row + 1, :] = _to_row(eye, jnp.sum(e, axis=1, keepdims=True))


def _far(perm, far, f, wt, wd, acc, prev, chunk, chunks, feats, cols):
    rows2, width = far.shape
    rows, vocab = rows2 // 2, wt.shape[1]
    first = prev is None
    piece = lambda half: pl.BlockSpec((rows, width), lambda j, p: (half, 0))
    w_spec = lambda k: pl.BlockSpec((feats, cols), lambda j, p: (p[k], j))
    d_spec = lambda k: pl.BlockSpec((width - feats, cols), lambda j, p: (p[k], j))
    in_half = chunk % (acc[0].shape[0] // rows)
    acc_spec = pl.BlockSpec((rows, cols), lambda j, p: (in_half, j))
    e_spec = pl.BlockSpec((rows, vocab), lambda j, p: (chunk, 0))
    s_spec = pl.BlockSpec((2, 2 * chunks, rows), lambda j, p: (0, 0, 0))
    anywhere = pl.BlockSpec(memory_space=pl.ANY)
    return pl.pallas_call(
        functools.partial(_far_kernel, feats, chunk, first),
        grid_spec=pltpu.PrefetchScalarGridSpec(
            num_scalar_prefetch=1,
            grid=(vocab // cols,),
            in_specs=[piece(0), piece(1), piece(0), piece(1)]
            + [w_spec(k) for k in range(4, 8)]
            + [d_spec(k) for k in range(4, 8)]
            + [acc_spec, acc_spec]
            + ([] if first else [anywhere, anywhere, s_spec]),
            out_specs=[e_spec, e_spec, s_spec],
        ),
        out_shape=[jax.ShapeDtypeStruct((chunks * rows, vocab), F32)] * 2
        + [jax.ShapeDtypeStruct((2, 2 * chunks, rows), F32)],
        input_output_aliases={} if first else {15: 0, 16: 1},
        compiler_params=pltpu.CompilerParams(vmem_limit_bytes=VMEM_BYTES),
        cost_estimate=pl.CostEstimate(
            flops=2 * rows * 4 * width * vocab,
            bytes_accessed=8 * width * vocab + 16 * rows * vocab + 8 * rows * width,
            transcendentals=2 * rows * vocab,
        ),
        name="far_logits",
    )(perm, far, far, f, f, *[wt] * 4, *[wd] * 4, *acc, *(() if first else prev))


def _slope_kernel(full, e_t, e_d, mine, total, slope_out, scaled_out, sums):
    i = pl.program_id(0)
    rows = e_t.shape[0]
    eye = _eye(rows)

    def scale(kind):
        row = pl.ds(2 * i + kind, 1)
        return _to_column(eye, jnp.exp(mine[0, row, :] - total[0, row, :]) / total[1, row, :])

    target = e_t[...] * (scale(0) * full)
    draft = e_d[...] * (scale(1) * full)
    spread = draft - target
    square = spread * spread + 1.0
    inverse = lax.rsqrt(square)
    slope = spread * inverse
    slope_out[...] = slope
    scaled_out[...] = draft
    loss = jnp.sum(square * inverse - 1.0, axis=1, keepdims=True) * (1.0 / (2.0 * full))
    inner = jnp.sum(draft * slope, axis=1, keepdims=True) * (1.0 / full)
    sums[pl.ds(2 * i, 1), :] = _to_row(eye, loss)
    sums[pl.ds(2 * i + 1, 1), :] = _to_row(eye, inner)


def _slopes(e_t, e_d, mine, total, chunks, full):
    rows_all, vocab = e_t.shape
    rows = rows_all // chunks
    block = pl.BlockSpec((rows, vocab), lambda i: (i, 0))
    whole = pl.BlockSpec(mine.shape, lambda i: (0, 0, 0))
    return pl.pallas_call(
        functools.partial(_slope_kernel, full),
        grid=(chunks,),
        in_specs=[block, block, whole, whole],
        out_specs=[block, block, pl.BlockSpec((2 * chunks, rows), lambda i: (0, 0))],
        out_shape=[jax.ShapeDtypeStruct((rows_all, vocab), F32)] * 2
        + [jax.ShapeDtypeStruct((2 * chunks, rows), F32)],
        input_output_aliases={0: 0, 1: 1},
        compiler_params=pltpu.CompilerParams(vmem_limit_bytes=VMEM_BYTES),
        cost_estimate=pl.CostEstimate(
            flops=12 * rows_all * vocab, bytes_accessed=16 * rows_all * vocab, transcendentals=rows_all * vocab
        ),
        name="slopes",
    )(e_t, e_d, mine, total)


def _turn_kernel(chunks, perm, own, p1a, p1b, oa, ob, aa, ab, *refs):
    fars, fs, out = refs[:chunks], refs[chunks : 2 * chunks], refs[2 * chunks]
    half = p1a.shape[0]
    rows = fars[0].shape[0] // 2

    def put(k, start, value):
        place = pl.ds(pl.multiple_of(perm[k] * LANES, LANES), LANES)
        out[place, start : start + value.shape[0]] = jnp.transpose(value)

    put(0, 0, own[...])
    for k, pair in enumerate(((p1a, p1b), (oa, ob), (aa, ab))):
        put(k + 1, 0, pair[0][...])
        put(k + 1, half, pair[1][...])
    for k, parts in ((4, fars), (6, fs)):
        for c in range(chunks):
            put(k, c * rows, parts[c][:rows, :])
            put(k + 1, c * rows, parts[c][rows:, :])


def _turn(perm, own, halves, fars, fs, feats):
    rows_all = own.shape[0]
    column = feats // LANES
    spec = lambda x: pl.BlockSpec((x.shape[0], LANES), lambda i, p: (0, column))
    arrays = [own, *halves, *fars, *fs]
    return pl.pallas_call(
        functools.partial(_turn_kernel, len(fars)),
        grid_spec=pltpu.PrefetchScalarGridSpec(
            num_scalar_prefetch=1,
            grid=(1,),
            in_specs=[spec(x) for x in arrays],
            out_specs=pl.BlockSpec((8 * LANES, rows_all), lambda i, p: (0, 0)),
        ),
        out_shape=jax.ShapeDtypeStruct((8 * LANES, rows_all), BF16),
        compiler_params=pltpu.CompilerParams(vmem_limit_bytes=VMEM_BYTES),
        cost_estimate=pl.CostEstimate(
            flops=16 * LANES * rows_all, bytes_accessed=32 * LANES * rows_all, transcendentals=0
        ),
        name="turned_features",
    )(perm, *arrays)


def _send_kernel(chunks, tokens, tok, features, slope, scaled, inner, grad_out, part_out, column):
    rows = inner.shape[1]

    @pl.when(pl.program_id(0) == 0)
    def _():
        eye = _eye(rows)
        for c in range(chunks):
            column[c * rows : (c + 1) * rows, :] = _to_column(eye, inner[2 * c + 1 : 2 * c + 2, :])

    grad = (scaled[...] * (slope[...] - column[...])).astype(BF16)
    grad_out[...] = grad
    part_out[...] = (_dot(features[...], grad) * (1.0 / tokens)).astype(part_out.dtype)


def _send(tok, features, slope, scaled, inner, chunks, tokens, cols):
    rows_all, vocab = slope.shape
    half = features.shape[0] // 2
    block = pl.BlockSpec((rows_all, cols), lambda j, t: (0, j))
    return pl.pallas_call(
        functools.partial(_send_kernel, chunks, tokens),
        grid_spec=pltpu.PrefetchScalarGridSpec(
            num_scalar_prefetch=1,
            grid=(vocab // cols,),
            in_specs=[
                pl.BlockSpec((half, rows_all), lambda j, t: (1 - t[0], 0)),
                block,
                block,
                pl.BlockSpec(inner.shape, lambda j, t: (0, 0)),
            ],
            out_specs=[block, pl.BlockSpec((half, cols), lambda j, t: (0, j))],
            scratch_shapes=[pltpu.VMEM((rows_all, 1), F32)],
        ),
        out_shape=[
            jax.ShapeDtypeStruct((rows_all, vocab), BF16),
            jax.ShapeDtypeStruct((half, vocab), BF16),
        ],
        compiler_params=pltpu.CompilerParams(vmem_limit_bytes=VMEM_BYTES),
        cost_estimate=pl.CostEstimate(
            flops=2 * half * rows_all * vocab,
            bytes_accessed=10 * rows_all * vocab + 2 * half * (vocab + rows_all),
            transcendentals=0,
        ),
        name="gradient_to_send",
    )(tok, features, slope, scaled, inner)


def _keep_kernel(tokens, tok, features, grad, out):
    out[...] = _dot(features[...], grad[...]) * (1.0 / tokens)


def _keep(tok, features, grad, tokens, cols):
    rows_all, vocab = grad.shape
    half = features.shape[0] // 2
    return pl.pallas_call(
        functools.partial(_keep_kernel, tokens),
        grid_spec=pltpu.PrefetchScalarGridSpec(
            num_scalar_prefetch=1,
            grid=(vocab // cols,),
            in_specs=[
                pl.BlockSpec((half, rows_all), lambda j, t: (t[0], 0)),
                pl.BlockSpec((rows_all, cols), lambda j, t: (0, j)),
            ],
            out_specs=pl.BlockSpec((half, cols), lambda j, t: (0, j)),
        ),
        out_shape=jax.ShapeDtypeStruct((half, vocab), F32),
        compiler_params=pltpu.CompilerParams(vmem_limit_bytes=VMEM_BYTES),
        cost_estimate=pl.CostEstimate(
            flops=2 * half * rows_all * vocab,
            bytes_accessed=2 * rows_all * vocab + 2 * half * rows_all + 4 * half * vocab,
            transcendentals=0,
        ),
        name="gradient_to_keep",
    )(tok, features, grad)


class _Slots:
    def __init__(self):
        self.before, self.last, self.now = [], [], []

    def next(self):
        self.before, self.last, self.now = self.last, self.now, []

    def move(self, x, pairs):
        if self.before:
            x = lax.optimization_barrier((x, *self.before))[0]
        y = lax.ppermute(x, "voc", pairs)
        self.now.append(y)
        return y


def _xor(k):
    return [(i, i ^ k) for i in range(8)]


MIDDLE = [(2, 4), (4, 2), (3, 5), (5, 3)]
OUTWARD = [(2, 0), (3, 1), (4, 6), (5, 7)]


def _gather(own, z):
    rows = own.shape[0] // 4
    end = (z == 0) | (z == 3)
    slots = _Slots()
    halves = [own[: 2 * rows], own[2 * rows :]]
    p1, o, a, middle, outward, far, f = [], [], [], [], [], [], []

    def near(c):
        start = (c % 2) * rows
        return jnp.concatenate([h[start : start + rows] for h in (halves[c // 2], p1[c // 2])])

    for slot in range(8):
        if slot < 2:
            p1.append(slots.move(halves[slot], _xor(2)))
            o.append(slots.move(halves[slot], _xor(1)))
        elif slot < 4:
            a.append(slots.move(p1[slot - 2], _xor(1)))
        if 2 <= slot < 6:
            outward.append(slots.move(middle[slot - 2], OUTWARD))
        if 1 <= slot < 5:
            middle.append(slots.move(near(slot - 1), MIDDLE))
        if slot >= 4:
            c = slot - 4
            far.append(jnp.where(end, outward[c], middle[c]))
            f.append(slots.move(far[c], _xor(1)))
        slots.next()
    return p1, o, a, far, f


def _all_reduce(x, merge):
    for k in (1, 2, 4):
        x = merge(x, lax.ppermute(x, "voc", _xor(k)))
    return x


def _merge_softmax(a, b):
    top = jnp.maximum(a[0], b[0])
    return jnp.stack([top, a[1] * jnp.exp(a[0] - top) + b[1] * jnp.exp(b[0] - top)])


def _body_4x2(target_hidden, draft_hidden, target_head, draft_head):
    rows_all, feats = target_hidden.shape
    draft_feats = draft_hidden.shape[1]
    vocab = target_head.shape[1]
    chunks, cols = 4, 256
    rows = rows_all // chunks
    full = float(vocab * lax.axis_size("voc"))
    tokens = float(rows_all * lax.axis_size("tok"))
    me, tok = lax.axis_index("voc"), lax.axis_index("tok")
    z, x = me // 2, me % 2

    far_z = jnp.where(z < 2, jnp.array([2, 3]), jnp.array([1, 0]))
    perm = jnp.stack(
        [me, me ^ 2, me ^ 1, me ^ 3]
        + [far_z[0] * 2 + x, far_z[1] * 2 + x, far_z[0] * 2 + 1 - x, far_z[1] * 2 + 1 - x]
    ).astype(jnp.int32)
    tok_index = tok.reshape(1).astype(jnp.int32)

    own = jnp.concatenate(
        [target_hidden, jnp.pad(draft_hidden, ((0, 0), (0, LANES - draft_feats)))], axis=1
    )
    p1, o, a, far, f = _gather(own, z)

    other_head = lax.ppermute(draft_head, "tok", [(0, 1), (1, 0)])
    head = jnp.where(tok == 0, jnp.stack([draft_head, other_head]), jnp.stack([other_head, draft_head]))
    head = jnp.pad(head.reshape(8, draft_feats, vocab), ((0, 0), (0, LANES - draft_feats), (0, 0)))
    head = head.reshape(8 * LANES, vocab)

    acc = [_near(perm, own, p1[h], o[h], a[h], target_head, head, h, rows, feats) for h in range(2)]
    state = None
    for c in range(chunks):
        state = _far(perm, far[c], f[c], target_head, head, acc[c // 2], state, c, chunks, feats, cols)
    e_t, e_d, mine = state
    total = _all_reduce(mine, _merge_softmax)
    slope, scaled, sums = _slopes(e_t, e_d, mine, total, chunks, full)
    features = _turn(perm, own, [*p1, *o, *a], far, f, feats)
    sums = _all_reduce(sums, jnp.add)
    row_loss = sums.reshape(chunks, 2, rows)[:, 0].reshape(rows_all)
    grad, send = _send(tok_index, features, slope, scaled, sums, chunks, tokens, cols)
    received = lax.ppermute(send, "tok", [(0, 1), (1, 0)])
    keep = _keep(tok_index, features, grad, tokens, cols)
    draft_grad = (keep + received.astype(F32)).astype(BF16)
    draft_grad = draft_grad.reshape(4, LANES, vocab)[:, :draft_feats].reshape(4 * draft_feats, vocab)
    return row_loss, draft_grad


def _body_any(target_hidden, draft_hidden, target_head, draft_head):
    rows, vocab = target_hidden.shape[0], target_head.shape[1]
    full = float(vocab * lax.axis_size("voc"))
    tokens = float(rows * lax.axis_size("tok"))
    draft_weights = lax.all_gather(draft_head, "tok", axis=0, tiled=True)
    hidden = lax.all_gather(target_hidden, "voc", axis=1, tiled=True)
    target_logits = jnp.dot(hidden, target_head, preferred_element_type=F32)
    features = lax.all_gather(draft_hidden, "voc", axis=1, tiled=True)
    draft_logits = jnp.dot(features, draft_weights, preferred_element_type=F32)
    top_t, top_d = lax.pmax((jnp.max(target_logits, axis=1), jnp.max(draft_logits, axis=1)), "voc")
    target_exp = jnp.exp(target_logits - top_t[:, None])
    draft_exp = jnp.exp(draft_logits - top_d[:, None])
    total_t, total_d = lax.psum((jnp.sum(target_exp, axis=1), jnp.sum(draft_exp, axis=1)), "voc")
    target_prob = target_exp / total_t[:, None]
    draft_prob = draft_exp / total_d[:, None]
    spread = full * (draft_prob - target_prob)
    root = jnp.sqrt(spread * spread + 1.0)
    slope = spread / root
    loss = jnp.sum(root - 1.0, axis=1) / (2.0 * full)
    row_loss, inner = lax.psum((loss, jnp.sum(draft_prob * slope, axis=1)), "voc")
    logit_grad = (full * draft_prob * (slope - inner[:, None])).astype(BF16)
    summed = lax.dot_general(features, logit_grad, (((0,), (0,)), ((), ())), preferred_element_type=F32)
    draft_grad = lax.psum_scatter((summed / tokens).astype(BF16), "tok", scatter_dimension=0, tiled=True)
    return row_loss, draft_grad


def solution(mesh):
    body = _body_4x2 if (mesh.shape["voc"], mesh.shape["tok"]) == (8, 2) else _body_any
    return jax.shard_map(
        body,
        mesh=mesh,
        in_specs=(
            P(("grp", "tok"), "voc"),
            P(("grp", "tok"), "voc"),
            P(None, "voc"),
            P("tok", "voc"),
        ),
        out_specs=(P(("grp", "tok")), P(("grp", "tok"), "voc")),
        check_vma=False,
    )
```

time: 277 us -> 180 us (0.65)
  waiting for transfers between devices: 163 us -> 57 us
  Pallas kernels: 0 us -> 63.9 us
  blocking collectives: 56.1 us -> 0 us
  starting transfers between devices: 0.15 us -> 37.3 us
  matrix products: 29 us -> 0 us
  between operations: 13.8 us -> 2.3 us
  local copies, waits for them, and re-layouts: 2.54 us -> 12.1 us
  other arithmetic: 12.1 us -> 6.28 us
    all_gather x3 -> x0, waiting for transfers between devices: 154 us -> none  [the longest x1 94.3 us: body(): lax.all_gather(target_hidden, 'voc', axis=1, tiled=True)]
    pallas_call x0 -> x10, Pallas kernels: none -> 63.9 us  [the longest x4 30.4 us: _far(): pl.pallas_call(functools.partial(_far_kernel, feats, chunk, first), grid_...]
    ppermute x0 -> x26, waiting for transfers between devices: none -> 57 us  [the longest x18 46 us: move(): y = lax.ppermute(x, 'voc', pairs)]
    ppermute x0 -> x26, starting transfers between devices: none -> 37.3 us  [the longest x6 18.7 us: _all_reduce(): x = merge(x, lax.ppermute(x, 'voc', _xor(k)))]
    psum x2 -> x0, blocking collectives: 37.3 us -> none  [the longest x1 19.4 us: body(): row_loss, inner = lax.psum((loss_part, inner_part), 'voc')]
    dot_general x3 -> x0, matrix products: 29 us -> none  [the longest x1 14.8 us: body(): jnp.dot(lax.all_gather(target_hidden, 'voc', axis=1, tiled=True), target_...]
    pmax x1 -> x0, blocking collectives: 18.8 us -> none  [body(): top_target, top_draft = lax.pmax((local_top_target, local_top_draft), 'voc')]
    reduce_sum x2 -> x0, other arithmetic: 12.1 us -> none  [the longest x1 7.47 us: body(): inner_part = jnp.sum(draft_prob * slope, axis=1)]
  transfers between devices with their start and end apart: 4 -> 26, of which waited for: 4 -> 13; matrix products, arithmetic and copies ran while one was open for 2% -> 4% of each run, Pallas kernels for 0% -> 24%
where the time goes in v1:
time: 180 us; the launch traced here: 179 us
  Pallas kernels  63.9 us (36%)
  waiting for transfers between devices  57 us (32%)
  starting transfers between devices  37.3 us (21%)
  local copies, waits for them, and re-layouts  12.1 us (7%)
  other arithmetic  6.28 us (3%)
  between operations  2.3 us (1%)
    ppermute x18, waiting for transfers between devices, move(): y = lax.ppermute(x, 'voc', pairs)  46 us
    pallas_call x4, Pallas kernels, _far(): pl.pallas_call(functools.partial(_far_kernel, feats, chunk, first), grid_...  30.4 us
    ppermute x6, starting transfers between devices, _all_reduce(): x = merge(x, lax.ppermute(x, 'voc', _xor(k)))  18.7 us
    ppermute x18, starting transfers between devices, move(): y = lax.ppermute(x, 'voc', pairs)  18.6 us
    pallas_call x2, Pallas kernels, _near(): pl.pallas_call(functools.partial(_near_kernel, feats), grid_spec=pltpu.Pr...  14.8 us
    ppermute x6, waiting for transfers between devices, _all_reduce(): x = merge(x, lax.ppermute(x, 'voc', _xor(k)))  10.5 us
    pallas_call x1, Pallas kernels, _send(): pl.pallas_call(functools.partial(_send_kernel, chunks, tokens), grid_spec...  6.99 us
    unnamed x41, local copies, waits for them, and re-layouts  6.56 us
  transfers between devices with their start and end apart: 26, of which 13 were waited for; matrix products, arithmetic and copies ran while one was open for 4% of the time, Pallas kernels for 24%

profile of v1, /device:TPU:0, one launch (start us, length us, event | category | flops | bytes accessed | tf_op | source)
XLA Modules:
  0.0 178.9 jit_solution(18002506619751826890)
XLA Ops:
  4.1 3.0 %collective-permute-start.1 = (bf16[384,640]{1,0:T(8,128)(2,1)}, bf16[384,640]{1,0:T(8,128)(2,1)S(1)}, u32[]{:S(2)}, u32[]{:S(2)}) collective-permute-start(bf16[384,640]{1,0:T(8,128)(2,1)} %get-tuple-element.78), channel_id=1, source_target_pairs={{0,4},{2,6},{4,0},{6,2},{8,12},{10,14},{12,8},{14,10},{1,5},{3,7},... | collective-permute-start | bytes 1474568 | tf_op jit(solution)/shard_map/ppermute | solution.py:313
  11.2 8.2 %collective-permute-done.1.x1.p1a = bf16[384,640]{1,0:T(8,128)(2,1)S(1)} collective-permute-done((bf16[384,640]{1,0:T(8,128)(2,1)}, bf16[384,640]{1,0:T(8,128)(2,1)S(1)}, u32[]{:S(2)}, u32[]{:S(2)}) %collective-permute-start.1) | collective-permute-done | bytes 491552 | tf_op jit(solution)/shard_map/ppermute | solution.py:313
  22.2 6.9 %collective-permute-done.x1.p1b = bf16[384,640]{1,0:T(8,128)(2,1)S(1)} collective-permute-done((bf16[384,640]{1,0:T(8,128)(2,1)}, bf16[384,640]{1,0:T(8,128)(2,1)S(1)}, u32[]{:S(2)}, u32[]{:S(2)}) %collective-permute-start) | collective-permute-done | bytes 491552 | tf_op jit(solution)/shard_map/ppermute | solution.py:313
  34.7 2.9 %maximum_select_fusion = bf16[2,448,1280]{2,1,0:T(8,128)(2,1)S(1)} fusion(bf16[1,448,1280]{2,1,0:T(8,128)(2,1)} %bitcast.11, bf16[1,448,1280]{2,1,0:T(8,128)(2,1)} %bitcast.10, pred[]{:T(512)S(6)} %eq.13), kind=kLoop, calls=%fused_computation.1 | loop fusion | flops 3440640 | bytes 4587521 | tf_op jit(solution)/shard_map/jit(_where)/select_n | solution.py:390
  39.4 3.9 %collective-permute-done.3.x3.aa = bf16[384,640]{1,0:T(8,128)(2,1)S(1)} collective-permute-done((bf16[384,640]{1,0:T(8,128)(2,1)S(1)}, bf16[384,640]{1,0:T(8,128)(2,1)S(1)}, u32[]{:S(2)}, u32[]{:S(2)}) %collective-permute-start.3) | collective-permute-done | bytes 491552 | tf_op jit(solution)/shard_map/ppermute | solution.py:313
  43.3 4.1 %collective-permute-done.5 = bf16[384,640]{1,0:T(8,128)(2,1)S(1)} collective-permute-done((bf16[384,640]{1,0:T(8,128)(2,1)S(1)}, bf16[384,640]{1,0:T(8,128)(2,1)S(1)}, u32[]{:S(2)}, u32[]{:S(2)}) %collective-permute-start.5) | collective-permute-done | bytes 491552 | tf_op jit(solution)/shard_map/ppermute | solution.py:313
  48.1 7.4 %near_logits.3 = (f32[384,1280]{1,0:T(8,128)S(1)}, f32[384,1280]{1,0:T(8,128)}) custom-call(s32[8]{0:T(128)S(1)} %stack.64.perm, bf16[768,640]{1,0:T(8,128)(2,1)S(1)} %fusion.1.x0.own, bf16[384,640]{1,0:T(8,128)(2,1)S(1)} %collective-permute-done.1.x1.p1a, bf16[384,640]{1,0:T(8,128)(2,1)S(1)} %collective-permute-done.2.x2.oa, ...), custom_call_target="tpu_custom_call" | custom-call | flops 2516582400 | bytes 12451840 | tf_op jit(solution)/shard_map/near_logits/pallas_call | solution.py:56
  60.6 17.1 %collective-permute-done.16 = bf16[384,640]{1,0:T(8,128)(2,1)S(1)} collective-permute-done((bf16[384,640]{1,0:T(8,128)(2,1)S(1)}, bf16[384,640]{1,0:T(8,128)(2,1)S(1)}, u32[]{:S(2)}, u32[]{:S(2)}) %collective-permute-start.16) | collective-permute-done | bytes 491552 | tf_op jit(solution)/shard_map/ppermute | solution.py:313
  78.3 4.6 %collective-permute-done.12 = bf16[384,640]{1,0:T(8,128)(2,1)S(1)} collective-permute-done((bf16[384,640]{1,0:T(8,128)(2,1)S(1)}, bf16[384,640]{1,0:T(8,128)(2,1)S(1)}, u32[]{:S(2)}, u32[]{:S(2)}) %collective-permute-start.12) | collective-permute-done | bytes 491552 | tf_op jit(solution)/shard_map/ppermute | solution.py:313
  83.6 7.4 %near_logits.2 = (f32[384,1280]{1,0:T(8,128)S(1)}, f32[384,1280]{1,0:T(8,128)}) custom-call(s32[8]{0:T(128)S(1)} %stack.64.perm, bf16[768,640]{1,0:T(8,128)(2,1)S(1)} %fusion.1.x0.own, bf16[384,640]{1,0:T(8,128)(2,1)S(1)} %collective-permute-done.x1.p1b, bf16[384,640]{1,0:T(8,128)(2,1)S(1)} %copy-done.12, bf16[384,640]{1,0:T(8,128)(2,1)S(1)} %collective-permute-done.9.x3.ab, ...), custom_call_target="tpu_custom_call" | custom-call | flops 2516582400 | bytes 12451840 | tf_op jit(solution)/shard_map/near_logits/pallas_call | solution.py:56
  91.0 7.6 %far_logits.4 = (f32[768,1280]{1,0:T(8,128)}, f32[768,1280]{1,0:T(8,128)}, f32[2,8,192]{2,1,0:T(8,128)S(1)}) custom-call(s32[8]{0:T(128)S(1)} %stack.64.perm, bf16[384,640]{1,0:T(8,128)(2,1)S(1)} %broadcast_select_fusion.refs_0_.refs_1_, bf16[384,640]{1,0:T(8,128)(2,1)S(1)} %broadcast_select_fusion.refs_0_.refs_1_, ...), custom_call_target="tpu_custom_call" | custom-call | flops 1258291200 | bytes 11468800 | tf_op jit(solution)/shard_map/far_logits/pallas_call | solution.py:118
  98.6 7.5 %far_logits.5 = (f32[768,1280]{1,0:T(8,128)}, f32[768,1280]{1,0:T(8,128)}, f32[2,8,192]{2,1,0:T(8,128)S(1)}) custom-call(s32[8]{0:T(128)S(1)} %stack.64.perm, bf16[384,640]{1,0:T(8,128)(2,1)S(1)} %broadcast_select_fusion.2.refs_0_.refs_1_, ...), custom_call_target="tpu_custom_call", output_to_operand_aliasing={{0}: (15, {}), {1}: (16, {})} | custom-call | flops 1258291200 | bytes 11468800 | tf_op jit(solution)/shard_map/far_logits/pallas_call | solution.py:118
  106.2 7.5 %far_logits.6 = (f32[768,1280]{1,0:T(8,128)}, f32[768,1280]{1,0:T(8,128)}, f32[2,8,192]{2,1,0:T(8,128)S(1)}) custom-call(s32[8]{0:T(128)S(1)} %stack.64.perm, bf16[384,640]{1,0:T(8,128)(2,1)S(1)} %broadcast_select_fusion.1.refs_0_.refs_1_.refs_2_, ...), custom_call_target="tpu_custom_call", output_to_operand_aliasing={{0}: (15, {}), {1}: (16, {})} | custom-call | flops 1258291200 | bytes 11468800 | tf_op jit(solution)/shard_map/far_logits/pallas_call | solution.py:118
  113.8 7.7 %far_logits.7 = (f32[768,1280]{1,0:T(8,128)}, f32[768,1280]{1,0:T(8,128)}, f32[2,8,192]{2,1,0:T(8,128)S(1)}) custom-call(s32[8]{0:T(128)S(1)} %stack.64.perm, bf16[384,640]{1,0:T(8,128)(2,1)S(1)} %broadcast_select_fusion.3.refs_0_.refs_1_.refs_3_, ...), custom_call_target="tpu_custom_call", output_to_operand_aliasing={{0}: (15, {}), {1}: (16, {})} | custom-call | flops 1258291200 | bytes 11468800 | tf_op jit(solution)/shard_map/far_logits/pallas_call | solution.py:118
  123.0 2.2 %collective-permute-done.19 = f32[2,8,192]{2,1,0:T(8,128)S(1)} collective-permute-done((f32[2,8,192]{2,1,0:T(8,128)S(1)}, f32[2,8,192]{2,1,0:T(8,128)S(1)}, u32[]{:S(2)}, u32[]{:S(2)}) %collective-permute-start.19) | collective-permute-done | bytes 12320 | tf_op jit(solution)/shard_map/ppermute | solution.py:357
  125.3 9.8 %collective-permute-start.20 = (f32[2,8,192]{2,1,0:T(8,128)S(1)}, f32[2,8,192]{2,1,0:T(8,128)S(1)}, u32[]{:S(2)}, u32[]{:S(2)}) collective-permute-start(f32[2,8,192]{2,1,0:T(8,128)S(1)} %pad_maximum_fusion.4), channel_id=1, source_target_pairs={{0,4},{2,6},{4,0},{6,2},{8,12},{10,14},{12,8},{14,10},{1,5},{3,7},... | collective-permute-start | bytes 36872 | tf_op jit(solution)/shard_map/ppermute | solution.py:357
  138.8 2.7 %collective-permute-done.21 = f32[2,8,192]{2,1,0:T(8,128)S(1)} collective-permute-done((f32[2,8,192]{2,1,0:T(8,128)S(1)}, f32[2,8,192]{2,1,0:T(8,128)S(1)}, u32[]{:S(2)}, u32[]{:S(2)}) %collective-permute-start.21) | collective-permute-done | bytes 12320 | tf_op jit(solution)/shard_map/ppermute | solution.py:357
  141.6 2.1 %copy-done = f32[768,1280]{1,0:T(8,128)S(1)} copy-done((f32[768,1280]{1,0:T(8,128)S(1)}, f32[768,1280]{1,0:T(8,128)}, u32[]{:S(2)}) %copy-start) | copy-done | bytes 3932184
  143.7 6.0 %slopes.1 = (f32[768,1280]{1,0:T(8,128)S(1)}, f32[768,1280]{1,0:T(8,128)}, f32[8,192]{1,0:T(8,128)S(1)}) custom-call(f32[768,1280]{1,0:T(8,128)S(1)} %copy-done, f32[768,1280]{1,0:T(8,128)} %get-tuple-element.63.e_d, f32[2,8,192]{2,1,0:T(8,128)S(1)} %get-tuple-element.64.mine, ...), custom_call_target="tpu_custom_call", output_to_operand_aliasing={{0}: (0, {}), {1}: (1, {})} | custom-call | flops 11796480 | bytes 15728640 | tf_op jit(solution)/shard_map/slopes/pallas_call | solution.py:171
  153.1 2.2 %collective-permute-done.22 = f32[8,192]{1,0:T(8,128)S(1)} collective-permute-done((f32[8,192]{1,0:T(8,128)S(1)}, f32[8,192]{1,0:T(8,128)S(1)}, u32[]{:S(2)}, u32[]{:S(2)}) %collective-permute-start.22) | collective-permute-done | bytes 6176 | tf_op jit(solution)/shard_map/ppermute | solution.py:357
  155.2 2.0 %collective-permute-start.23 = (f32[8,192]{1,0:T(8,128)S(1)}, f32[8,192]{1,0:T(8,128)S(1)}, u32[]{:S(2)}, u32[]{:S(2)}) collective-permute-start(f32[8,192]{1,0:T(8,128)S(1)} %add.56), channel_id=1, source_target_pairs={{0,4},{2,6},{4,0},{6,2},{8,12},{10,14},{12,8},{14,10},{1,5},{3,7},... | collective-permute-start | bytes 18440 | tf_op jit(solution)/shard_map/ppermute | solution.py:357
  160.8 3.6 %turned_features.1.features = bf16[1024,768]{1,0:T(8,128)(2,1)} custom-call(s32[8]{0:T(128)S(1)} %stack.64.perm, bf16[768,640]{1,0:T(8,128)(2,1)} %copy-done.2, bf16[384,640]{1,0:T(8,128)(2,1)S(1)} %collective-permute-done.1.x1.p1a, bf16[384,640]{1,0:T(8,128)(2,1)S(1)} %collective-permute-done.x1.p1b, bf16[384,640]{1,0:T(8,128)(2,1)S(1)} %copy-done.10, ...), custom_call_target="tpu_custom_call" | custom-call | flops 1572864 | bytes 3145728 | tf_op jit(solution)/shard_map/turned_features/pallas_call | solution.py:211
  165.8 7.0 %gradient_to_send.1 = (bf16[768,1280]{1,0:T(8,128)(2,1)S(1)}, bf16[512,1280]{1,0:T(8,128)(2,1)}) custom-call(s32[1]{0:T(128)} %bitcast.14.tok, bf16[1024,768]{1,0:T(8,128)(2,1)S(1)} %copy-done.3, f32[768,1280]{1,0:T(8,128)} %copy-done.1, f32[768,1280]{1,0:T(8,128)} %get-tuple-element.67.scaled, f32[8,192]{1,0:T(8,128)S(1)} %add.58.inner), custom_call_target="tpu_custom_call" | custom-call | flops 1006632960 | bytes 11927552 | tf_op jit(solution)/shard_map/gradient_to_send/pallas_call | solution.py:246
  173.5 2.2 %gradient_to_keep.1 = f32[512,1280]{1,0:T(8,128)S(1)} custom-call(s32[1]{0:T(128)} %bitcast.14.tok, bf16[1024,768]{1,0:T(8,128)(2,1)S(1)} %copy-done.4, bf16[768,1280]{1,0:T(8,128)(2,1)S(1)} %get-tuple-element.68.grad), custom_call_target="tpu_custom_call" | custom-call | flops 1006632960 | bytes 5373952 | tf_op jit(solution)/shard_map/gradient_to_keep/pallas_call | solution.py:281
  (111 shorter events, 41.0 us)
Async XLA Ops:
  4.1 15.3 %collective-permute-start.1 = (bf16[384,640]{1,0:T(8,128)(2,1)}, bf16[384,640]{1,0:T(8,128)(2,1)S(1)}, u32[]{:S(2)}, u32[]{:S(2)}) collective-permute-start(bf16[384,640]{1,0:T(8,128)(2,1)} %get-tuple-element.78), channel_id=1, source_target_pairs={{0,4},{2,6},{4,0},{6,2},{8,12},{10,14},{12,8},{14,10},{1,5},{3,7},... | collective-permute-start | bytes 1474568 | tf_op jit(solution)/shard_map/ppermute | solution.py:313
  7.1 14.4 %collective-permute-start.2 = (bf16[384,640]{1,0:T(8,128)(2,1)}, bf16[384,640]{1,0:T(8,128)(2,1)S(1)}, u32[]{:S(2)}, u32[]{:S(2)}) collective-permute-start(bf16[384,640]{1,0:T(8,128)(2,1)} %get-tuple-element.78), channel_id=1, source_target_pairs={{0,2},{2,0},{4,6},{6,4},{8,10},{10,8},{12,14},{14,12},{1,3},{3,1},... | collective-permute-start | bytes 1474568 | tf_op jit(solution)/shard_map/ppermute | solution.py:313
  8.6 20.5 %collective-permute-start = (bf16[384,640]{1,0:T(8,128)(2,1)}, bf16[384,640]{1,0:T(8,128)(2,1)S(1)}, u32[]{:S(2)}, u32[]{:S(2)}) collective-permute-start(bf16[384,640]{1,0:T(8,128)(2,1)} %get-tuple-element.79), channel_id=1, source_target_pairs={{0,4},{2,6},{4,0},{6,2},{8,12},{10,14},{12,8},{14,10},{1,5},{3,7},... | collective-permute-start | bytes 1474568 | tf_op jit(solution)/shard_map/ppermute | solution.py:313
  9.1 23.1 %collective-permute-start.8 = (bf16[384,640]{1,0:T(8,128)(2,1)}, bf16[384,640]{1,0:T(8,128)(2,1)S(1)}, u32[]{:S(2)}, u32[]{:S(2)}) collective-permute-start(bf16[384,640]{1,0:T(8,128)(2,1)} %get-tuple-element.79), channel_id=1, source_target_pairs={{0,2},{2,0},{4,6},{6,4},{8,10},{10,8},{12,14},{14,12},{1,3},{3,1},... | collective-permute-start | bytes 1474568 | tf_op jit(solution)/shard_map/ppermute | solution.py:313
  9.2 25.1 %collective-permute-start.15 = (bf16[448,1280]{1,0:T(8,128)(2,1)}, bf16[448,1280]{1,0:T(8,128)(2,1)}, u32[]{:S(2)}, u32[]{:S(2)}) collective-permute-start(bf16[448,1280]{1,0:T(8,128)(2,1)} %param.9), channel_id=1, source_target_pairs={{0,1},{1,0},{2,3},{3,2},{4,5},{5,4},{6,7},{7,6},{8,9},{9,8},{10,11... | collective-permute-start | bytes 3440648 | tf_op jit(solution)/shard_map/ppermute | solution.py:389
  19.5 11.4 %collective-permute-start.4 = (bf16[384,640]{1,0:T(8,128)(2,1)S(1)}, bf16[384,640]{1,0:T(8,128)(2,1)S(1)}, u32[]{:S(2)}, u32[]{:S(2)}) collective-permute-start(bf16[384,640]{1,0:T(8,128)(2,1)S(1)} %pad_maximum_fusion.1), channel_id=1, source_target_pairs={{4,8},{8,4},{6,10},{10,6},{5,9},{9,5},{7,11},{11,7},{20,24},{24,20... | collective-permute-start | bytes 1474568 | tf_op jit(solution)/shard_map/ppermute | solution.py:313
  21.5 11.4 %collective-permute-start.6 = (bf16[384,640]{1,0:T(8,128)(2,1)S(1)}, bf16[384,640]{1,0:T(8,128)(2,1)S(1)}, u32[]{:S(2)}, u32[]{:S(2)}) collective-permute-start(bf16[384,640]{1,0:T(8,128)(2,1)S(1)} %pad_maximum_fusion.2), channel_id=1, source_target_pairs={{4,8},{8,4},{6,10},{10,6},{5,9},{9,5},{7,11},{11,7},{20,24},{24,20... | collective-permute-start | bytes 1474568 | tf_op jit(solution)/shard_map/ppermute | solution.py:313
  29.1 14.2 %collective-permute-start.3 = (bf16[384,640]{1,0:T(8,128)(2,1)S(1)}, bf16[384,640]{1,0:T(8,128)(2,1)S(1)}, u32[]{:S(2)}, u32[]{:S(2)}) collective-permute-start(bf16[384,640]{1,0:T(8,128)(2,1)S(1)} %collective-permute-done.1.x1.p1a), channel_id=1, source_target_pairs={{0,2},{2,0},{4,6},{6,4},{8,10},{10,8},{12,14},{14,12},{1,3},{3,1},... | collective-permute-start | bytes 1474568 | tf_op jit(solution)/shard_map/ppermute | solution.py:313
  30.9 16.5 %collective-permute-start.5 = (bf16[384,640]{1,0:T(8,128)(2,1)S(1)}, bf16[384,640]{1,0:T(8,128)(2,1)S(1)}, u32[]{:S(2)}, u32[]{:S(2)}) collective-permute-start(bf16[384,640]{1,0:T(8,128)(2,1)S(1)} %collective-permute-done.4), channel_id=1, source_target_pairs={{4,0},{6,2},{8,12},{10,14},{5,1},{7,3},{9,13},{11,15},{20,16},{22,... | collective-permute-start | bytes 1474568 | tf_op jit(solution)/shard_map/ppermute | solution.py:313
  32.2 23.2 %collective-permute-start.11 = (bf16[384,640]{1,0:T(8,128)(2,1)S(1)}, bf16[384,640]{1,0:T(8,128)(2,1)S(1)}, u32[]{:S(2)}, u32[]{:S(2)}) collective-permute-start(bf16[384,640]{1,0:T(8,128)(2,1)S(1)} %pad_maximum_fusion.3), channel_id=1, source_target_pairs={{4,8},{8,4},{6,10},{10,6},{5,9},{9,5},{7,11},{11,7},{20,24},{24,20... | collective-permute-start | bytes 1474568 | tf_op jit(solution)/shard_map/ppermute | solution.py:313
  33.0 25.4 %collective-permute-start.10 = (bf16[384,640]{1,0:T(8,128)(2,1)S(1)}, bf16[384,640]{1,0:T(8,128)(2,1)S(1)}, u32[]{:S(2)}, u32[]{:S(2)}) collective-permute-start(bf16[384,640]{1,0:T(8,128)(2,1)S(1)} %collective-permute-done.6), channel_id=1, source_target_pairs={{4,0},{6,2},{8,12},{10,14},{5,1},{7,3},{9,13},{11,15},{20,16},{22,... | collective-permute-start | bytes 1474568 | tf_op jit(solution)/shard_map/ppermute | solution.py:313
  34.3 24.1 %collective-permute-start.9 = (bf16[384,640]{1,0:T(8,128)(2,1)S(1)}, bf16[384,640]{1,0:T(8,128)(2,1)S(1)}, u32[]{:S(2)}, u32[]{:S(2)}) collective-permute-start(bf16[384,640]{1,0:T(8,128)(2,1)S(1)} %collective-permute-done.x1.p1b), channel_id=1, source_target_pairs={{0,2},{2,0},{4,6},{6,4},{8,10},{10,8},{12,14},{14,12},{1,3},{3,1},... | collective-permute-start | bytes 1474568 | tf_op jit(solution)/shard_map/ppermute | solution.py:313
  47.4 11.0 %collective-permute-start.7 = (bf16[384,640]{1,0:T(8,128)(2,1)S(1)}, bf16[384,640]{1,0:T(8,128)(2,1)S(1)}, u32[]{:S(2)}, u32[]{:S(2)}) collective-permute-start(bf16[384,640]{1,0:T(8,128)(2,1)S(1)} %pad_maximum_fusion), channel_id=1, source_target_pairs={{4,8},{8,4},{6,10},{10,6},{5,9},{9,5},{7,11},{11,7},{20,24},{24,20... | collective-permute-start | bytes 1474568 | tf_op jit(solution)/shard_map/ppermute | solution.py:313
  55.4 22.2 %collective-permute-start.16 = (bf16[384,640]{1,0:T(8,128)(2,1)S(1)}, bf16[384,640]{1,0:T(8,128)(2,1)S(1)}, u32[]{:S(2)}, u32[]{:S(2)}) collective-permute-start(bf16[384,640]{1,0:T(8,128)(2,1)S(1)} %collective-permute-done.11), channel_id=1, source_target_pairs={{4,0},{6,2},{8,12},{10,14},{5,1},{7,3},{9,13},{11,15},{20,16},{22,... | collective-permute-start | bytes 1474568 | tf_op jit(solution)/shard_map/ppermute | solution.py:313
  56.8 20.9 %collective-permute-start.17 = (bf16[384,640]{1,0:T(8,128)(2,1)S(1)}, bf16[384,640]{1,0:T(8,128)(2,1)S(1)}, u32[]{:S(2)}, u32[]{:S(2)}) collective-permute-start(bf16[384,640]{1,0:T(8,128)(2,1)S(1)} %broadcast_select_fusion.refs_0_.refs_1_), channel_id=1, source_target_pairs={{0,2},{2,0},{4,6},{6,4},{8,10},{10,8},{12,14},{14,12},{1,3},{3,1},... | collective-permute-start | bytes 1474568 | tf_op jit(solution)/shard_map/ppermute | solution.py:313
  58.4 24.5 %collective-permute-start.12 = (bf16[384,640]{1,0:T(8,128)(2,1)S(1)}, bf16[384,640]{1,0:T(8,128)(2,1)S(1)}, u32[]{:S(2)}, u32[]{:S(2)}) collective-permute-start(bf16[384,640]{1,0:T(8,128)(2,1)S(1)} %collective-permute-done.7), channel_id=1, source_target_pairs={{4,0},{6,2},{8,12},{10,14},{5,1},{7,3},{9,13},{11,15},{20,16},{22,... | collective-permute-start | bytes 1474568 | tf_op jit(solution)/shard_map/ppermute | solution.py:313
  60.0 23.1 %collective-permute-start.13 = (bf16[384,640]{1,0:T(8,128)(2,1)S(1)}, bf16[384,640]{1,0:T(8,128)(2,1)S(1)}, u32[]{:S(2)}, u32[]{:S(2)}) collective-permute-start(bf16[384,640]{1,0:T(8,128)(2,1)S(1)} %broadcast_select_fusion.2.refs_0_.refs_1_), channel_id=1, source_target_pairs={{0,2},{2,0},{4,6},{6,4},{8,10},{10,8},{12,14},{14,12},{1,3},{3,1},... | collective-permute-start | bytes 1474568 | tf_op jit(solution)/shard_map/ppermute | solution.py:313
  77.7 28.4 %collective-permute-start.18 = (bf16[384,640]{1,0:T(8,128)(2,1)S(1)}, bf16[384,640]{1,0:T(8,128)(2,1)S(1)}, u32[]{:S(2)}, u32[]{:S(2)}) collective-permute-start(bf16[384,640]{1,0:T(8,128)(2,1)S(1)} %broadcast_select_fusion.1.refs_0_.refs_1_.refs_2_), channel_id=1, source_target_pairs={{0,2},{2,0},{4,6},{6,4},{8,10},{10,8},{12,14},{14,12},{1,3},{3,1},... | collective-permute-start | bytes 1474568 | tf_op jit(solution)/shard_map/ppermute | solution.py:313
  83.0 30.7 %collective-permute-start.14 = (bf16[384,640]{1,0:T(8,128)(2,1)S(1)}, bf16[384,640]{1,0:T(8,128)(2,1)S(1)}, u32[]{:S(2)}, u32[]{:S(2)}) collective-permute-start(bf16[384,640]{1,0:T(8,128)(2,1)S(1)} %broadcast_select_fusion.3.refs_0_.refs_1_.refs_3_), channel_id=1, source_target_pairs={{0,2},{2,0},{4,6},{6,4},{8,10},{10,8},{12,14},{14,12},{1,3},{3,1},... | collective-permute-start | bytes 1474568 | tf_op jit(solution)/shard_map/ppermute | solution.py:313
  121.5 3.8 %collective-permute-start.19 = (f32[2,8,192]{2,1,0:T(8,128)S(1)}, f32[2,8,192]{2,1,0:T(8,128)S(1)}, u32[]{:S(2)}, u32[]{:S(2)}) collective-permute-start(f32[2,8,192]{2,1,0:T(8,128)S(1)} %get-tuple-element.64.mine), channel_id=1, source_target_pairs={{0,2},{2,0},{4,6},{6,4},{8,10},{10,8},{12,14},{14,12},{1,3},{3,1},... | collective-permute-start | bytes 36872 | tf_op jit(solution)/shard_map/ppermute | solution.py:357
  125.3 11.5 %collective-permute-start.20 = (f32[2,8,192]{2,1,0:T(8,128)S(1)}, f32[2,8,192]{2,1,0:T(8,128)S(1)}, u32[]{:S(2)}, u32[]{:S(2)}) collective-permute-start(f32[2,8,192]{2,1,0:T(8,128)S(1)} %pad_maximum_fusion.4), channel_id=1, source_target_pairs={{0,4},{2,6},{4,0},{6,2},{8,12},{10,14},{12,8},{14,10},{1,5},{3,7},... | collective-permute-start | bytes 36872 | tf_op jit(solution)/shard_map/ppermute | solution.py:357
  136.8 4.7 %collective-permute-start.21 = (f32[2,8,192]{2,1,0:T(8,128)S(1)}, f32[2,8,192]{2,1,0:T(8,128)S(1)}, u32[]{:S(2)}, u32[]{:S(2)}) collective-permute-start(f32[2,8,192]{2,1,0:T(8,128)S(1)} %pad_maximum_fusion.5), channel_id=1, source_target_pairs={{0,8},{2,10},{4,12},{6,14},{8,0},{10,2},{12,4},{14,6},{1,9},{3,11}... | collective-permute-start | bytes 36872 | tf_op jit(solution)/shard_map/ppermute | solution.py:357
  151.6 3.7 %collective-permute-start.22 = (f32[8,192]{1,0:T(8,128)S(1)}, f32[8,192]{1,0:T(8,128)S(1)}, u32[]{:S(2)}, u32[]{:S(2)}) collective-permute-start(f32[8,192]{1,0:T(8,128)S(1)} %get-tuple-element.65), channel_id=1, source_target_pairs={{0,2},{2,0},{4,6},{6,4},{8,10},{10,8},{12,14},{14,12},{1,3},{3,1},... | collective-permute-start | bytes 18440 | tf_op jit(solution)/shard_map/ppermute | solution.py:357
  158.9 5.5 %collective-permute-start.24 = (f32[8,192]{1,0:T(8,128)S(1)}, f32[8,192]{1,0:T(8,128)S(1)}, u32[]{:S(2)}, u32[]{:S(2)}) collective-permute-start(f32[8,192]{1,0:T(8,128)S(1)} %add.57), channel_id=1, source_target_pairs={{0,8},{2,10},{4,12},{6,14},{8,0},{10,2},{12,4},{14,6},{1,9},{3,11}... | collective-permute-start | bytes 18440 | tf_op jit(solution)/shard_map/ppermute | solution.py:357
  (22 other events, 320.9 us)

commit v2 on v0

v2 whole, which is shorter than its diff:
```python
import functools

import jax
import jax.numpy as jnp
from jax import lax
from jax.experimental import pallas as pl
from jax.experimental.pallas import tpu as pltpu
from jax.sharding import PartitionSpec as P

F32, BF16 = jnp.float32, jnp.bfloat16
SCOPED_BYTES = 12 * 2**20
LANES = 128
BLOCK = 32

VMEM = pl.BlockSpec(memory_space=pltpu.VMEM)
SMEM = pl.BlockSpec(memory_space=pltpu.SMEM)
ANYWHERE = pl.BlockSpec(memory_space=pl.ANY)


def _kernel(body, outs, ins, name, flops=0, scratch=(), specs=None, out_specs=None, exps=0):
    specs = specs or [VMEM] * len(ins)
    ins = [pltpu.with_memory_space_constraint(x, pltpu.VMEM) if s is VMEM else x for x, s in zip(ins, specs, strict=True)]
    return pl.pallas_call(
        body,
        in_specs=specs,
        out_specs=out_specs or [VMEM] * len(outs),
        out_shape=outs,
        scratch_shapes=scratch,
        compiler_params=pltpu.CompilerParams(vmem_limit_bytes=SCOPED_BYTES),
        cost_estimate=pl.CostEstimate(
            flops=flops,
            bytes_accessed=sum(x.size * x.dtype.itemsize for x in ins),
            transcendentals=exps,
        ),
        name=name,
    )(*ins)


def _eye(n):
    return lax.broadcasted_iota(jnp.int32, (n, n), 0) == lax.broadcasted_iota(jnp.int32, (n, n), 1)


def _to_row(eye, column):
    return jnp.sum(jnp.where(eye, column, 0.0), axis=0, keepdims=True)


def _to_column(eye, row):
    return jnp.sum(jnp.where(eye, row, 0.0), axis=1, keepdims=True)


def _dot(a, b):
    return jnp.dot(a, b, preferred_element_type=F32)


def _place(index, size):
    return pl.ds(pl.multiple_of(index * size, size), size)


def _pack_kernel(target, draft, low, high):
    half, feats, draft_feats = low.shape[0], target.shape[1], draft.shape[1]
    for start, out in ((0, low), (half, high)):
        out[:, :feats] = target[start : start + half, :]
        out[:, feats:] = jnp.zeros((half, LANES), BF16)
        out[:, feats : feats + draft_feats] = draft[start : start + half, :]


def _pack(target, draft):
    rows, feats = target.shape
    out = pltpu.VMEM((rows // 2, feats + LANES), BF16)
    plain = pl.BlockSpec()
    return _kernel(_pack_kernel, [out, out], [target, draft], "packed_hidden", specs=[plain, plain])


def _fetch_kernel(source, out, sem):
    copy = pltpu.make_async_copy(source, out, sem)
    copy.start()
    copy.wait()


def _fetch(x):
    return _kernel(
        _fetch_kernel, [pltpu.VMEM(x.shape, x.dtype)], [x], "target_head", specs=[ANYWHERE], scratch=[pltpu.SemaphoreType.DMA]
    )[0]


def _head_kernel(tok, mine, other, out):
    part = mine.shape[0] // 4
    out[...] = jnp.zeros_like(out)
    for which, ref in ((tok[0], mine), (1 - tok[0], other)):
        for b in range(4):
            start = pl.multiple_of(which * (4 * LANES) + b * LANES, LANES)
            out[pl.ds(start, part), :] = ref[b * part : (b + 1) * part, :]


def _head(tok, mine, other):
    plain = pl.BlockSpec()
    return _kernel(
        _head_kernel,
        [pltpu.VMEM((8 * LANES, mine.shape[1]), BF16)],
        [tok, mine, other],
        "draft_head",
        specs=[SMEM, plain, VMEM],
    )[0]


def _products(perm, xs, first, wt, wd, cols):
    feats = xs[0].shape[1] - LANES
    target = None
    for k, x in enumerate(xs):
        term = _dot(x[:, :feats], wt[_place(perm[first + k], feats), cols])
        target = term if target is None else target + term
    draft = _dot(
        jnp.concatenate([x[:, feats:] for x in xs], axis=1),
        jnp.concatenate([wd[_place(perm[first + k], LANES), cols] for k in range(len(xs))], axis=0),
    )
    return target, draft


def _columns(vocab, cols):
    return [slice(n, n + cols) for n in range(0, vocab, cols)]


def _near_kernel(perm, x0, x1, x2, x3, wt, wd, acc_t, acc_d):
    for c in _columns(wt.shape[1], 256):
        acc_t[:, c], acc_d[:, c] = _products(perm, (x0, x1, x2, x3), 0, wt, wd, c)


def _near(perm, own, p1, o, a, wt, wd):
    rows, vocab = own.shape[0], wt.shape[1]
    out = pltpu.VMEM((rows, vocab), F32)
    return _kernel(
        _near_kernel,
        [out, out],
        [perm, own, p1, o, a, wt, wd],
        "near_logits",
        flops=8 * rows * own.shape[1] * vocab,
        specs=[SMEM] + [VMEM] * 6,
    )


def _far_kernel(chunk, perm, far, f, wt, wd, acc_t, acc_d, before, e_t, e_d, stats):
    rows = e_t.shape[0]
    at = (chunk % 2) * rows
    pieces = [ref.at[half * rows : (half + 1) * rows, :] for ref in (far, f) for half in (0, 1)]
    for c in _columns(wt.shape[1], 256):
        target, draft = _products(perm, pieces, 4, wt, wd, c)
        e_t[:, c] = target + acc_t[at : at + rows, c]
        e_d[:, c] = draft + acc_d[at : at + rows, c]
    eye = _eye(rows)
    stats[...] = before[...]
    for kind, ref in enumerate((e_t, e_d)):
        tops, sums = [], []
        for r in range(0, rows, BLOCK):
            logits = ref[r : r + BLOCK, :]
            top = jnp.max(logits, axis=1, keepdims=True)
            e = jnp.exp(logits - top)
            ref[r : r + BLOCK, :] = e
            tops.append(top)
            sums.append(jnp.sum(e, axis=1, keepdims=True))
        row = 2 * chunk + kind
        stats[0, row : row + 1, :] = _to_row(eye, jnp.concatenate(tops, axis=0))
        stats[1, row : row + 1, :] = _to_row(eye, jnp.concatenate(sums, axis=0))


def _far(chunk, perm, far, f, wt, wd, acc, before):
    rows, vocab = far.shape[0] // 2, wt.shape[1]
    out = pltpu.VMEM((rows, vocab), F32)
    return _kernel(
        functools.partial(_far_kernel, chunk),
        [out, out, pltpu.VMEM(before.shape, F32)],
        [perm, far, f, wt, wd, *acc, before],
        "far_logits",
        flops=8 * rows * far.shape[1] * vocab,
        exps=2 * rows * vocab,
        specs=[SMEM] + [VMEM] * 7,
    )


def _slope_kernel(full, *refs):
    chunks = (len(refs) - 5) // 2
    es_t, es_d = refs[:chunks], refs[chunks : 2 * chunks]
    mine, total, slope_out, scaled_out, sums = refs[2 * chunks :]
    rows = mine.shape[2]
    eye = _eye(rows)
    for i in range(chunks):
        scales = [
            full
            * _to_column(eye, jnp.exp(mine[0, r : r + 1, :] - total[0, r : r + 1, :]) / total[1, r : r + 1, :])
            for r in (2 * i, 2 * i + 1)
        ]
        losses, inners = [], []
        for r in range(0, rows, BLOCK):
            target = es_t[i][r : r + BLOCK, :] * scales[0][r : r + BLOCK]
            draft = es_d[i][r : r + BLOCK, :] * scales[1][r : r + BLOCK]
            spread = draft - target
            square = spread * spread + 1.0
            inverse = lax.rsqrt(square)
            slope = spread * inverse
            slope_out[i * rows + r : i * rows + r + BLOCK, :] = slope
            scaled_out[i * rows + r : i * rows + r + BLOCK, :] = draft
            losses.append(jnp.sum(square * inverse - 1.0, axis=1, keepdims=True))
            inners.append(jnp.sum(draft * slope, axis=1, keepdims=True))
        sums[2 * i : 2 * i + 1, :] = _to_row(eye, jnp.concatenate(losses, axis=0)) * (0.5 / full)
        sums[2 * i + 1 : 2 * i + 2, :] = _to_row(eye, jnp.concatenate(inners, axis=0)) * (1.0 / full)


def _slopes(es_t, es_d, mine, total, full):
    chunks, (rows, vocab) = len(es_t), es_t[0].shape
    out = pltpu.VMEM((chunks * rows, vocab), F32)
    return _kernel(
        functools.partial(_slope_kernel, full),
        [out, out, pltpu.VMEM((2 * chunks, rows), F32)],
        [*es_t, *es_d, mine, total],
        "slopes",
        flops=12 * chunks * rows * vocab,
        exps=chunks * rows * vocab,
    )


def _turn_kernel(chunks, perm, *refs):
    out = refs[-1]
    pairs, fars, fs = refs[:8], refs[8 : 8 + chunks], refs[8 + chunks : 8 + 2 * chunks]
    half, width = pairs[0].shape
    rows = half // 2
    feats = width - LANES
    for k in range(4):
        for h in range(2):
            out[_place(perm[k], LANES), h * half : (h + 1) * half] = jnp.transpose(pairs[2 * k + h][:, feats:])
    for k, parts in ((4, fars), (6, fs)):
        for side in range(2):
            whole = jnp.concatenate([x[side * rows : (side + 1) * rows, feats:] for x in parts], axis=0)
            out[_place(perm[k + side], LANES), :] = jnp.transpose(whole)


def _turn(perm, pairs, fars, fs):
    rows_all = 2 * pairs[0].shape[0]
    return _kernel(
        functools.partial(_turn_kernel, len(fars)),
        [pltpu.VMEM((8 * LANES, rows_all), BF16)],
        [perm, *pairs, *fars, *fs],
        "turned_features",
        specs=[SMEM] + [VMEM] * (8 + 2 * len(fars)),
        flops=16 * LANES * rows_all,
    )[0]


def _gradient(features, which, grad, out, scale):
    part = out.shape[0] // 4
    half = features.shape[0] // 2
    for c in _columns(grad.shape[1], 256):
        product = _dot(features[_place(which, half), :], grad[:, c]) * scale
        for b in range(4):
            out[b * part : (b + 1) * part, c] = product[b * LANES : b * LANES + part].astype(out.dtype)


def _send_kernel(tokens, tok, features, slope, scaled, inner, grad, out):
    chunks, rows = inner.shape[0] // 2, inner.shape[1]
    eye = _eye(rows)
    for i in range(chunks):
        column = _to_column(eye, inner[2 * i + 1 : 2 * i + 2, :])
        for r in range(0, rows, BLOCK):
            here = slice(i * rows + r, i * rows + r + BLOCK)
            grad[here, :] = (scaled[here, :] * (slope[here, :] - column[r : r + BLOCK])).astype(BF16)
    _gradient(features, 1 - tok[0], grad, out, 1.0 / tokens)


def _send(tok, features, slope, scaled, inner, tokens, part):
    rows_all, vocab = slope.shape
    return _kernel(
        functools.partial(_send_kernel, tokens),
        [pltpu.VMEM((rows_all, vocab), BF16), pltpu.VMEM((part, vocab), BF16)],
        [tok, features, slope, scaled, inner],
        "gradient_to_send",
        specs=[SMEM] + [VMEM] * 4,
        flops=features.shape[0] * rows_all * vocab,
    )


def _keep_kernel(tokens, tok, features, grad, out):
    _gradient(features, tok[0], grad, out, 1.0 / tokens)


def _keep(tok, features, grad, tokens, part):
    rows_all, vocab = grad.shape
    return _kernel(
        functools.partial(_keep_kernel, tokens),
        [pltpu.VMEM((part, vocab), F32)],
        [tok, features, grad],
        "gradient_to_keep",
        specs=[SMEM, VMEM, VMEM],
        flops=features.shape[0] * rows_all * vocab,
    )[0]


def _add_kernel(keep, received, out):
    out[...] = (keep[...] + received[...].astype(F32)).astype(out.dtype)


def _add(keep, received):
    return _kernel(
        _add_kernel,
        [jax.ShapeDtypeStruct(keep.shape, BF16)],
        [keep, received],
        "summed_gradient",
        out_specs=[pl.BlockSpec()],
        flops=keep.size,
    )[0]


class _Slots:
    def __init__(self):
        self.before, self.last, self.now = [], [], []

    def next(self):
        self.before, self.last, self.now = self.last, self.now, []

    def move(self, x, pairs, *after):
        if self.before or after:
            x = lax.optimization_barrier((x, *self.before, *after))[0]
        y = lax.ppermute(x, "voc", pairs)
        self.now.append(y)
        return y


def _xor(k):
    return [(i, i ^ k) for i in range(8)]


MIDDLE = [(2, 4), (4, 2), (3, 5), (5, 3)]
OUTWARD = [(2, 0), (3, 1), (4, 6), (5, 7)]


def _all_reduce(x, merge):
    for k in (1, 2, 4):
        x = merge(x, lax.ppermute(x, "voc", _xor(k)))
    return x


def _merge_softmax(a, b):
    top = jnp.maximum(a[0], b[0])
    return jnp.stack([top, a[1] * jnp.exp(a[0] - top) + b[1] * jnp.exp(b[0] - top)])


def _body_4x2(target_hidden, draft_hidden, target_head, draft_head):
    rows_all = target_hidden.shape[0]
    part, vocab = draft_head.shape
    chunks = 4
    rows = rows_all // chunks
    full = float(vocab * lax.axis_size("voc"))
    tokens = float(rows_all * lax.axis_size("tok"))
    me, tok = lax.axis_index("voc"), lax.axis_index("tok")
    z, x = me // 2, me % 2
    end = (z == 0) | (z == 3)
    far_z = (jnp.where(z < 2, 2, 1), jnp.where(z < 2, 3, 0))
    perm = [me, me ^ 2, me ^ 1, me ^ 3] + [2 * fz + side for side in (x, 1 - x) for fz in far_z]
    perm = jnp.stack(perm).astype(jnp.int32)
    tok_index = tok.reshape(1).astype(jnp.int32)

    halves = _pack(target_hidden, draft_hidden)
    wt = _fetch(target_head)
    wd = _head(tok_index, draft_head, lax.ppermute(draft_head, "tok", [(0, 1), (1, 0)]))

    slots = _Slots()
    p1, o, a, middle, outward, far, f, acc, es_t, es_d = ([] for _ in range(10))
    stats = jnp.zeros((2, 2 * chunks, rows), F32)
    done = []

    def near_pair(c):
        start = (c % 2) * rows
        return jnp.concatenate([h[start : start + rows] for h in (halves[c // 2], p1[c // 2])])

    for slot in range(8):
        if slot < 2:
            p1.append(slots.move(halves[slot], _xor(2)))
            o.append(slots.move(halves[slot], _xor(1)))
        elif slot < 4:
            a.append(slots.move(p1[slot - 2], _xor(1)))
        if 2 <= slot < 6:
            outward.append(slots.move(middle[slot - 2], OUTWARD, *done))
        if 1 <= slot < 5:
            middle.append(slots.move(near_pair(slot - 1), MIDDLE, *done))
        if slot >= 4:
            c = slot - 4
            far.append(jnp.where(end, outward[c], middle[c]))
            f.append(slots.move(far[c], _xor(1), *done))
        done = []
        if slot in (4, 5):
            h = slot - 4
            acc.append(_near(perm, halves[h], p1[h], o[h], a[h], wt, wd))
            done = [acc[h][0]]
        if slot >= 6:
            e_t, e_d, stats = _far(slot - 6, perm, far[slot - 6], f[slot - 6], wt, wd, acc[0], stats)
            es_t.append(e_t)
            es_d.append(e_d)
            done = [e_t]
        slots.next()
    for c in (2, 3):
        e_t, e_d, stats = _far(c, perm, far[c], f[c], wt, wd, acc[1], stats)
        es_t.append(e_t)
        es_d.append(e_d)

    total = _all_reduce(stats, _merge_softmax)
    slope, scaled, sums = _slopes(es_t, es_d, stats, total, full)
    pairs = [m[h] for m in (halves, p1, o, a) for h in range(2)]
    features = _turn(perm, pairs, far, f)
    sums = _all_reduce(sums, jnp.add)
    grad, send = _send(tok_index, features, slope, scaled, sums, tokens, part)
    received = lax.ppermute(send, "tok", [(0, 1), (1, 0)])
    keep = _keep(tok_index, features, grad, tokens, part)
    row_loss = sums.reshape(chunks, 2, rows)[:, 0].reshape(rows_all)
    return row_loss, _add(keep, received)


def _body_any(target_hidden, draft_hidden, target_head, draft_head):
    rows, vocab = target_hidden.shape[0], target_head.shape[1]
    full = float(vocab * lax.axis_size("voc"))
    tokens = float(rows * lax.axis_size("tok"))
    draft_weights = lax.all_gather(draft_head, "tok", axis=0, tiled=True)
    hidden = lax.all_gather(target_hidden, "voc", axis=1, tiled=True)
    target_logits = jnp.dot(hidden, target_head, preferred_element_type=F32)
    features = lax.all_gather(draft_hidden, "voc", axis=1, tiled=True)
    draft_logits = jnp.dot(features, draft_weights, preferred_element_type=F32)
    top_t, top_d = lax.pmax((jnp.max(target_logits, axis=1), jnp.max(draft_logits, axis=1)), "voc")
    target_exp = jnp.exp(target_logits - top_t[:, None])
    draft_exp = jnp.exp(draft_logits - top_d[:, None])
    total_t, total_d = lax.psum((jnp.sum(target_exp, axis=1), jnp.sum(draft_exp, axis=1)), "voc")
    target_prob = target_exp / total_t[:, None]
    draft_prob = draft_exp / total_d[:, None]
    spread = full * (draft_prob - target_prob)
    root = jnp.sqrt(spread * spread + 1.0)
    slope = spread / root
    loss = jnp.sum(root - 1.0, axis=1) / (2.0 * full)
    row_loss, inner = lax.psum((loss, jnp.sum(draft_prob * slope, axis=1)), "voc")
    logit_grad = (full * draft_prob * (slope - inner[:, None])).astype(BF16)
    summed = lax.dot_general(features, logit_grad, (((0,), (0,)), ((), ())), preferred_element_type=F32)
    draft_grad = lax.psum_scatter((summed / tokens).astype(BF16), "tok", scatter_dimension=0, tiled=True)
    return row_loss, draft_grad


def solution(mesh):
    body = _body_4x2 if (mesh.shape["voc"], mesh.shape["tok"]) == (8, 2) else _body_any
    return jax.shard_map(
        body,
        mesh=mesh,
        in_specs=(
            P(("grp", "tok"), "voc"),
            P(("grp", "tok"), "voc"),
            P(None, "voc"),
            P("tok", "voc"),
        ),
        out_specs=(P(("grp", "tok")), P(("grp", "tok"), "voc")),
        check_vma=False,
    )
```

time: 277 us -> 141 us (0.51)
  waiting for transfers between devices: 163 us -> 56.7 us
  blocking collectives: 56.1 us -> 0 us
  starting transfers between devices: 0.15 us -> 36.7 us
  matrix products: 29 us -> 0 us
  Pallas kernels: 0 us -> 29 us
  between operations: 13.8 us -> 0.99 us
  local copies, waits for them, and re-layouts: 2.54 us -> 15.2 us
  other arithmetic: 12.1 us -> 2.05 us
    all_gather x3 -> x0, waiting for transfers between devices: 154 us -> none  [the longest x1 94.3 us: body(): lax.all_gather(target_hidden, 'voc', axis=1, tiled=True)]
    ppermute x0 -> x26, waiting for transfers between devices: none -> 56.7 us  [the longest x18 44.3 us: move(): y = lax.ppermute(x, 'voc', pairs)]
    psum x2 -> x0, blocking collectives: 37.3 us -> none  [the longest x1 19.4 us: body(): row_loss, inner = lax.psum((loss_part, inner_part), 'voc')]
    ppermute x0 -> x26, starting transfers between devices: none -> 36.7 us  [the longest x18 21.5 us: move(): y = lax.ppermute(x, 'voc', pairs)]
    dot_general x3 -> x0, matrix products: 29 us -> none  [the longest x1 14.8 us: body(): jnp.dot(lax.all_gather(target_hidden, 'voc', axis=1, tiled=True), target_...]
    pallas_call x0 -> x14, Pallas kernels: none -> 29 us  [_kernel(): pl.pallas_call(body, in_specs=specs, out_specs=out_specs or [VMEM] * len(...]
    pmax x1 -> x0, blocking collectives: 18.8 us -> none  [body(): top_target, top_draft = lax.pmax((local_top_target, local_top_draft), 'voc')]
    reduce_sum x2 -> x0, other arithmetic: 12.1 us -> none  [the longest x1 7.47 us: body(): inner_part = jnp.sum(draft_prob * slope, axis=1)]
  transfers between devices with their start and end apart: 4 -> 26, of which waited for: 4 -> 14; matrix products, arithmetic and copies ran while one was open for 2% -> 2% of each run, Pallas kernels for 0% -> 13%
where the time goes in v2:
time: 141 us
  waiting for transfers between devices  56.7 us (40%)
  starting transfers between devices  36.7 us (26%)
  Pallas kernels  29 us (21%)
  local copies, waits for them, and re-layouts  15.2 us (11%)
  other arithmetic  2.05 us (1%)
    ppermute x18, waiting for transfers between devices, move(): y = lax.ppermute(x, 'voc', pairs)  44.3 us
    pallas_call x14, Pallas kernels, _kernel(): pl.pallas_call(body, in_specs=specs, out_specs=out_specs or [VMEM] * len(...  29 us
    ppermute x18, starting transfers between devices, move(): y = lax.ppermute(x, 'voc', pairs)  21.5 us
    ppermute x6, starting transfers between devices, _all_reduce(): x = merge(x, lax.ppermute(x, 'voc', _xor(k)))  15.2 us
    unnamed x21, local copies, waits for them, and re-layouts  14.2 us
    ppermute x6, waiting for transfers between devices, _all_reduce(): x = merge(x, lax.ppermute(x, 'voc', _xor(k)))  11.2 us
  transfers between devices with their start and end apart: 26, of which 14 were waited for; matrix products, arithmetic and copies ran while one was open for 2% of the time, Pallas kernels for 13%

profile of v2, /device:TPU:0, one launch (start us, length us, event | category | flops | bytes accessed | tf_op | source)
XLA Modules:
  0.0 140.6 jit_solution(12678049432436008761)
XLA Ops:
  3.0 3.1 %collective-permute-start = (bf16[384,640]{1,0:T(8,128)(2,1)S(1)}, bf16[384,640]{1,0:T(8,128)(2,1)S(1)}, u32[]{:S(2)}, u32[]{:S(2)}) collective-permute-start(bf16[384,640]{1,0:T(8,128)(2,1)S(1)} %get-tuple-element.38.x0.refs_0_), channel_id=1, source_target_pairs={{0,4},{2,6},{4,0},{6,2},{8,12},{10,14},{12,8},{14,10},{1,5},{3,7},... | collective-permute-start | bytes 1474568 | tf_op jit(solution)/shard_map/ppermute | solution.py:320
  8.2 9.9 %collective-permute-done.x1.refs_2_ = bf16[384,640]{1,0:T(8,128)(2,1)S(1)} collective-permute-done((bf16[384,640]{1,0:T(8,128)(2,1)S(1)}, bf16[384,640]{1,0:T(8,128)(2,1)S(1)}, u32[]{:S(2)}, u32[]{:S(2)}) %collective-permute-start) | collective-permute-done | bytes 491552 | tf_op jit(solution)/shard_map/ppermute | solution.py:320
  22.7 4.0 %copy-done.3 = bf16[4096,1280]{1,0:T(8,128)(2,1)S(1)} copy-done((bf16[4096,1280]{1,0:T(8,128)(2,1)S(1)}, bf16[4096,1280]{1,0:T(8,128)(2,1)}, u32[]{:S(2)}) %copy-start.3) | copy-done | bytes 10485784
  27.4 4.0 %copy-done = bf16[4096,1280]{1,0:T(8,128)(2,1)} copy-done((bf16[4096,1280]{1,0:T(8,128)(2,1)}, bf16[4096,1280]{1,0:T(8,128)(2,1)S(1)}, u32[]{:S(2)}) %copy-start) | copy-done | bytes 10485784
  38.9 6.9 %collective-permute-done.4.x3.refs_6_ = bf16[384,640]{1,0:T(8,128)(2,1)S(1)} collective-permute-done((bf16[384,640]{1,0:T(8,128)(2,1)S(1)}, bf16[384,640]{1,0:T(8,128)(2,1)S(1)}, u32[]{:S(2)}, u32[]{:S(2)}) %collective-permute-start.4) | collective-permute-done | bytes 491552 | tf_op jit(solution)/shard_map/ppermute | solution.py:320
  45.8 4.0 %copy-done.1 = bf16[4096,1280]{1,0:T(8,128)(2,1)S(1)} copy-done((bf16[4096,1280]{1,0:T(8,128)(2,1)S(1)}, bf16[4096,1280]{1,0:T(8,128)(2,1)}, u32[]{:S(2)}) %copy-start.1) | copy-done | bytes 10485784
  49.7 3.2 %near_logits.2 = (f32[384,1280]{1,0:T(8,128)S(1)}, f32[384,1280]{1,0:T(8,128)S(1)}) custom-call(s32[8]{0:T(128)S(1)} %stack.50.perm, bf16[384,640]{1,0:T(8,128)(2,1)S(1)} %get-tuple-element.38.x0.refs_0_, bf16[384,640]{1,0:T(8,128)(2,1)S(1)} %collective-permute-done.x1.refs_2_, bf16[384,640]{1,0:T(8,128)(2,1)S(1)} %collective-permute-done.2.x2.refs_4_, ...), custom_call_target="tpu_custom_call" | custom-call | flops 2516582400 | bytes 15073312 | tf_op jit(solution)/shard_map/near_logits/pallas_call | solution.py:23
  53.7 4.8 %collective-permute-done.10 = bf16[384,640]{1,0:T(8,128)(2,1)S(1)} collective-permute-done((bf16[384,640]{1,0:T(8,128)(2,1)}, bf16[384,640]{1,0:T(8,128)(2,1)S(1)}, u32[]{:S(2)}, u32[]{:S(2)}) %collective-permute-start.10) | collective-permute-done | bytes 491552 | tf_op jit(solution)/shard_map/ppermute | solution.py:320
  63.6 3.2 %near_logits.3 = (f32[384,1280]{1,0:T(8,128)S(1)}, f32[384,1280]{1,0:T(8,128)S(1)}) custom-call(s32[8]{0:T(128)S(1)} %stack.50.perm, bf16[384,640]{1,0:T(8,128)(2,1)S(1)} %get-tuple-element.46.x0.refs_1_, bf16[384,640]{1,0:T(8,128)(2,1)S(1)} %collective-permute-done.8.x1.refs_3_, bf16[384,640]{1,0:T(8,128)(2,1)S(1)} %collective-permute-done.9.x2.refs_5_, ...), custom_call_target="tpu_custom_call" | custom-call | flops 2516582400 | bytes 15073312 | tf_op jit(solution)/shard_map/near_logits/pallas_call | solution.py:23
  66.8 9.4 %collective-permute-done.14 = bf16[384,640]{1,0:T(8,128)(2,1)S(1)} collective-permute-done((bf16[384,640]{1,0:T(8,128)(2,1)S(1)}, bf16[384,640]{1,0:T(8,128)(2,1)S(1)}, u32[]{:S(2)}, u32[]{:S(2)}) %collective-permute-start.14) | collective-permute-done | bytes 491552 | tf_op jit(solution)/shard_map/ppermute | solution.py:320
  76.2 3.7 %collective-permute-done.6.f.refs_12_ = bf16[384,640]{1,0:T(8,128)(2,1)S(1)} collective-permute-done((bf16[384,640]{1,0:T(8,128)(2,1)S(1)}, bf16[384,640]{1,0:T(8,128)(2,1)S(1)}, u32[]{:S(2)}, u32[]{:S(2)}) %collective-permute-start.6) | collective-permute-done | bytes 491552 | tf_op jit(solution)/shard_map/ppermute | solution.py:320
  81.2 2.5 %far_logits.4 = (f32[192,1280]{1,0:T(8,128)S(1)}, f32[192,1280]{1,0:T(8,128)S(1)}, f32[2,8,192]{2,1,0:T(8,128)S(1)}) custom-call(s32[8]{0:T(128)S(1)} %stack.50.perm, bf16[384,640]{1,0:T(8,128)(2,1)S(1)} %broadcast_select_fusion.3.far.refs_8_, bf16[384,640]{1,0:T(8,128)(2,1)S(1)} %collective-permute-done.6.f.refs_12_, bf16[4096,1280]{1,0:T(8,128)(2,1)S(1)} %copy-done.2, ...), custom_call_target="tpu_custom_call" | custom-call | flops 1258291200 | bytes 18034720 | tf_op jit(solution)/shard_map/far_logits/pallas_call | solution.py:23
  84.8 2.5 %far_logits.5 = (f32[192,1280]{1,0:T(8,128)S(1)}, f32[192,1280]{1,0:T(8,128)S(1)}, f32[2,8,192]{2,1,0:T(8,128)S(1)}) custom-call(s32[8]{0:T(128)S(1)} %stack.50.perm, bf16[384,640]{1,0:T(8,128)(2,1)S(1)} %broadcast_select_fusion.2.far.refs_9_, bf16[384,640]{1,0:T(8,128)(2,1)S(1)} %collective-permute-done.13.f.refs_13_, bf16[4096,1280]{1,0:T(8,128)(2,1)S(1)} %copy-done.2, ...), custom_call_target="tpu_custom_call" | custom-call | flops 1258291200 | bytes 18034720 | tf_op jit(solution)/shard_map/far_logits/pallas_call | solution.py:23
  87.3 6.8 %collective-permute-done.16.f.refs_14_ = bf16[384,640]{1,0:T(8,128)(2,1)S(1)} collective-permute-done((bf16[384,640]{1,0:T(8,128)(2,1)S(1)}, bf16[384,640]{1,0:T(8,128)(2,1)S(1)}, u32[]{:S(2)}, u32[]{:S(2)}) %collective-permute-start.16) | collective-permute-done | bytes 491552 | tf_op jit(solution)/shard_map/ppermute | solution.py:320
  94.1 2.5 %far_logits.6 = (f32[192,1280]{1,0:T(8,128)S(1)}, f32[192,1280]{1,0:T(8,128)S(1)}, f32[2,8,192]{2,1,0:T(8,128)S(1)}) custom-call(s32[8]{0:T(128)S(1)} %stack.50.perm, bf16[384,640]{1,0:T(8,128)(2,1)S(1)} %broadcast_select_fusion.1.far.refs_10_, bf16[384,640]{1,0:T(8,128)(2,1)S(1)} %collective-permute-done.16.f.refs_14_, bf16[4096,1280]{1,0:T(8,128)(2,1)S(1)} %copy-done.2, ...), custom_call_target="tpu_custom_call" | custom-call | flops 1258291200 | bytes 18034720 | tf_op jit(solution)/shard_map/far_logits/pallas_call | solution.py:23
  96.6 2.9 %collective-permute-done.18.f.refs_15_ = bf16[384,640]{1,0:T(8,128)(2,1)S(1)} collective-permute-done((bf16[384,640]{1,0:T(8,128)(2,1)S(1)}, bf16[384,640]{1,0:T(8,128)(2,1)S(1)}, u32[]{:S(2)}, u32[]{:S(2)}) %collective-permute-start.18) | collective-permute-done | bytes 491552 | tf_op jit(solution)/shard_map/ppermute | solution.py:320
  99.5 2.5 %far_logits.7 = (f32[192,1280]{1,0:T(8,128)S(1)}, f32[192,1280]{1,0:T(8,128)S(1)}, f32[2,8,192]{2,1,0:T(8,128)S(1)}) custom-call(s32[8]{0:T(128)S(1)} %stack.50.perm, bf16[384,640]{1,0:T(8,128)(2,1)S(1)} %broadcast_select_fusion.far.refs_11_, bf16[384,640]{1,0:T(8,128)(2,1)S(1)} %collective-permute-done.18.f.refs_15_, bf16[4096,1280]{1,0:T(8,128)(2,1)S(1)} %copy-done.2, ...), custom_call_target="tpu_custom_call" | custom-call | flops 1258291200 | bytes 18034720 | tf_op jit(solution)/shard_map/far_logits/pallas_call | solution.py:23
  105.9 5.2 %collective-permute-start.20 = (f32[2,8,192]{2,1,0:T(8,128)S(1)}, f32[2,8,192]{2,1,0:T(8,128)S(1)}, u32[]{:S(2)}, u32[]{:S(2)}) collective-permute-start(f32[2,8,192]{2,1,0:T(8,128)S(1)} %pad_maximum_fusion.4), channel_id=1, source_target_pairs={{0,4},{2,6},{4,0},{6,2},{8,12},{10,14},{12,8},{14,10},{1,5},{3,7},... | collective-permute-start | bytes 36872 | tf_op jit(solution)/shard_map/ppermute | solution.py:335
  112.8 3.1 %collective-permute-start.21 = (f32[2,8,192]{2,1,0:T(8,128)S(1)}, f32[2,8,192]{2,1,0:T(8,128)S(1)}, u32[]{:S(2)}, u32[]{:S(2)}) collective-permute-start(f32[2,8,192]{2,1,0:T(8,128)S(1)} %pad_maximum_fusion.5), channel_id=1, source_target_pairs={{0,8},{2,10},{4,12},{6,14},{8,0},{10,2},{12,4},{14,6},{1,9},{3,11}... | collective-permute-start | bytes 36872 | tf_op jit(solution)/shard_map/ppermute | solution.py:335
  117.6 2.9 %slopes.1 = (f32[768,1280]{1,0:T(8,128)S(1)}, f32[768,1280]{1,0:T(8,128)S(1)}, f32[8,192]{1,0:T(8,128)S(1)}) custom-call(f32[192,1280]{1,0:T(8,128)S(1)} %get-tuple-element.45.refs_0_, f32[192,1280]{1,0:T(8,128)S(1)} %get-tuple-element.52.refs_1_, f32[192,1280]{1,0:T(8,128)S(1)} %get-tuple-element.59.refs_2_, f32[192,1280]{1,0:T(8,128)S(1)} %get-tuple-element.63.refs_3_, ...), custom_call_target="tpu_custom_call" | custom-call | flops 11796480 | bytes 7888896 | tf_op jit(solution)/shard_map/slopes/pallas_call | solution.py:23
  121.2 3.1 %collective-permute-done.22 = f32[8,192]{1,0:T(8,128)S(1)} collective-permute-done((f32[8,192]{1,0:T(8,128)S(1)}, f32[8,192]{1,0:T(8,128)S(1)}, u32[]{:S(2)}, u32[]{:S(2)}) %collective-permute-start.22) | collective-permute-done | bytes 6176 | tf_op jit(solution)/shard_map/ppermute | solution.py:335
  127.9 2.9 %collective-permute-start.24 = (f32[8,192]{1,0:T(8,128)S(1)}, f32[8,192]{1,0:T(8,128)S(1)}, u32[]{:S(2)}, u32[]{:S(2)}) collective-permute-start(f32[8,192]{1,0:T(8,128)S(1)} %add.50), channel_id=1, source_target_pairs={{0,8},{2,10},{4,12},{6,14},{8,0},{10,2},{12,4},{14,6},{1,9},{3,11}... | collective-permute-start | bytes 18440 | tf_op jit(solution)/shard_map/ppermute | solution.py:335
  132.5 2.5 %gradient_to_send.1 = (bf16[768,1280]{1,0:T(8,128)(2,1)S(1)}, bf16[448,1280]{1,0:T(8,128)(2,1)}) custom-call(s32[1]{0:T(128)} %bitcast.8.tok, bf16[1024,768]{1,0:T(8,128)(2,1)S(1)} %turned_features.1.features, f32[768,1280]{1,0:T(8,128)S(1)} %get-tuple-element.70.slope, f32[768,1280]{1,0:T(8,128)S(1)} %get-tuple-element.71.scaled, f32[8,192]{1,0:T(8,128)S(1)} %add.51.inner), custom_call_target="tpu_custom_call" | custom-call | flops 1006632960 | bytes 9443332 | tf_op jit(solution)/shard_map/gradient_to_send/pallas_call | solution.py:23
  138.2 2.4 %summed_gradient.1 = bf16[448,1280]{1,0:T(8,128)(2,1)} custom-call(f32[448,1280]{1,0:T(8,128)S(1)} %gradient_to_keep.1.keep, bf16[448,1280]{1,0:T(8,128)(2,1)} %collective-permute-done.25.received), custom_call_target="tpu_custom_call" | custom-call | flops 573440 | bytes 3440640 | tf_op jit(solution)/shard_map/summed_gradient/pallas_call | solution.py:23
  (88 shorter events, 41.6 us)
Async XLA Ops:
  3.0 15.1 %collective-permute-start = (bf16[384,640]{1,0:T(8,128)(2,1)S(1)}, bf16[384,640]{1,0:T(8,128)(2,1)S(1)}, u32[]{:S(2)}, u32[]{:S(2)}) collective-permute-start(bf16[384,640]{1,0:T(8,128)(2,1)S(1)} %get-tuple-element.38.x0.refs_0_), channel_id=1, source_target_pairs={{0,4},{2,6},{4,0},{6,2},{8,12},{10,14},{12,8},{14,10},{1,5},{3,7},... | collective-permute-start | bytes 1474568 | tf_op jit(solution)/shard_map/ppermute | solution.py:320
  6.0 15.2 %collective-permute-start.2 = (bf16[384,640]{1,0:T(8,128)(2,1)S(1)}, bf16[384,640]{1,0:T(8,128)(2,1)S(1)}, u32[]{:S(2)}, u32[]{:S(2)}) collective-permute-start(bf16[384,640]{1,0:T(8,128)(2,1)S(1)} %get-tuple-element.38.x0.refs_0_), channel_id=1, source_target_pairs={{0,2},{2,0},{4,6},{6,4},{8,10},{10,8},{12,14},{14,12},{1,3},{3,1},... | collective-permute-start | bytes 1474568 | tf_op jit(solution)/shard_map/ppermute | solution.py:320
  7.5 26.0 %collective-permute-start.8 = (bf16[384,640]{1,0:T(8,128)(2,1)S(1)}, bf16[384,640]{1,0:T(8,128)(2,1)S(1)}, u32[]{:S(2)}, u32[]{:S(2)}) collective-permute-start(bf16[384,640]{1,0:T(8,128)(2,1)S(1)} %get-tuple-element.46.x0.refs_1_), channel_id=1, source_target_pairs={{0,4},{2,6},{4,0},{6,2},{8,12},{10,14},{12,8},{14,10},{1,5},{3,7},... | collective-permute-start | bytes 1474568 | tf_op jit(solution)/shard_map/ppermute | solution.py:320
  8.0 26.9 %collective-permute-start.9 = (bf16[384,640]{1,0:T(8,128)(2,1)S(1)}, bf16[384,640]{1,0:T(8,128)(2,1)S(1)}, u32[]{:S(2)}, u32[]{:S(2)}) collective-permute-start(bf16[384,640]{1,0:T(8,128)(2,1)S(1)} %get-tuple-element.46.x0.refs_1_), channel_id=1, source_target_pairs={{0,2},{2,0},{4,6},{6,4},{8,10},{10,8},{12,14},{14,12},{1,3},{3,1},... | collective-permute-start | bytes 1474568 | tf_op jit(solution)/shard_map/ppermute | solution.py:320
  8.2 28.9 %collective-permute-start.7 = (bf16[448,1280]{1,0:T(8,128)(2,1)}, bf16[448,1280]{1,0:T(8,128)(2,1)}, u32[]{:S(2)}, u32[]{:S(2)}) collective-permute-start(bf16[448,1280]{1,0:T(8,128)(2,1)} %mine.1), channel_id=1, source_target_pairs={{0,1},{1,0},{2,3},{3,2},{4,5},{5,4},{6,7},{7,6},{8,9},{9,8},{10,11... | collective-permute-start | bytes 3440648 | tf_op jit(solution)/shard_map/ppermute | solution.py:361
  19.0 12.6 %collective-permute-start.1 = (bf16[384,640]{1,0:T(8,128)(2,1)}, bf16[384,640]{1,0:T(8,128)(2,1)}, u32[]{:S(2)}, u32[]{:S(2)}) collective-permute-start(bf16[384,640]{1,0:T(8,128)(2,1)} %pad_maximum_fusion), channel_id=1, source_target_pairs={{4,8},{8,4},{6,10},{10,6},{5,9},{9,5},{7,11},{11,7},{20,24},{24,20... | collective-permute-start | bytes 1474568 | tf_op jit(solution)/shard_map/ppermute | solution.py:320
  21.3 13.6 %collective-permute-start.5 = (bf16[384,640]{1,0:T(8,128)(2,1)}, bf16[384,640]{1,0:T(8,128)(2,1)}, u32[]{:S(2)}, u32[]{:S(2)}) collective-permute-start(bf16[384,640]{1,0:T(8,128)(2,1)} %pad_maximum_fusion.1), channel_id=1, source_target_pairs={{4,8},{8,4},{6,10},{10,6},{5,9},{9,5},{7,11},{11,7},{20,24},{24,20... | collective-permute-start | bytes 1474568 | tf_op jit(solution)/shard_map/ppermute | solution.py:320
  31.5 14.2 %collective-permute-start.4 = (bf16[384,640]{1,0:T(8,128)(2,1)S(1)}, bf16[384,640]{1,0:T(8,128)(2,1)S(1)}, u32[]{:S(2)}, u32[]{:S(2)}) collective-permute-start(bf16[384,640]{1,0:T(8,128)(2,1)S(1)} %collective-permute-done.x1.refs_2_), channel_id=1, source_target_pairs={{0,2},{2,0},{4,6},{6,4},{8,10},{10,8},{12,14},{14,12},{1,3},{3,1},... | collective-permute-start | bytes 1474568 | tf_op jit(solution)/shard_map/ppermute | solution.py:320
  33.6 19.4 %collective-permute-start.3 = (bf16[384,640]{1,0:T(8,128)(2,1)}, bf16[384,640]{1,0:T(8,128)(2,1)S(1)}, u32[]{:S(2)}, u32[]{:S(2)}) collective-permute-start(bf16[384,640]{1,0:T(8,128)(2,1)} %collective-permute-done.1), channel_id=1, source_target_pairs={{4,0},{6,2},{8,12},{10,14},{5,1},{7,3},{9,13},{11,15},{20,16},{22,... | collective-permute-start | bytes 1474568 | tf_op jit(solution)/shard_map/ppermute | solution.py:320
  34.9 23.6 %collective-permute-start.10 = (bf16[384,640]{1,0:T(8,128)(2,1)}, bf16[384,640]{1,0:T(8,128)(2,1)S(1)}, u32[]{:S(2)}, u32[]{:S(2)}) collective-permute-start(bf16[384,640]{1,0:T(8,128)(2,1)} %collective-permute-done.5), channel_id=1, source_target_pairs={{4,0},{6,2},{8,12},{10,14},{5,1},{7,3},{9,13},{11,15},{20,16},{22,... | collective-permute-start | bytes 1474568 | tf_op jit(solution)/shard_map/ppermute | solution.py:320
  36.3 22.2 %collective-permute-start.12 = (bf16[384,640]{1,0:T(8,128)(2,1)S(1)}, bf16[384,640]{1,0:T(8,128)(2,1)S(1)}, u32[]{:S(2)}, u32[]{:S(2)}) collective-permute-start(bf16[384,640]{1,0:T(8,128)(2,1)S(1)} %pad_maximum_fusion.2), channel_id=1, source_target_pairs={{4,8},{8,4},{6,10},{10,6},{5,9},{9,5},{7,11},{11,7},{20,24},{24,20... | collective-permute-start | bytes 1474568 | tf_op jit(solution)/shard_map/ppermute | solution.py:320
  37.1 21.5 %collective-permute-start.11 = (bf16[384,640]{1,0:T(8,128)(2,1)S(1)}, bf16[384,640]{1,0:T(8,128)(2,1)S(1)}, u32[]{:S(2)}, u32[]{:S(2)}) collective-permute-start(bf16[384,640]{1,0:T(8,128)(2,1)S(1)} %collective-permute-done.8.x1.refs_3_), channel_id=1, source_target_pairs={{0,2},{2,0},{4,6},{6,4},{8,10},{10,8},{12,14},{14,12},{1,3},{3,1},... | collective-permute-start | bytes 1474568 | tf_op jit(solution)/shard_map/ppermute | solution.py:320
  53.0 9.1 %collective-permute-start.15 = (bf16[384,640]{1,0:T(8,128)(2,1)S(1)}, bf16[384,640]{1,0:T(8,128)(2,1)S(1)}, u32[]{:S(2)}, u32[]{:S(2)}) collective-permute-start(bf16[384,640]{1,0:T(8,128)(2,1)S(1)} %pad_maximum_fusion.3), channel_id=1, source_target_pairs={{4,8},{8,4},{6,10},{10,6},{5,9},{9,5},{7,11},{11,7},{20,24},{24,20... | collective-permute-start | bytes 1474568 | tf_op jit(solution)/shard_map/ppermute | solution.py:320
  58.6 25.2 %collective-permute-start.13 = (bf16[384,640]{1,0:T(8,128)(2,1)S(1)}, bf16[384,640]{1,0:T(8,128)(2,1)S(1)}, u32[]{:S(2)}, u32[]{:S(2)}) collective-permute-start(bf16[384,640]{1,0:T(8,128)(2,1)S(1)} %broadcast_select_fusion.2.far.refs_9_), channel_id=1, source_target_pairs={{0,2},{2,0},{4,6},{6,4},{8,10},{10,8},{12,14},{14,12},{1,3},{3,1},... | collective-permute-start | bytes 1474568 | tf_op jit(solution)/shard_map/ppermute | solution.py:320
  59.3 16.9 %collective-permute-start.14 = (bf16[384,640]{1,0:T(8,128)(2,1)S(1)}, bf16[384,640]{1,0:T(8,128)(2,1)S(1)}, u32[]{:S(2)}, u32[]{:S(2)}) collective-permute-start(bf16[384,640]{1,0:T(8,128)(2,1)S(1)} %collective-permute-done.12), channel_id=1, source_target_pairs={{4,0},{6,2},{8,12},{10,14},{5,1},{7,3},{9,13},{11,15},{20,16},{22,... | collective-permute-start | bytes 1474568 | tf_op jit(solution)/shard_map/ppermute | solution.py:320
  60.6 19.3 %collective-permute-start.6 = (bf16[384,640]{1,0:T(8,128)(2,1)S(1)}, bf16[384,640]{1,0:T(8,128)(2,1)S(1)}, u32[]{:S(2)}, u32[]{:S(2)}) collective-permute-start(bf16[384,640]{1,0:T(8,128)(2,1)S(1)} %broadcast_select_fusion.3.far.refs_8_), channel_id=1, source_target_pairs={{0,2},{2,0},{4,6},{6,4},{8,10},{10,8},{12,14},{14,12},{1,3},{3,1},... | collective-permute-start | bytes 1474568 | tf_op jit(solution)/shard_map/ppermute | solution.py:320
  62.1 21.6 %collective-permute-start.17 = (bf16[384,640]{1,0:T(8,128)(2,1)S(1)}, bf16[384,640]{1,0:T(8,128)(2,1)S(1)}, u32[]{:S(2)}, u32[]{:S(2)}) collective-permute-start(bf16[384,640]{1,0:T(8,128)(2,1)S(1)} %collective-permute-done.15), channel_id=1, source_target_pairs={{4,0},{6,2},{8,12},{10,14},{5,1},{7,3},{9,13},{11,15},{20,16},{22,... | collective-permute-start | bytes 1474568 | tf_op jit(solution)/shard_map/ppermute | solution.py:320
  80.0 14.2 %collective-permute-start.16 = (bf16[384,640]{1,0:T(8,128)(2,1)S(1)}, bf16[384,640]{1,0:T(8,128)(2,1)S(1)}, u32[]{:S(2)}, u32[]{:S(2)}) collective-permute-start(bf16[384,640]{1,0:T(8,128)(2,1)S(1)} %broadcast_select_fusion.1.far.refs_10_), channel_id=1, source_target_pairs={{0,2},{2,0},{4,6},{6,4},{8,10},{10,8},{12,14},{14,12},{1,3},{3,1},... | collective-permute-start | bytes 1474568 | tf_op jit(solution)/shard_map/ppermute | solution.py:320
  83.8 15.7 %collective-permute-start.18 = (bf16[384,640]{1,0:T(8,128)(2,1)S(1)}, bf16[384,640]{1,0:T(8,128)(2,1)S(1)}, u32[]{:S(2)}, u32[]{:S(2)}) collective-permute-start(bf16[384,640]{1,0:T(8,128)(2,1)S(1)} %broadcast_select_fusion.far.refs_11_), channel_id=1, source_target_pairs={{0,2},{2,0},{4,6},{6,4},{8,10},{10,8},{12,14},{14,12},{1,3},{3,1},... | collective-permute-start | bytes 1474568 | tf_op jit(solution)/shard_map/ppermute | solution.py:320
  102.0 3.8 %collective-permute-start.19 = (f32[2,8,192]{2,1,0:T(8,128)S(1)}, f32[2,8,192]{2,1,0:T(8,128)S(1)}, u32[]{:S(2)}, u32[]{:S(2)}) collective-permute-start(f32[2,8,192]{2,1,0:T(8,128)S(1)} %get-tuple-element.68.refs_8_), channel_id=1, source_target_pairs={{0,2},{2,0},{4,6},{6,4},{8,10},{10,8},{12,14},{14,12},{1,3},{3,1},... | collective-permute-start | bytes 36872 | tf_op jit(solution)/shard_map/ppermute | solution.py:335
  105.9 6.9 %collective-permute-start.20 = (f32[2,8,192]{2,1,0:T(8,128)S(1)}, f32[2,8,192]{2,1,0:T(8,128)S(1)}, u32[]{:S(2)}, u32[]{:S(2)}) collective-permute-start(f32[2,8,192]{2,1,0:T(8,128)S(1)} %pad_maximum_fusion.4), channel_id=1, source_target_pairs={{0,4},{2,6},{4,0},{6,2},{8,12},{10,14},{12,8},{14,10},{1,5},{3,7},... | collective-permute-start | bytes 36872 | tf_op jit(solution)/shard_map/ppermute | solution.py:335
  112.8 4.8 %collective-permute-start.21 = (f32[2,8,192]{2,1,0:T(8,128)S(1)}, f32[2,8,192]{2,1,0:T(8,128)S(1)}, u32[]{:S(2)}, u32[]{:S(2)}) collective-permute-start(f32[2,8,192]{2,1,0:T(8,128)S(1)} %pad_maximum_fusion.5), channel_id=1, source_target_pairs={{0,8},{2,10},{4,12},{6,14},{8,0},{10,2},{12,4},{14,6},{1,9},{3,11}... | collective-permute-start | bytes 36872 | tf_op jit(solution)/shard_map/ppermute | solution.py:335
  120.6 3.7 %collective-permute-start.22 = (f32[8,192]{1,0:T(8,128)S(1)}, f32[8,192]{1,0:T(8,128)S(1)}, u32[]{:S(2)}, u32[]{:S(2)}) collective-permute-start(f32[8,192]{1,0:T(8,128)S(1)} %get-tuple-element.69), channel_id=1, source_target_pairs={{0,2},{2,0},{4,6},{6,4},{8,10},{10,8},{12,14},{14,12},{1,3},{3,1},... | collective-permute-start | bytes 18440 | tf_op jit(solution)/shard_map/ppermute | solution.py:335
  127.9 4.5 %collective-permute-start.24 = (f32[8,192]{1,0:T(8,128)S(1)}, f32[8,192]{1,0:T(8,128)S(1)}, u32[]{:S(2)}, u32[]{:S(2)}) collective-permute-start(f32[8,192]{1,0:T(8,128)S(1)} %add.50), channel_id=1, source_target_pairs={{0,8},{2,10},{4,12},{6,14},{8,0},{10,2},{12,4},{14,6},{1,9},{3,11}... | collective-permute-start | bytes 18440 | tf_op jit(solution)/shard_map/ppermute | solution.py:335
  (12 other events, 119.2 us)

commit v3 on v2

v3 whole, which is shorter than its diff:
```python
import functools

import jax
import jax.numpy as jnp
from jax import lax
from jax.experimental import pallas as pl
from jax.experimental.pallas import tpu as pltpu
from jax.sharding import PartitionSpec as P

F32, BF16 = jnp.float32, jnp.bfloat16
SCOPED_BYTES = 12 * 2**20
LANES = 128
BLOCK = 16

VMEM = pl.BlockSpec(memory_space=pltpu.VMEM)
SMEM = pl.BlockSpec(memory_space=pltpu.SMEM)
ANYWHERE = pl.BlockSpec(memory_space=pl.ANY)


def _kernel(body, outs, ins, name, flops=0, scratch=(), specs=None, out_specs=None, exps=0):
    specs = specs or [VMEM] * len(ins)
    ins = [pltpu.with_memory_space_constraint(x, pltpu.VMEM) if s is VMEM else x for x, s in zip(ins, specs, strict=True)]
    return pl.pallas_call(
        body,
        in_specs=specs,
        out_specs=out_specs or [VMEM] * len(outs),
        out_shape=outs,
        scratch_shapes=scratch,
        compiler_params=pltpu.CompilerParams(vmem_limit_bytes=SCOPED_BYTES),
        cost_estimate=pl.CostEstimate(
            flops=flops,
            bytes_accessed=sum(x.size * x.dtype.itemsize for x in ins),
            transcendentals=exps,
        ),
        name=name,
    )(*ins)


def _eye(n):
    return lax.broadcasted_iota(jnp.int32, (n, n), 0) == lax.broadcasted_iota(jnp.int32, (n, n), 1)


def _to_row(eye, column):
    return jnp.sum(jnp.where(eye, column, 0.0), axis=0, keepdims=True)


def _to_column(eye, row):
    return jnp.sum(jnp.where(eye, row, 0.0), axis=1, keepdims=True)


def _dot(a, b):
    return jnp.dot(a, b, preferred_element_type=F32)


def _place(index, size):
    return pl.ds(pl.multiple_of(index * size, size), size)


def _pack_kernel(starts, target, draft, *refs):
    *outs, drafts, sems = refs
    feats, draft_feats = target.shape[1], draft.shape[0]
    first = pltpu.make_async_copy(draft, drafts.at[:draft_feats, :], sems.at[len(outs)])
    first.start()
    copies = []
    for n, (out, start) in enumerate(zip(outs, starts, strict=True)):
        copies.append(
            pltpu.make_async_copy(target.at[start : start + out.shape[0], :], out.at[:, :feats], sems.at[n])
        )
        copies[-1].start()
    drafts[draft_feats:, :] = jnp.zeros((LANES - draft_feats, drafts.shape[1]), BF16)
    first.wait()
    turned = jnp.transpose(drafts[...])
    for out, start in zip(outs, starts, strict=True):
        out[:, feats:] = turned[start : start + out.shape[0], :]
    for copy in copies:
        copy.wait()


def _pack(target, draft, sizes, joint):
    rows_all, feats = target.shape
    starts = [sum(sizes[:n]) for n in range(len(sizes))]
    if joint:
        sizes, starts = [*sizes, sizes[0] + sizes[1]], [*starts, 0]
    hbm = pl.BlockSpec(memory_space=pltpu.HBM)
    return _kernel(
        functools.partial(_pack_kernel, starts),
        [pltpu.VMEM((rows, feats + LANES), BF16) for rows in sizes],
        [pltpu.with_memory_space_constraint(x, pltpu.HBM) for x in (target, draft.T)],
        "packed_hidden",
        specs=[hbm, hbm],
        scratch=[pltpu.VMEM((LANES, rows_all), BF16), pltpu.SemaphoreType.DMA((len(sizes) + 1,))],
    )


def _head_kernel(tok, mine, other, out):
    part = mine.shape[0] // 4
    out[...] = jnp.zeros_like(out)
    for which, ref in ((tok[0], mine), (1 - tok[0], other)):
        for b in range(4):
            start = pl.multiple_of(which * (4 * LANES) + b * LANES, LANES)
            out[pl.ds(start, part), :] = ref[b * part : (b + 1) * part, :]


def _head(tok, mine, other):
    plain = pl.BlockSpec()
    return _kernel(
        _head_kernel,
        [pltpu.VMEM((8 * LANES, mine.shape[1]), BF16)],
        [tok, mine, other],
        "draft_head",
        specs=[SMEM, plain, VMEM],
    )[0]


def _join_kernel(start, first, second, out):
    rows = out.shape[0] // 2
    out[:rows, :] = first[start : start + rows, :]
    out[rows:, :] = second[start : start + rows, :]


def _join(first, second, start, rows):
    out = pltpu.VMEM((2 * rows, first.shape[1]), first.dtype)
    return _kernel(functools.partial(_join_kernel, start), [out], [first, second], "joined_rows")[0]


def _columns(vocab, cols=256):
    return [slice(n, n + cols) for n in range(0, vocab, cols)]


def _accumulate(blocks, pieces, wt, wd, before, out_t, out_d, rows):
    feats = pieces[0][0].shape[1] - LANES
    xs = [ref[start : start + rows, :] for ref, start, _ in pieces]
    drafts = jnp.concatenate([x[:, feats:] for x in xs], axis=1)
    for c in _columns(wt.shape[1]):
        target = before[0][before[2] : before[2] + rows, c] if before else None
        for x, (_, _, block) in zip(xs, pieces, strict=True):
            term = _dot(x[:, :feats], wt[_place(blocks[block], feats), c])
            target = term if target is None else target + term
        head = jnp.concatenate([wd[_place(blocks[block], LANES), c] for _, _, block in pieces], axis=0)
        draft = _dot(drafts, head)
        out_t[:rows, c] = target
        out_d[:rows, c] = draft + before[1][before[2] : before[2] + rows, c] if before else draft


def _logits_kernel(where, start, rows, blocks, *refs):
    arrays, (wt, wd, *acc, out_t, out_d) = refs[: len(where)], refs[len(where) :]
    pieces = [(ref, first, block) for ref, group in zip(arrays, where, strict=True) for first, block in group]
    _accumulate(blocks, pieces, wt, wd, (*acc, start) if acc else None, out_t, out_d, rows)


def _logits(blocks, pieces, rows, wt, wd, acc=(), start=0):
    out = pltpu.VMEM((rows, wt.shape[1]), F32)
    where = [group for _, group in pieces]
    return _kernel(
        functools.partial(_logits_kernel, where, start, rows),
        [out, out],
        [blocks, *[array for array, _ in pieces], wt, wd, *acc],
        "logits",
        flops=2 * rows * pieces[0][0].shape[1] * wt.shape[1] * sum(map(len, where)),
        specs=[SMEM] + [VMEM] * (len(pieces) + 2 + len(acc)),
    )


def _exp_kernel(where, start, rows, index, extra, blocks, *refs):
    arrays, (wt, wd, acc_t, acc_d, *rest) = refs[: len(where)], refs[len(where) :]
    *more, before, e_t, e_d, stats = rest
    pieces = [(ref, first, block) for ref, group in zip(arrays, where, strict=True) for first, block in group]
    _accumulate(blocks, pieces, wt, wd, (acc_t, acc_d, start), e_t, e_d, rows)
    whole = rows + extra
    eye = _eye(whole)
    stats[...] = before[...]
    for kind, ref in enumerate((e_t, e_d)):
        tops, sums = [], []
        for r in range(0, whole, BLOCK):
            logits = ref[r : r + BLOCK, :] if r < rows else more[kind][r - rows : r - rows + BLOCK, :]
            top = jnp.max(logits, axis=1, keepdims=True)
            e = jnp.exp(logits - top)
            ref[r : r + BLOCK, :] = e
            tops.append(top)
            sums.append(jnp.sum(e, axis=1, keepdims=True))
        row = 2 * index + kind
        stats[0, row : row + 1, :whole] = _to_row(eye, jnp.concatenate(tops, axis=0))
        stats[1, row : row + 1, :whole] = _to_row(eye, jnp.concatenate(sums, axis=0))


def _exps(blocks, pieces, rows, wt, wd, acc, start, stats, index, more=()):
    extra = more[0].shape[0] if more else 0
    out = pltpu.VMEM((rows + extra, wt.shape[1]), F32)
    where = [group for _, group in pieces]
    return _kernel(
        functools.partial(_exp_kernel, where, start, rows, index, extra),
        [out, out, pltpu.VMEM(stats.shape, F32)],
        [blocks, *[array for array, _ in pieces], wt, wd, *acc, *more, stats],
        "exp_logits",
        flops=2 * rows * pieces[0][0].shape[1] * wt.shape[1] * sum(map(len, where)),
        exps=2 * (rows + extra) * wt.shape[1],
        specs=[SMEM] + [VMEM] * (len(pieces) + 5 + len(more)),
    )


def _slope_kernel(full, *refs):
    sets = (len(refs) - 5) // 2
    es_t, es_d = refs[:sets], refs[sets : 2 * sets]
    mine, total, slope_out, scaled_out, sums = refs[2 * sets :]
    sums[...] = jnp.zeros_like(sums)
    first = 0
    for i in range(sets):
        rows = es_t[i].shape[0]
        eye = _eye(rows)
        scales = [
            full
            * _to_column(
                eye,
                jnp.exp(mine[0, r : r + 1, :rows] - total[0, r : r + 1, :rows]) / total[1, r : r + 1, :rows],
            )
            for r in (2 * i, 2 * i + 1)
        ]
        losses, inners = [], []
        for r in range(0, rows, BLOCK):
            target = es_t[i][r : r + BLOCK, :] * scales[0][r : r + BLOCK]
            draft = es_d[i][r : r + BLOCK, :] * scales[1][r : r + BLOCK]
            spread = draft - target
            square = spread * spread + 1.0
            inverse = lax.rsqrt(square)
            slope = spread * inverse
            slope_out[first + r : first + r + BLOCK, :] = slope
            scaled_out[first + r : first + r + BLOCK, :] = draft
            losses.append(jnp.sum(square * inverse - 1.0, axis=1, keepdims=True))
            inners.append(jnp.sum(draft * slope, axis=1, keepdims=True))
        sums[2 * i : 2 * i + 1, :rows] = _to_row(eye, jnp.concatenate(losses, axis=0)) * (0.5 / full)
        sums[2 * i + 1 : 2 * i + 2, :rows] = _to_row(eye, jnp.concatenate(inners, axis=0)) * (1.0 / full)
        first += rows


def _slopes(es_t, es_d, mine, total, full):
    rows_all, vocab = sum(e.shape[0] for e in es_t), es_t[0].shape[1]
    out = pltpu.VMEM((rows_all, vocab), F32)
    return _kernel(
        functools.partial(_slope_kernel, full),
        [out, out, pltpu.VMEM(mine.shape[1:], F32)],
        [*es_t, *es_d, mine, total],
        "slopes",
        flops=12 * rows_all * vocab,
        exps=rows_all * vocab,
    )


def _turn_kernel(plan, blocks, *refs):
    out = refs[-1]
    feats = refs[0].shape[1] - LANES
    part = lambda ref, start, rows: refs[ref][start : start + rows, feats:]
    for block, rows_of in plan:
        columns = []
        for choices in rows_of:
            value = part(*choices[0])
            if len(choices) == 2:
                value = jnp.where(blocks[16] == 1, value, part(*choices[1]))
            columns.append(value)
        out[_place(blocks[block], LANES), :] = jnp.transpose(jnp.concatenate(columns, axis=0))


def _turn(blocks, arrays, plan, rows_all):
    return _kernel(
        functools.partial(_turn_kernel, plan),
        [pltpu.VMEM((8 * LANES, rows_all), BF16)],
        [blocks, *arrays],
        "turned_features",
        specs=[SMEM] + [VMEM] * len(arrays),
        flops=16 * LANES * rows_all,
    )[0]


def _gradient(features, which, grad, out, scale):
    part = out.shape[0] // 4
    half = features.shape[0] // 2
    for c in _columns(grad.shape[1], 256):
        product = _dot(features[_place(which, half), :], grad[:, c]) * scale
        for b in range(4):
            out[b * part : (b + 1) * part, c] = product[b * LANES : b * LANES + part].astype(out.dtype)


def _send_kernel(tokens, sizes, tok, features, slope, scaled, inner, grad, out):
    first = 0
    for i, rows in enumerate(sizes):
        column = _to_column(_eye(rows), inner[2 * i + 1 : 2 * i + 2, :rows])
        for r in range(0, rows, BLOCK):
            here = slice(first + r, first + r + BLOCK)
            grad[here, :] = (scaled[here, :] * (slope[here, :] - column[r : r + BLOCK])).astype(BF16)
        first += rows
    _gradient(features, 1 - tok[0], grad, out, 1.0 / tokens)


def _send(tok, features, slope, scaled, inner, tokens, sizes, part):
    rows_all, vocab = slope.shape
    return _kernel(
        functools.partial(_send_kernel, tokens, sizes),
        [pltpu.VMEM((rows_all, vocab), BF16), pltpu.VMEM((part, vocab), BF16)],
        [tok, features, slope, scaled, inner],
        "gradient_to_send",
        specs=[SMEM] + [VMEM] * 4,
        flops=features.shape[0] * rows_all * vocab,
    )


def _keep_kernel(tokens, tok, features, grad, out):
    _gradient(features, tok[0], grad, out, 1.0 / tokens)


def _keep(tok, features, grad, tokens, part):
    rows_all, vocab = grad.shape
    return _kernel(
        functools.partial(_keep_kernel, tokens),
        [pltpu.VMEM((part, vocab), F32)],
        [tok, features, grad],
        "gradient_to_keep",
        specs=[SMEM, VMEM, VMEM],
        flops=features.shape[0] * rows_all * vocab,
    )[0]


def _add_kernel(keep, received, out, came, summed, came_sem, out_sem):
    blocks, part = came.shape[:2]
    place = lambda b: slice(b * part, (b + 1) * part)
    fetch = [pltpu.make_async_copy(received.at[place(b), :], came.at[b], came_sem.at[b]) for b in range(blocks)]
    store = [pltpu.make_async_copy(summed.at[b], out.at[place(b), :], out_sem.at[b]) for b in range(blocks)]
    for copy in fetch:
        copy.start()
    for b in range(blocks):
        fetch[b].wait()
        summed[b] = (keep[place(b), :] + came[b].astype(F32)).astype(BF16)
        store[b].start()
    for copy in store:
        copy.wait()


def _add(keep, received):
    rows, vocab = keep.shape
    blocks = pltpu.VMEM((4, rows // 4, vocab), BF16)
    return _kernel(
        _add_kernel,
        [jax.ShapeDtypeStruct(keep.shape, BF16)],
        [keep, received],
        "summed_gradient",
        specs=[VMEM, ANYWHERE],
        out_specs=[ANYWHERE],
        scratch=[blocks, blocks, pltpu.SemaphoreType.DMA((4,)), pltpu.SemaphoreType.DMA((4,))],
        flops=keep.size,
    )[0]


REST = 64
MERGED = False
SLOTS = (
    ("O0", "S", "P0", "P1", "T",),
    ("M0", "O1",),
    ("M1", "U0", "A0",),
    ("M2", "U1", "A1",),
    ("M3", "U2", "F0",),
    ("U3", "F1",),
    ("X", "Y", "F2",),
    ("W", "F3",),
)
FREE = ("T",)
EARLY = ()
WORK = ((), (), (), (), ("G", "N0",), ("N1",), ("E0",), ("E1", "H",), ("R", "E2", "D", "E3",))


def _xor(k):
    return [(i, i ^ k) for i in range(8)]


MIDDLE = [(2, 4), (4, 2), (3, 5), (5, 3)]
OUTWARD = [(2, 0), (3, 1), (4, 6), (5, 7)]
PAIRS = {"S": _xor(1), "O": _xor(1), "A": _xor(1), "F": _xor(1), "P": _xor(2), "X": _xor(2), "Y": _xor(4), "W": _xor(6)}
PAIRS["T"] = [(0, 1), (1, 0)]
PAIRS |= {"M": MIDDLE, "U": OUTWARD}


def _all_reduce(x, merge):
    for k in (1, 2, 4):
        x = merge(x, lax.ppermute(x, "voc", _xor(k)))
    return x


def _merge_softmax(a, b):
    top = jnp.maximum(a[0], b[0])
    return jnp.stack([top, a[1] * jnp.exp(a[0] - top) + b[1] * jnp.exp(b[0] - top)])


def _body_4x2(target_hidden, draft_hidden, target_head, draft_head):
    rows_all = target_hidden.shape[0]
    part, vocab = draft_head.shape
    rest, chunks = REST, 4
    q = (rows_all - rest) // chunks
    sizes = (q, q, q, q + rest)
    full = float(vocab * lax.axis_size("voc"))
    tokens = float(rows_all * lax.axis_size("tok"))
    me, tok = lax.axis_index("voc"), lax.axis_index("tok")
    z, x = me // 2, me % 2
    end = (z == 0) | (z == 3)
    far_z = (jnp.where(z < 2, 2, 1), jnp.where(z < 2, 3, 0))
    blocks = [me, me ^ 2, me ^ 1, me ^ 3] + [2 * fz + side for side in (x, 1 - x) for fz in far_z]
    blocks = jnp.stack(blocks + [me ^ k for k in range(8)] + [end]).astype(jnp.int32)
    tok_index = tok.reshape(1).astype(jnp.int32)

    own0, own1, own_rest, *own_both = _pack(target_hidden, draft_hidden, [2 * q, 2 * q, rest], MERGED)
    own = (own0, own1)
    wt = target_head
    got, far, acc, wd = {}, {}, {}, None

    def rest_of(name):
        if name == "S" and "SS" not in got:
            got["SS"] = jnp.concatenate([own_rest, got["S"]])
        return got["SS" if name == "S" else name]

    def operand(name):
        kind, index = name[0], int(name[1:] or 0)
        if kind == "S":
            return own_rest
        if kind == "T":
            return draft_head
        if kind == "O" and MERGED:
            return own_both[0]
        if kind in "XYW":
            return rest_of("S")
        if kind in "PO":
            return own[index]
        if kind == "A":
            return got[f"P{index}"]
        if kind == "M":
            return jnp.concatenate([h[(index % 2) * q : (index % 2) * q + q] for h in (own[index // 2], got[f"P{index // 2}"])])
        if kind == "U":
            return got[f"M{index}"]
        far[index] = jnp.where(end, got[f"U{index}"], got[f"M{index}"])
        return far[index]

    def after(earlier):
        return lax.optimization_barrier((blocks, earlier))[0] if earlier is not None else blocks

    def other_x(h):
        return (got["O"], 2 * q * h) if MERGED else (got[f"O{h}"], 0)

    es_t, es_d, stats = [], [], jnp.zeros((2, 8, -(-max(sizes) // LANES) * LANES), F32)
    result = None

    def far_pieces(c):
        return [(far[c], [(0, 4), (q, 5)]), (got[f"F{c}"], [(0, 6), (q, 7)])]

    def rest_pieces(names, first):
        return [(rest_of(name), [(0, first + 2 * k), (rest, first + 2 * k + 1)]) for k, name in enumerate(names)]

    def work(name):
        nonlocal stats, result, wd
        tied = lax.optimization_barrier((blocks, result))[0] if result is not None else blocks
        kind, c = name[0], int(name[1:] or 0)
        if kind == "G":
            wd = result = _head(tok_index, draft_head, got["T"])
        elif kind == "N":
            pieces = ((own[c], 0), (got[f"P{c}"], 0), other_x(c), (got[f"A{c}"], 0))
            acc[c] = _logits(tied, [(array, [(at, k)]) for k, (array, at) in enumerate(pieces)], 2 * q, wt, wd)
            result = acc[c][0]
        elif kind in "HRD":
            if kind == "H":
                acc[kind] = _logits(tied, far_pieces(3)[:1], q, wt, wd, acc[1], q)
            elif kind == "R":
                acc[kind] = _logits(tied, rest_pieces("SX", 8), rest, wt, wd)
            else:
                acc[kind] = _logits(tied, rest_pieces("YW", 12), rest, wt, wd, acc["R"])
            result = acc[kind][0]
        else:
            last = c == chunks - 1
            e_t, e_d, stats = _exps(
                tied,
                far_pieces(c)[last:],
                q,
                wt,
                wd,
                acc["H"] if last else acc[c // 2],
                0 if last else (c % 2) * q,
                stats,
                c,
                acc["D"] if last else (),
            )
            es_t.append(e_t)
            es_d.append(e_d)
            result = e_t

    before, last, done = [], [], []
    for number, slot in enumerate(SLOTS):
        operands = [operand(name) for name in slot]
        for name, array in zip(slot, operands, strict=True):
            if before or done:
                array = lax.optimization_barrier((array, *before, *done))[0]
            got[name] = lax.ppermute(array, "tok" if name == "T" else "voc", PAIRS[name[0]])
        before = last + [got[name] for name in slot if name in EARLY]
        last, done = [got[name] for name in slot if name not in FREE + EARLY], []
        for name in WORK[number]:
            work(name)
            done = [result]
    for name in WORK[len(SLOTS)]:
        work(name)

    total = _all_reduce(stats, _merge_softmax)
    slope, scaled, sums = _slopes(es_t, es_d, stats, total, full)

    both = rest_of("S")
    arrays, plan = [], []

    def at(array, start, rows):
        arrays.append(array)
        return (len(arrays) - 1, start, rows)

    for k, (name, tail) in enumerate(((None, (both, 0)), ("P", (got["X"], 0)), ("O", (both, rest)), ("A", (got["X"], rest)))):
        if name is None:
            groups = [(g, 0) for g in own]
        elif name == "O":
            groups = [other_x(h) for h in range(2)]
        else:
            groups = [(got[f"{name}{h}"], 0) for h in range(2)]
        plan.append((k, [[at(*g, 2 * q)] for g in groups] + [[at(*tail, rest)]]))
    for k, (fars, side) in enumerate(((far, 0), (far, 1), ({c: got[f"F{c}"] for c in range(4)}, 0), ({c: got[f"F{c}"] for c in range(4)}, 1))):
        choices = [(got["Y"], (k // 2) * rest), (got["W"], (k // 2) * rest)]
        tail = [at(array, start, rest) for array, start in (choices if side == 0 else choices[::-1])]
        plan.append((4 + k, [[at(fars[c], side * q, q)] for c in range(4)] + [tail]))
    features = _turn(blocks, arrays, plan, rows_all)

    sums = _all_reduce(sums, jnp.add)
    grad, send = _send(tok_index, features, slope, scaled, sums, tokens, sizes, part)
    received = lax.ppermute(send, "tok", [(0, 1), (1, 0)])
    keep = _keep(tok_index, features, grad, tokens, part)
    row_loss = jnp.concatenate([sums[2 * i, :rows] for i, rows in enumerate(sizes)])
    return row_loss, _add(keep, received)


def _body_any(target_hidden, draft_hidden, target_head, draft_head):
    rows, vocab = target_hidden.shape[0], target_head.shape[1]
    full = float(vocab * lax.axis_size("voc"))
    tokens = float(rows * lax.axis_size("tok"))
    draft_weights = lax.all_gather(draft_head, "tok", axis=0, tiled=True)
    hidden = lax.all_gather(target_hidden, "voc", axis=1, tiled=True)
    target_logits = jnp.dot(hidden, target_head, preferred_element_type=F32)
    features = lax.all_gather(draft_hidden, "voc", axis=1, tiled=True)
    draft_logits = jnp.dot(features, draft_weights, preferred_element_type=F32)
    top_t, top_d = lax.pmax((jnp.max(target_logits, axis=1), jnp.max(draft_logits, axis=1)), "voc")
    target_exp = jnp.exp(target_logits - top_t[:, None])
    draft_exp = jnp.exp(draft_logits - top_d[:, None])
    total_t, total_d = lax.psum((jnp.sum(target_exp, axis=1), jnp.sum(draft_exp, axis=1)), "voc")
    target_prob = target_exp / total_t[:, None]
    draft_prob = draft_exp / total_d[:, None]
    spread = full * (draft_prob - target_prob)
    root = jnp.sqrt(spread * spread + 1.0)
    slope = spread / root
    loss = jnp.sum(root - 1.0, axis=1) / (2.0 * full)
    row_loss, inner = lax.psum((loss, jnp.sum(draft_prob * slope, axis=1)), "voc")
    logit_grad = (full * draft_prob * (slope - inner[:, None])).astype(BF16)
    summed = lax.dot_general(features, logit_grad, (((0,), (0,)), ((), ())), preferred_element_type=F32)
    draft_grad = lax.psum_scatter((summed / tokens).astype(BF16), "tok", scatter_dimension=0, tiled=True)
    return row_loss, draft_grad


def solution(mesh):
    body = _body_4x2 if (mesh.shape["voc"], mesh.shape["tok"]) == (8, 2) else _body_any
    return jax.shard_map(
        body,
        mesh=mesh,
        in_specs=(
            P(("grp", "tok"), "voc"),
            P(("grp", "tok"), "voc"),
            P(None, "voc"),
            P("tok", "voc"),
        ),
        out_specs=(P(("grp", "tok")), P(("grp", "tok"), "voc")),
        check_vma=False,
    )
```

time: 141 us -> 130 us (0.922)
  local copies, waits for them, and re-layouts: 15.2 us -> 2.02 us
  waiting for transfers between devices: 56.7 us -> 50.6 us
  other arithmetic: 2.05 us -> 5.03 us
  Pallas kernels: 29 us -> 31.3 us
  starting transfers between devices: 36.7 us -> 39 us
    unnamed x21 -> x5, local copies, waits for them, and re-layouts: 14.2 us -> 0.02 us
    ppermute x19 -> x23, waiting for transfers between devices: 44.3 us -> 38.3 us  [_body_4x2(): lax.ppermute(array, 'tok' if name == 'T' else 'voc', PAIRS[name[0]])]
    ppermute x19 -> x23, starting transfers between devices: 21.5 us -> 26.7 us  [_body_4x2(): lax.ppermute(array, 'tok' if name == 'T' else 'voc', PAIRS[name[0]])]
    concatenate x4 -> x5, other arithmetic: 1.75 us -> 4.73 us  [the longest x4 4.06 us: operand(): jnp.concatenate([h[index % 2 * q:index % 2 * q + q] for h in (own[index /...]
    ppermute x6, starting transfers between devices: 15.2 us -> 12.3 us  [_all_reduce(): x = merge(x, lax.ppermute(x, 'voc', _xor(k)))]
    pallas_call x14 -> x16, Pallas kernels: 29 us -> 31.3 us  [_kernel(): pl.pallas_call(body, in_specs=specs, out_specs=out_specs or [VMEM] * len(...]
  transfers between devices with their start and end apart: 26 -> 30, of which waited for: 14 -> 16; matrix products, arithmetic and copies ran while one was open for 2% -> 5% of each run, Pallas kernels for 13% -> 17%
where the time goes in v3:
time: 130 us; the launch traced here: 129 us
  waiting for transfers between devices  50.6 us (39%)
  starting transfers between devices  39 us (30%)
  Pallas kernels  31.3 us (24%)
  other arithmetic  5.03 us (4%)
  local copies, waits for them, and re-layouts  2.02 us (2%)
    ppermute x23, waiting for transfers between devices, _body_4x2(): lax.ppermute(array, 'tok' if name == 'T' else 'voc', PAIRS[name[0]])  38.3 us
    pallas_call x16, Pallas kernels, _kernel(): pl.pallas_call(body, in_specs=specs, out_specs=out_specs or [VMEM] * len(...  31.3 us
    ppermute x23, starting transfers between devices, _body_4x2(): lax.ppermute(array, 'tok' if name == 'T' else 'voc', PAIRS[name[0]])  26.7 us
    ppermute x6, starting transfers between devices, _all_reduce(): x = merge(x, lax.ppermute(x, 'voc', _xor(k)))  12.3 us
    ppermute x6, waiting for transfers between devices, _all_reduce(): x = merge(x, lax.ppermute(x, 'voc', _xor(k)))  11.5 us
    concatenate x4, other arithmetic, operand(): jnp.concatenate([h[index % 2 * q:index % 2 * q + q] for h in (own[index /...  4.06 us
  transfers between devices with their start and end apart: 30, of which 16 were waited for; matrix products, arithmetic and copies ran while one was open for 5% of the time, Pallas kernels for 17%

profile of v3, /device:TPU:0, one launch (start us, length us, event | category | flops | bytes accessed | tf_op | source)
XLA Modules:
  0.0 129.2 jit_solution(5540454631714899886)
XLA Ops:
  1.9 3.1 %collective-permute-start.1 = (bf16[352,640]{1,0:T(8,128)(2,1)S(1)}, bf16[352,640]{1,0:T(8,128)(2,1)S(1)}, u32[]{:S(2)}, u32[]{:S(2)}) collective-permute-start(bf16[352,640]{1,0:T(8,128)(2,1)S(1)} %get-tuple-element.57.refs_0_), channel_id=1, source_target_pairs={{0,4},{2,6},{4,0},{6,2},{8,12},{10,14},{12,8},{14,10},{1,5},{3,7},... | collective-permute-start | bytes 1351688 | tf_op jit(solution)/shard_map/ppermute | solution.py:494
  8.1 8.0 %collective-permute-done.1.refs_1_.refs_3_ = bf16[352,640]{1,0:T(8,128)(2,1)S(1)} collective-permute-done((bf16[352,640]{1,0:T(8,128)(2,1)S(1)}, bf16[352,640]{1,0:T(8,128)(2,1)S(1)}, u32[]{:S(2)}, u32[]{:S(2)}) %collective-permute-start.1) | collective-permute-done | bytes 450592 | tf_op jit(solution)/shard_map/ppermute | solution.py:494
  20.2 4.8 %collective-permute-done.4.refs_1_.refs_4_ = bf16[352,640]{1,0:T(8,128)(2,1)S(1)} collective-permute-done((bf16[352,640]{1,0:T(8,128)(2,1)S(1)}, bf16[352,640]{1,0:T(8,128)(2,1)S(1)}, u32[]{:S(2)}, u32[]{:S(2)}) %collective-permute-start.4) | collective-permute-done | bytes 450592 | tf_op jit(solution)/shard_map/ppermute | solution.py:494
  37.1 4.5 %collective-permute-done.5.refs_3_.refs_9_ = bf16[352,640]{1,0:T(8,128)(2,1)S(1)} collective-permute-done((bf16[352,640]{1,0:T(8,128)(2,1)S(1)}, bf16[352,640]{1,0:T(8,128)(2,1)S(1)}, u32[]{:S(2)}, u32[]{:S(2)}) %collective-permute-start.5) | collective-permute-done | bytes 450592 | tf_op jit(solution)/shard_map/ppermute | solution.py:494
  41.6 3.1 %logits.5 = (f32[352,1280]{1,0:T(8,128)S(1)}, f32[352,1280]{1,0:T(8,128)S(1)}) custom-call(s32[17]{0:T(128)S(1)} %stack.78.blocks, bf16[352,640]{1,0:T(8,128)(2,1)S(1)} %get-tuple-element.57.refs_0_, bf16[352,640]{1,0:T(8,128)(2,1)S(1)} %collective-permute-done.1.refs_1_.refs_3_, bf16[352,640]{1,0:T(8,128)(2,1)S(1)} %collective-permute-done.2.refs_2_.refs_6_, ...), custom_call_target="tpu_custom_call" | custom-call | flops 2306867200 | bytes 14909508 | tf_op jit(solution)/shard_map/logits/pallas_call | solution.py:23
  48.4 4.2 %collective-permute-done.12 = bf16[352,640]{1,0:T(8,128)(2,1)S(1)} collective-permute-done((bf16[352,640]{1,0:T(8,128)(2,1)S(1)}, bf16[352,640]{1,0:T(8,128)(2,1)S(1)}, u32[]{:S(2)}, u32[]{:S(2)}) %collective-permute-start.12) | collective-permute-done | bytes 450592 | tf_op jit(solution)/shard_map/ppermute | solution.py:494
  54.9 3.2 %logits.6 = (f32[352,1280]{1,0:T(8,128)S(1)}, f32[352,1280]{1,0:T(8,128)S(1)}) custom-call(s32[17]{0:T(128)S(1)} %stack.78.blocks, bf16[352,640]{1,0:T(8,128)(2,1)S(1)} %get-tuple-element.59.refs_0_.refs_1_, bf16[352,640]{1,0:T(8,128)(2,1)S(1)} %collective-permute-done.4.refs_1_.refs_4_, bf16[352,640]{1,0:T(8,128)(2,1)S(1)} %collective-permute-done.6.refs_2_.refs_7_, ...), custom_call_target="tpu_custom_call" | custom-call | flops 2306867200 | bytes 14909508 | tf_op jit(solution)/shard_map/logits/pallas_call | solution.py:23
  58.0 7.7 %collective-permute-done.17 = bf16[352,640]{1,0:T(8,128)(2,1)S(1)} collective-permute-done((bf16[352,640]{1,0:T(8,128)(2,1)S(1)}, bf16[352,640]{1,0:T(8,128)(2,1)S(1)}, u32[]{:S(2)}, u32[]{:S(2)}) %collective-permute-start.17) | collective-permute-done | bytes 450592 | tf_op jit(solution)/shard_map/ppermute | solution.py:494
  66.6 2.4 %exp_logits.4 = (f32[176,1280]{1,0:T(8,128)S(1)}, f32[176,1280]{1,0:T(8,128)S(1)}, f32[2,8,256]{2,1,0:T(8,128)S(1)}) custom-call(s32[17]{0:T(128)S(1)} %stack.78.blocks, bf16[352,640]{1,0:T(8,128)(2,1)S(1)} %broadcast_select_fusion.3.refs_0_.refs_14_.refs_20_, bf16[352,640]{1,0:T(8,128)(2,1)S(1)} %collective-permute-done.11.refs_1_.refs_26_.refs_32_, ...), custom_call_target="tpu_custom_call" | custom-call | flops 1153433600 | bytes 17629252 | tf_op jit(solution)/shard_map/exp_logits/pallas_call | solution.py:23
  69.0 6.8 %collective-permute-done.16 = bf16[352,640]{1,0:T(8,128)(2,1)S(1)} collective-permute-done((bf16[352,640]{1,0:T(8,128)(2,1)S(1)}, bf16[352,640]{1,0:T(8,128)(2,1)S(1)}, u32[]{:S(2)}, u32[]{:S(2)}) %collective-permute-start.16) | collective-permute-done | bytes 450592 | tf_op jit(solution)/shard_map/ppermute | solution.py:494
  78.6 2.5 %collective-permute-start.20 = (bf16[128,640]{1,0:T(8,128)(2,1)S(1)}, bf16[128,640]{1,0:T(8,128)(2,1)S(1)}, u32[]{:S(2)}, u32[]{:S(2)}) collective-permute-start(bf16[128,640]{1,0:T(8,128)(2,1)S(1)} %constant_dynamic-update-slice_fusion.refs_0_.refs_2_.refs_8_), channel_id=1, source_target_pairs={{0,8},{2,10},{4,12},{6,14},{8,0},{10,2},{12,4},{14,6},{1,9},{3,11}... | collective-permute-start | bytes 491528 | tf_op jit(solution)/shard_map/ppermute | solution.py:494
  81.2 2.5 %exp_logits.5 = (f32[176,1280]{1,0:T(8,128)S(1)}, f32[176,1280]{1,0:T(8,128)S(1)}, f32[2,8,256]{2,1,0:T(8,128)S(1)}) custom-call(s32[17]{0:T(128)S(1)} %stack.78.blocks, bf16[352,640]{1,0:T(8,128)(2,1)S(1)} %broadcast_select_fusion.2.refs_0_.refs_15_.refs_21_, bf16[352,640]{1,0:T(8,128)(2,1)S(1)} %collective-permute-done.14.refs_1_.refs_27_.refs_33_, ...), custom_call_target="tpu_custom_call" | custom-call | flops 1153433600 | bytes 17629252 | tf_op jit(solution)/shard_map/exp_logits/pallas_call | solution.py:23
  85.9 1.8 %logits.8 = (f32[64,1280]{1,0:T(8,128)S(1)}, f32[64,1280]{1,0:T(8,128)S(1)}) custom-call(s32[17]{0:T(128)S(1)} %stack.78.blocks, bf16[128,640]{1,0:T(8,128)(2,1)S(1)} %constant_dynamic-update-slice_fusion.refs_0_.refs_2_.refs_8_, bf16[128,640]{1,0:T(8,128)(2,1)S(1)} %collective-permute-done.18.refs_1_.refs_5_.refs_11_, bf16[4096,1280]{1,0:T(8,128)(2,1)S(1)} %copy-done, ...), custom_call_target="tpu_custom_call" | custom-call | flops 419430400 | bytes 13434948 | tf_op jit(solution)/shard_map/logits/pallas_call | solution.py:23
  87.7 2.4 %exp_logits.6 = (f32[176,1280]{1,0:T(8,128)S(1)}, f32[176,1280]{1,0:T(8,128)S(1)}, f32[2,8,256]{2,1,0:T(8,128)S(1)}) custom-call(s32[17]{0:T(128)S(1)} %stack.78.blocks, bf16[352,640]{1,0:T(8,128)(2,1)S(1)} %broadcast_select_fusion.refs_0_.refs_16_.refs_22_, bf16[352,640]{1,0:T(8,128)(2,1)S(1)} %collective-permute-done.19.refs_1_.refs_28_.refs_34_, ...), custom_call_target="tpu_custom_call" | custom-call | flops 1153433600 | bytes 17629252 | tf_op jit(solution)/shard_map/exp_logits/pallas_call | solution.py:23
  91.7 1.8 %logits.9 = (f32[64,1280]{1,0:T(8,128)S(1)}, f32[64,1280]{1,0:T(8,128)S(1)}) custom-call(s32[17]{0:T(128)S(1)} %stack.78.blocks, bf16[128,640]{1,0:T(8,128)(2,1)S(1)} %collective-permute-done.20.refs_0_.refs_12_.refs_19_.refs_24_.refs_31_, bf16[128,640]{1,0:T(8,128)(2,1)S(1)} %collective-permute-done.21.refs_1_.refs_13_.refs_18_.refs_25_.refs_30_, ...), custom_call_target="tpu_custom_call" | custom-call | flops 419430400 | bytes 14090308 | tf_op jit(solution)/shard_map/logits/pallas_call | solution.py:23
  93.5 2.0 %exp_logits.7 = (f32[240,1280]{1,0:T(8,128)S(1)}, f32[240,1280]{1,0:T(8,128)S(1)}, f32[2,8,256]{2,1,0:T(8,128)S(1)}) custom-call(s32[17]{0:T(128)S(1)} %stack.78.blocks, bf16[352,640]{1,0:T(8,128)(2,1)S(1)} %collective-permute-done.22.refs_0_.refs_29_.refs_35_, bf16[4096,1280]{1,0:T(8,128)(2,1)S(1)} %copy-done, ...), custom_call_target="tpu_custom_call" | custom-call | flops 576716800 | bytes 16031812 | tf_op jit(solution)/shard_map/exp_logits/pallas_call | solution.py:23
  96.5 2.9 %collective-permute-done.23 = f32[2,8,256]{2,1,0:T(8,128)S(1)} collective-permute-done((f32[2,8,256]{2,1,0:T(8,128)S(1)}, f32[2,8,256]{2,1,0:T(8,128)S(1)}, u32[]{:S(2)}, u32[]{:S(2)}) %collective-permute-start.23) | collective-permute-done | bytes 16416 | tf_op jit(solution)/shard_map/ppermute | solution.py:381
  99.4 2.6 %collective-permute-start.24 = (f32[2,8,256]{2,1,0:T(8,128)S(1)}, f32[2,8,256]{2,1,0:T(8,128)S(1)}, u32[]{:S(2)}, u32[]{:S(2)}) collective-permute-start(f32[2,8,256]{2,1,0:T(8,128)S(1)} %pad_maximum_fusion.4), channel_id=1, source_target_pairs={{0,4},{2,6},{4,0},{6,2},{8,12},{10,14},{12,8},{14,10},{1,5},{3,7},... | collective-permute-start | bytes 49160 | tf_op jit(solution)/shard_map/ppermute | solution.py:381
  103.7 3.0 %collective-permute-start.25 = (f32[2,8,256]{2,1,0:T(8,128)S(1)}, f32[2,8,256]{2,1,0:T(8,128)S(1)}, u32[]{:S(2)}, u32[]{:S(2)}) collective-permute-start(f32[2,8,256]{2,1,0:T(8,128)S(1)} %pad_maximum_fusion.5), channel_id=1, source_target_pairs={{0,8},{2,10},{4,12},{6,14},{8,0},{10,2},{12,4},{14,6},{1,9},{3,11}... | collective-permute-start | bytes 49160 | tf_op jit(solution)/shard_map/ppermute | solution.py:381
  106.7 1.7 %collective-permute-done.25 = f32[2,8,256]{2,1,0:T(8,128)S(1)} collective-permute-done((f32[2,8,256]{2,1,0:T(8,128)S(1)}, f32[2,8,256]{2,1,0:T(8,128)S(1)}, u32[]{:S(2)}, u32[]{:S(2)}) %collective-permute-start.25) | collective-permute-done | bytes 16416 | tf_op jit(solution)/shard_map/ppermute | solution.py:381
  108.4 2.9 %slopes.1 = (f32[768,1280]{1,0:T(8,128)S(1)}, f32[768,1280]{1,0:T(8,128)S(1)}, f32[8,256]{1,0:T(8,128)S(1)}) custom-call(f32[176,1280]{1,0:T(8,128)S(1)} %get-tuple-element.70.refs_0_, f32[176,1280]{1,0:T(8,128)S(1)} %get-tuple-element.76.refs_1_, f32[176,1280]{1,0:T(8,128)S(1)} %get-tuple-element.89.refs_2_, f32[240,1280]{1,0:T(8,128)S(1)} %get-tuple-element.99.refs_3_, ...), custom_call_target="tpu_custom_call" | custom-call | flops 11796480 | bytes 7897088 | tf_op jit(solution)/shard_map/slopes/pallas_call | solution.py:23
  112.1 2.9 %collective-permute-done.26 = f32[8,256]{1,0:T(8,128)S(1)} collective-permute-done((f32[8,256]{1,0:T(8,128)S(1)}, f32[8,256]{1,0:T(8,128)S(1)}, u32[]{:S(2)}, u32[]{:S(2)}) %collective-permute-start.26) | collective-permute-done | bytes 8224 | tf_op jit(solution)/shard_map/ppermute | solution.py:381
  115.0 2.0 %collective-permute-start.27 = (f32[8,256]{1,0:T(8,128)S(1)}, f32[8,256]{1,0:T(8,128)S(1)}, u32[]{:S(2)}, u32[]{:S(2)}) collective-permute-start(f32[8,256]{1,0:T(8,128)S(1)} %add.49), channel_id=1, source_target_pairs={{0,4},{2,6},{4,0},{6,2},{8,12},{10,14},{12,8},{14,10},{1,5},{3,7},... | collective-permute-start | bytes 24584 | tf_op jit(solution)/shard_map/ppermute | solution.py:381
  118.7 2.9 %collective-permute-start.28 = (f32[8,256]{1,0:T(8,128)S(1)}, f32[8,256]{1,0:T(8,128)S(1)}, u32[]{:S(2)}, u32[]{:S(2)}) collective-permute-start(f32[8,256]{1,0:T(8,128)S(1)} %add.50), channel_id=1, source_target_pairs={{0,8},{2,10},{4,12},{6,14},{8,0},{10,2},{12,4},{14,6},{1,9},{3,11}... | collective-permute-start | bytes 24584 | tf_op jit(solution)/shard_map/ppermute | solution.py:381
  (83 shorter events, 46.5 us)
Async XLA Ops:
  1.9 14.3 %collective-permute-start.1 = (bf16[352,640]{1,0:T(8,128)(2,1)S(1)}, bf16[352,640]{1,0:T(8,128)(2,1)S(1)}, u32[]{:S(2)}, u32[]{:S(2)}) collective-permute-start(bf16[352,640]{1,0:T(8,128)(2,1)S(1)} %get-tuple-element.57.refs_0_), channel_id=1, source_target_pairs={{0,4},{2,6},{4,0},{6,2},{8,12},{10,14},{12,8},{14,10},{1,5},{3,7},... | collective-permute-start | bytes 1351688 | tf_op jit(solution)/shard_map/ppermute | solution.py:494
  4.9 15.2 %collective-permute-start.2 = (bf16[352,640]{1,0:T(8,128)(2,1)S(1)}, bf16[352,640]{1,0:T(8,128)(2,1)S(1)}, u32[]{:S(2)}, u32[]{:S(2)}) collective-permute-start(bf16[352,640]{1,0:T(8,128)(2,1)S(1)} %get-tuple-element.57.refs_0_), channel_id=1, source_target_pairs={{0,2},{2,0},{4,6},{6,4},{8,10},{10,8},{12,14},{14,12},{1,3},{3,1},... | collective-permute-start | bytes 1351688 | tf_op jit(solution)/shard_map/ppermute | solution.py:494
  6.4 12.2 %collective-permute-start.3 = (bf16[64,640]{1,0:T(8,128)(2,1)S(1)}, bf16[64,640]{1,0:T(8,128)(2,1)}, u32[]{:S(2)}, u32[]{:S(2)}) collective-permute-start(bf16[64,640]{1,0:T(8,128)(2,1)S(1)} %get-tuple-element.58), channel_id=1, source_target_pairs={{0,2},{2,0},{4,6},{6,4},{8,10},{10,8},{12,14},{14,12},{1,3},{3,1},... | collective-permute-start | bytes 245768 | tf_op jit(solution)/shard_map/ppermute | solution.py:494
  7.0 18.0 %collective-permute-start.4 = (bf16[352,640]{1,0:T(8,128)(2,1)S(1)}, bf16[352,640]{1,0:T(8,128)(2,1)S(1)}, u32[]{:S(2)}, u32[]{:S(2)}) collective-permute-start(bf16[352,640]{1,0:T(8,128)(2,1)S(1)} %get-tuple-element.59.refs_0_.refs_1_), channel_id=1, source_target_pairs={{0,4},{2,6},{4,0},{6,2},{8,12},{10,14},{12,8},{14,10},{1,5},{3,7},... | collective-permute-start | bytes 1351688 | tf_op jit(solution)/shard_map/ppermute | solution.py:494
  7.1 27.7 %collective-permute-start = (bf16[448,1280]{1,0:T(8,128)(2,1)}, bf16[448,1280]{1,0:T(8,128)(2,1)}, u32[]{:S(2)}, u32[]{:S(2)}) collective-permute-start(bf16[448,1280]{1,0:T(8,128)(2,1)} %mine.1), channel_id=1, source_target_pairs={{0,1},{1,0},{2,3},{3,2},{4,5},{5,4},{6,7},{7,6},{8,9},{9,8},{10,11... | collective-permute-start | bytes 3440648 | tf_op jit(solution)/shard_map/ppermute | solution.py:494
  17.3 11.0 %collective-permute-start.7 = (bf16[352,640]{1,0:T(8,128)(2,1)S(1)}, bf16[352,640]{1,0:T(8,128)(2,1)S(1)}, u32[]{:S(2)}, u32[]{:S(2)}) collective-permute-start(bf16[352,640]{1,0:T(8,128)(2,1)S(1)} %pad_maximum_fusion), channel_id=1, source_target_pairs={{4,8},{8,4},{6,10},{10,6},{5,9},{9,5},{7,11},{11,7},{20,24},{24,20... | collective-permute-start | bytes 1351688 | tf_op jit(solution)/shard_map/ppermute | solution.py:494
  18.6 13.3 %collective-permute-start.6 = (bf16[352,640]{1,0:T(8,128)(2,1)S(1)}, bf16[352,640]{1,0:T(8,128)(2,1)S(1)}, u32[]{:S(2)}, u32[]{:S(2)}) collective-permute-start(bf16[352,640]{1,0:T(8,128)(2,1)S(1)} %get-tuple-element.59.refs_0_.refs_1_), channel_id=1, source_target_pairs={{0,2},{2,0},{4,6},{6,4},{8,10},{10,8},{12,14},{14,12},{1,3},{3,1},... | collective-permute-start | bytes 1351688 | tf_op jit(solution)/shard_map/ppermute | solution.py:494
  24.9 16.6 %collective-permute-start.5 = (bf16[352,640]{1,0:T(8,128)(2,1)S(1)}, bf16[352,640]{1,0:T(8,128)(2,1)S(1)}, u32[]{:S(2)}, u32[]{:S(2)}) collective-permute-start(bf16[352,640]{1,0:T(8,128)(2,1)S(1)} %collective-permute-done.1.refs_1_.refs_3_), channel_id=1, source_target_pairs={{0,2},{2,0},{4,6},{6,4},{8,10},{10,8},{12,14},{14,12},{1,3},{3,1},... | collective-permute-start | bytes 1351688 | tf_op jit(solution)/shard_map/ppermute | solution.py:494
  28.3 16.3 %collective-permute-start.9 = (bf16[352,640]{1,0:T(8,128)(2,1)S(1)}, bf16[352,640]{1,0:T(8,128)(2,1)S(1)}, u32[]{:S(2)}, u32[]{:S(2)}) collective-permute-start(bf16[352,640]{1,0:T(8,128)(2,1)S(1)} %collective-permute-done.7), channel_id=1, source_target_pairs={{4,0},{6,2},{8,12},{10,14},{5,1},{7,3},{9,13},{11,15},{20,16},{22,... | collective-permute-start | bytes 1351688 | tf_op jit(solution)/shard_map/ppermute | solution.py:494
  31.9 20.7 %collective-permute-start.8 = (bf16[352,640]{1,0:T(8,128)(2,1)S(1)}, bf16[352,640]{1,0:T(8,128)(2,1)S(1)}, u32[]{:S(2)}, u32[]{:S(2)}) collective-permute-start(bf16[352,640]{1,0:T(8,128)(2,1)S(1)} %collective-permute-done.4.refs_1_.refs_4_), channel_id=1, source_target_pairs={{0,2},{2,0},{4,6},{6,4},{8,10},{10,8},{12,14},{14,12},{1,3},{3,1},... | collective-permute-start | bytes 1351688 | tf_op jit(solution)/shard_map/ppermute | solution.py:494
  33.5 19.1 %collective-permute-start.12 = (bf16[352,640]{1,0:T(8,128)(2,1)S(1)}, bf16[352,640]{1,0:T(8,128)(2,1)S(1)}, u32[]{:S(2)}, u32[]{:S(2)}) collective-permute-start(bf16[352,640]{1,0:T(8,128)(2,1)S(1)} %collective-permute-done.10), channel_id=1, source_target_pairs={{4,0},{6,2},{8,12},{10,14},{5,1},{7,3},{9,13},{11,15},{20,16},{22,... | collective-permute-start | bytes 1351688 | tf_op jit(solution)/shard_map/ppermute | solution.py:494
  34.8 12.3 %collective-permute-start.13 = (bf16[352,640]{1,0:T(8,128)(2,1)S(1)}, bf16[352,640]{1,0:T(8,128)(2,1)S(1)}, u32[]{:S(2)}, u32[]{:S(2)}) collective-permute-start(bf16[352,640]{1,0:T(8,128)(2,1)S(1)} %pad_maximum_fusion.2), channel_id=1, source_target_pairs={{4,8},{8,4},{6,10},{10,6},{5,9},{9,5},{7,11},{11,7},{20,24},{24,20... | collective-permute-start | bytes 1351688 | tf_op jit(solution)/shard_map/ppermute | solution.py:494
  44.7 8.7 %collective-permute-start.15 = (bf16[352,640]{1,0:T(8,128)(2,1)S(1)}, bf16[352,640]{1,0:T(8,128)(2,1)S(1)}, u32[]{:S(2)}, u32[]{:S(2)}) collective-permute-start(bf16[352,640]{1,0:T(8,128)(2,1)S(1)} %pad_maximum_fusion.3), channel_id=1, source_target_pairs={{4,8},{8,4},{6,10},{10,6},{5,9},{9,5},{7,11},{11,7},{20,24},{24,20... | collective-permute-start | bytes 1351688 | tf_op jit(solution)/shard_map/ppermute | solution.py:494
  45.4 20.3 %collective-permute-start.11 = (bf16[352,640]{1,0:T(8,128)(2,1)S(1)}, bf16[352,640]{1,0:T(8,128)(2,1)S(1)}, u32[]{:S(2)}, u32[]{:S(2)}) collective-permute-start(bf16[352,640]{1,0:T(8,128)(2,1)S(1)} %broadcast_select_fusion.3.refs_0_.refs_14_.refs_20_), channel_id=1, source_target_pairs={{0,2},{2,0},{4,6},{6,4},{8,10},{10,8},{12,14},{14,12},{1,3},{3,1},... | collective-permute-start | bytes 1351688 | tf_op jit(solution)/shard_map/ppermute | solution.py:494
  47.1 18.6 %collective-permute-start.17 = (bf16[352,640]{1,0:T(8,128)(2,1)S(1)}, bf16[352,640]{1,0:T(8,128)(2,1)S(1)}, u32[]{:S(2)}, u32[]{:S(2)}) collective-permute-start(bf16[352,640]{1,0:T(8,128)(2,1)S(1)} %collective-permute-done.13), channel_id=1, source_target_pairs={{4,0},{6,2},{8,12},{10,14},{5,1},{7,3},{9,13},{11,15},{20,16},{22,... | collective-permute-start | bytes 1351688 | tf_op jit(solution)/shard_map/ppermute | solution.py:494
  52.6 23.2 %collective-permute-start.14 = (bf16[352,640]{1,0:T(8,128)(2,1)S(1)}, bf16[352,640]{1,0:T(8,128)(2,1)S(1)}, u32[]{:S(2)}, u32[]{:S(2)}) collective-permute-start(bf16[352,640]{1,0:T(8,128)(2,1)S(1)} %broadcast_select_fusion.2.refs_0_.refs_15_.refs_21_), channel_id=1, source_target_pairs={{0,2},{2,0},{4,6},{6,4},{8,10},{10,8},{12,14},{14,12},{1,3},{3,1},... | collective-permute-start | bytes 1351688 | tf_op jit(solution)/shard_map/ppermute | solution.py:494
  53.4 22.4 %collective-permute-start.16 = (bf16[352,640]{1,0:T(8,128)(2,1)S(1)}, bf16[352,640]{1,0:T(8,128)(2,1)S(1)}, u32[]{:S(2)}, u32[]{:S(2)}) collective-permute-start(bf16[352,640]{1,0:T(8,128)(2,1)S(1)} %collective-permute-done.15), channel_id=1, source_target_pairs={{4,0},{6,2},{8,12},{10,14},{5,1},{7,3},{9,13},{11,15},{20,16},{22,... | collective-permute-start | bytes 1351688 | tf_op jit(solution)/shard_map/ppermute | solution.py:494
  65.8 21.9 %collective-permute-start.19 = (bf16[352,640]{1,0:T(8,128)(2,1)S(1)}, bf16[352,640]{1,0:T(8,128)(2,1)S(1)}, u32[]{:S(2)}, u32[]{:S(2)}) collective-permute-start(bf16[352,640]{1,0:T(8,128)(2,1)S(1)} %broadcast_select_fusion.refs_0_.refs_16_.refs_22_), channel_id=1, source_target_pairs={{0,2},{2,0},{4,6},{6,4},{8,10},{10,8},{12,14},{14,12},{1,3},{3,1},... | collective-permute-start | bytes 1351688 | tf_op jit(solution)/shard_map/ppermute | solution.py:494
  75.8 17.6 %collective-permute-start.22 = (bf16[352,640]{1,0:T(8,128)(2,1)S(1)}, bf16[352,640]{1,0:T(8,128)(2,1)S(1)}, u32[]{:S(2)}, u32[]{:S(2)}) collective-permute-start(bf16[352,640]{1,0:T(8,128)(2,1)S(1)} %broadcast_select_fusion.1.refs_0_.refs_17_.refs_23_), channel_id=1, source_target_pairs={{0,2},{2,0},{4,6},{6,4},{8,10},{10,8},{12,14},{14,12},{1,3},{3,1},... | collective-permute-start | bytes 1351688 | tf_op jit(solution)/shard_map/ppermute | solution.py:494
  77.4 8.5 %collective-permute-start.18 = (bf16[128,640]{1,0:T(8,128)(2,1)S(1)}, bf16[128,640]{1,0:T(8,128)(2,1)S(1)}, u32[]{:S(2)}, u32[]{:S(2)}) collective-permute-start(bf16[128,640]{1,0:T(8,128)(2,1)S(1)} %constant_dynamic-update-slice_fusion.refs_0_.refs_2_.refs_8_), channel_id=1, source_target_pairs={{0,4},{2,6},{4,0},{6,2},{8,12},{10,14},{12,8},{14,10},{1,5},{3,7},... | collective-permute-start | bytes 491528 | tf_op jit(solution)/shard_map/ppermute | solution.py:494
  78.6 13.0 %collective-permute-start.20 = (bf16[128,640]{1,0:T(8,128)(2,1)S(1)}, bf16[128,640]{1,0:T(8,128)(2,1)S(1)}, u32[]{:S(2)}, u32[]{:S(2)}) collective-permute-start(bf16[128,640]{1,0:T(8,128)(2,1)S(1)} %constant_dynamic-update-slice_fusion.refs_0_.refs_2_.refs_8_), channel_id=1, source_target_pairs={{0,8},{2,10},{4,12},{6,14},{8,0},{10,2},{12,4},{14,6},{1,9},{3,11}... | collective-permute-start | bytes 491528 | tf_op jit(solution)/shard_map/ppermute | solution.py:494
  83.7 7.9 %collective-permute-start.21 = (bf16[128,640]{1,0:T(8,128)(2,1)S(1)}, bf16[128,640]{1,0:T(8,128)(2,1)S(1)}, u32[]{:S(2)}, u32[]{:S(2)}) collective-permute-start(bf16[128,640]{1,0:T(8,128)(2,1)S(1)} %constant_dynamic-update-slice_fusion.refs_0_.refs_2_.refs_8_), channel_id=1, source_target_pairs={{0,12},{2,14},{4,8},{6,10},{8,4},{10,6},{12,0},{14,2},{1,13},{3,15... | collective-permute-start | bytes 491528 | tf_op jit(solution)/shard_map/ppermute | solution.py:494
  103.7 4.7 %collective-permute-start.25 = (f32[2,8,256]{2,1,0:T(8,128)S(1)}, f32[2,8,256]{2,1,0:T(8,128)S(1)}, u32[]{:S(2)}, u32[]{:S(2)}) collective-permute-start(f32[2,8,256]{2,1,0:T(8,128)S(1)} %pad_maximum_fusion.5), channel_id=1, source_target_pairs={{0,8},{2,10},{4,12},{6,14},{8,0},{10,2},{12,4},{14,6},{1,9},{3,11}... | collective-permute-start | bytes 49160 | tf_op jit(solution)/shard_map/ppermute | solution.py:381
  118.7 4.5 %collective-permute-start.28 = (f32[8,256]{1,0:T(8,128)S(1)}, f32[8,256]{1,0:T(8,128)S(1)}, u32[]{:S(2)}, u32[]{:S(2)}) collective-permute-start(f32[8,256]{1,0:T(8,128)S(1)} %add.50), channel_id=1, source_target_pairs={{0,8},{2,10},{4,12},{6,14},{8,0},{10,2},{12,4},{14,6},{1,9},{3,11}... | collective-permute-start | bytes 24584 | tf_op jit(solution)/shard_map/ppermute | solution.py:381
  (8 other events, 76.5 us)

commit v4 on v3

--- a/solution.py
+++ b/solution.py
@@ -270,11 +270,11 @@
     )[0]
 
 
-def _gradient(features, which, grad, out, scale):
+def _gradient(features, which, grad, out, scale, first=0):
     part = out.shape[0] // 4
     half = features.shape[0] // 2
-    for c in _columns(grad.shape[1], 256):
-        product = _dot(features[_place(which, half), :], grad[:, c]) * scale
+    for c in _columns(out.shape[1], 256):
+        product = _dot(features[_place(which, half), :], grad[:, first + c.start : first + c.stop]) * scale
         for b in range(4):
             out[b * part : (b + 1) * part, c] = product[b * LANES : b * LANES + part].astype(out.dtype)
 
@@ -290,16 +290,32 @@
     _gradient(features, 1 - tok[0], grad, out, 1.0 / tokens)
 
 
-def _send(tok, features, slope, scaled, inner, tokens, sizes, part):
+def _send(tok, features, slope, scaled, inner, tokens, sizes, part, cols):
     rows_all, vocab = slope.shape
     return _kernel(
         functools.partial(_send_kernel, tokens, sizes),
-        [pltpu.VMEM((rows_all, vocab), BF16), pltpu.VMEM((part, vocab), BF16)],
+        [pltpu.VMEM((rows_all, vocab), BF16), pltpu.VMEM((part, cols), BF16)],
         [tok, features, slope, scaled, inner],
         "gradient_to_send",
         specs=[SMEM] + [VMEM] * 4,
-        flops=features.shape[0] * rows_all * vocab,
+        flops=features.shape[0] * rows_all * cols,
     )
+
+
+def _more_kernel(tokens, first, tok, features, grad, out):
+    _gradient(features, 1 - tok[0], grad, out, 1.0 / tokens, first)
+
+
+def _more(tok, features, grad, tokens, part, first):
+    rows_all, vocab = grad.shape
+    return _kernel(
+        functools.partial(_more_kernel, tokens, first),
+        [pltpu.VMEM((part, vocab - first), BF16)],
+        [tok, features, grad],
+        "more_to_send",
+        specs=[SMEM, VMEM, VMEM],
+        flops=features.shape[0] * rows_all * (vocab - first),
+    )[0]
 
 
 def _keep_kernel(tokens, tok, features, grad, out):
@@ -318,32 +334,28 @@
     )[0]
 
 
-def _add_kernel(keep, received, out, came, summed, came_sem, out_sem):
-    blocks, part = came.shape[:2]
-    place = lambda b: slice(b * part, (b + 1) * part)
-    fetch = [pltpu.make_async_copy(received.at[place(b), :], came.at[b], came_sem.at[b]) for b in range(blocks)]
-    store = [pltpu.make_async_copy(summed.at[b], out.at[place(b), :], out_sem.at[b]) for b in range(blocks)]
-    for copy in fetch:
-        copy.start()
-    for b in range(blocks):
-        fetch[b].wait()
-        summed[b] = (keep[place(b), :] + came[b].astype(F32)).astype(BF16)
-        store[b].start()
-    for copy in store:
+def _add_kernel(keep, low, high, out, summed, sems):
+    rows, first = low.shape
+    part = rows // 4
+    copies = []
+    for b in range(4):
+        here = slice(b * part, (b + 1) * part)
+        summed[here, :first] = (keep[here, :first] + low[here, :].astype(F32)).astype(BF16)
+        summed[here, first:] = (keep[here, first:] + high[here, :].astype(F32)).astype(BF16)
+        copies.append(pltpu.make_async_copy(summed.at[here, :], out.at[here, :], sems.at[b]))
+        copies[-1].start()
+    for copy in copies:
         copy.wait()
 
 
-def _add(keep, received):
-    rows, vocab = keep.shape
-    blocks = pltpu.VMEM((4, rows // 4, vocab), BF16)
+def _add(keep, low, high):
     return _kernel(
         _add_kernel,
         [jax.ShapeDtypeStruct(keep.shape, BF16)],
-        [keep, received],
+        [keep, low, high],
         "summed_gradient",
-        specs=[VMEM, ANYWHERE],
         out_specs=[ANYWHERE],
-        scratch=[blocks, blocks, pltpu.SemaphoreType.DMA((4,)), pltpu.SemaphoreType.DMA((4,))],
+        scratch=[pltpu.VMEM(keep.shape, BF16), pltpu.SemaphoreType.DMA((4,))],
         flops=keep.size,
     )[0]
 
@@ -362,7 +374,7 @@
 )
 FREE = ("T",)
 EARLY = ()
-WORK = ((), (), (), (), ("G", "N0",), ("N1",), ("E0",), ("E1", "H",), ("R", "E2", "D", "E3",))
+WORK = ((), (), (), (), ("G", "N0",), ("N1",), ("E0",), ("H", "E1",), ("R", "E2", "D", "E3",))
 
 
 def _xor(k):
@@ -525,11 +537,13 @@
     features = _turn(blocks, arrays, plan, rows_all)
 
     sums = _all_reduce(sums, jnp.add)
-    grad, send = _send(tok_index, features, slope, scaled, sums, tokens, sizes, part)
-    received = lax.ppermute(send, "tok", [(0, 1), (1, 0)])
+    cols = -(-vocab // 512) * 256
+    grad, low = _send(tok_index, features, slope, scaled, sums, tokens, sizes, part, cols)
+    low = lax.ppermute(low, "tok", PAIRS["T"])
+    high = lax.ppermute(_more(tok_index, features, grad, tokens, part, cols), "tok", PAIRS["T"])
     keep = _keep(tok_index, features, grad, tokens, part)
     row_loss = jnp.concatenate([sums[2 * i, :rows] for i, rows in enumerate(sizes)])
-    return row_loss, _add(keep, received)
+    return row_loss, _add(keep, low, high)
 
 
 def _body_any(target_hidden, draft_hidden, target_head, draft_head):

time: 130 us -> 128 us (0.985)
  waiting for transfers between devices: 50.6 us -> 47.7 us
    ppermute x23, waiting for transfers between devices: 38.3 us -> 34.4 us  [_body_4x2(): lax.ppermute(array, 'tok' if name == 'T' else 'voc', PAIRS[name[0]])]
    ppermute x23, starting transfers between devices: 26.7 us -> 29.3 us  [_body_4x2(): lax.ppermute(array, 'tok' if name == 'T' else 'voc', PAIRS[name[0]])]
    ppermute x6, starting transfers between devices: 12.3 us -> 10.2 us  [_all_reduce(): x = merge(x, lax.ppermute(x, 'voc', _xor(k)))]
    ppermute x6, waiting for transfers between devices: 11.5 us -> 13.2 us  [_all_reduce(): x = merge(x, lax.ppermute(x, 'voc', _xor(k)))]
    pallas_call x16 -> x17, Pallas kernels: 31.3 us -> 31.5 us  [_kernel(): pl.pallas_call(body, in_specs=specs, out_specs=out_specs or [VMEM] * len(...]
  transfers between devices with their start and end apart: 30 -> 31, of which waited for: 16 -> 14; matrix products, arithmetic and copies ran while one was open for 5% -> 5% of each run, Pallas kernels for 17% -> 18%
where the time goes in v4:
time: 128 us
  waiting for transfers between devices  47.7 us (37%)
  starting transfers between devices  40.2 us (31%)
  Pallas kernels  31.5 us (25%)
  other arithmetic  5.02 us (4%)
  local copies, waits for them, and re-layouts  2.02 us (2%)
    ppermute x23, waiting for transfers between devices, _body_4x2(): lax.ppermute(array, 'tok' if name == 'T' else 'voc', PAIRS[name[0]])  34.4 us
    pallas_call x17, Pallas kernels, _kernel(): pl.pallas_call(body, in_specs=specs, out_specs=out_specs or [VMEM] * len(...  31.5 us
    ppermute x23, starting transfers between devices, _body_4x2(): lax.ppermute(array, 'tok' if name == 'T' else 'voc', PAIRS[name[0]])  29.3 us
    ppermute x6, waiting for transfers between devices, _all_reduce(): x = merge(x, lax.ppermute(x, 'voc', _xor(k)))  13.2 us
    ppermute x6, starting transfers between devices, _all_reduce(): x = merge(x, lax.ppermute(x, 'voc', _xor(k)))  10.2 us
    concatenate x4, other arithmetic, operand(): jnp.concatenate([h[index % 2 * q:index % 2 * q + q] for h in (own[index /...  4.06 us
  transfers between devices with their start and end apart: 31, of which 14 were waited for; matrix products, arithmetic and copies ran while one was open for 5% of the time, Pallas kernels for 18%

profile of v4, /device:TPU:0, one launch (start us, length us, event | category | flops | bytes accessed | tf_op | source)
XLA Modules:
  0.0 127.6 jit_solution(13235635045943985270)
XLA Ops:
  1.9 3.1 %collective-permute-start.1 = (bf16[352,640]{1,0:T(8,128)(2,1)S(1)}, bf16[352,640]{1,0:T(8,128)(2,1)S(1)}, u32[]{:S(2)}, u32[]{:S(2)}) collective-permute-start(bf16[352,640]{1,0:T(8,128)(2,1)S(1)} %get-tuple-element.57.refs_0_), channel_id=1, source_target_pairs={{0,4},{2,6},{4,0},{6,2},{8,12},{10,14},{12,8},{14,10},{1,5},{3,7},... | collective-permute-start | bytes 1351688 | tf_op jit(solution)/shard_map/ppermute | solution.py:506
  8.1 8.0 %collective-permute-done.1.refs_1_.refs_3_ = bf16[352,640]{1,0:T(8,128)(2,1)S(1)} collective-permute-done((bf16[352,640]{1,0:T(8,128)(2,1)S(1)}, bf16[352,640]{1,0:T(8,128)(2,1)S(1)}, u32[]{:S(2)}, u32[]{:S(2)}) %collective-permute-start.1) | collective-permute-done | bytes 450592 | tf_op jit(solution)/shard_map/ppermute | solution.py:506
  20.2 4.8 %collective-permute-done.4.refs_1_.refs_4_ = bf16[352,640]{1,0:T(8,128)(2,1)S(1)} collective-permute-done((bf16[352,640]{1,0:T(8,128)(2,1)S(1)}, bf16[352,640]{1,0:T(8,128)(2,1)S(1)}, u32[]{:S(2)}, u32[]{:S(2)}) %collective-permute-start.4) | collective-permute-done | bytes 450592 | tf_op jit(solution)/shard_map/ppermute | solution.py:506
  37.1 4.5 %collective-permute-done.5.refs_3_.refs_9_ = bf16[352,640]{1,0:T(8,128)(2,1)S(1)} collective-permute-done((bf16[352,640]{1,0:T(8,128)(2,1)S(1)}, bf16[352,640]{1,0:T(8,128)(2,1)S(1)}, u32[]{:S(2)}, u32[]{:S(2)}) %collective-permute-start.5) | collective-permute-done | bytes 450592 | tf_op jit(solution)/shard_map/ppermute | solution.py:506
  41.6 3.1 %logits.5 = (f32[352,1280]{1,0:T(8,128)S(1)}, f32[352,1280]{1,0:T(8,128)S(1)}) custom-call(s32[17]{0:T(128)S(1)} %stack.78.blocks, bf16[352,640]{1,0:T(8,128)(2,1)S(1)} %get-tuple-element.57.refs_0_, bf16[352,640]{1,0:T(8,128)(2,1)S(1)} %collective-permute-done.1.refs_1_.refs_3_, bf16[352,640]{1,0:T(8,128)(2,1)S(1)} %collective-permute-done.2.refs_2_.refs_6_, ...), custom_call_target="tpu_custom_call" | custom-call | flops 2306867200 | bytes 14909508 | tf_op jit(solution)/shard_map/logits/pallas_call | solution.py:23
  48.4 7.5 %collective-permute-done.14 = bf16[352,640]{1,0:T(8,128)(2,1)S(1)} collective-permute-done((bf16[352,640]{1,0:T(8,128)(2,1)S(1)}, bf16[352,640]{1,0:T(8,128)(2,1)S(1)}, u32[]{:S(2)}, u32[]{:S(2)}) %collective-permute-start.14) | collective-permute-done | bytes 450592 | tf_op jit(solution)/shard_map/ppermute | solution.py:506
  58.5 3.2 %logits.6 = (f32[352,1280]{1,0:T(8,128)S(1)}, f32[352,1280]{1,0:T(8,128)S(1)}) custom-call(s32[17]{0:T(128)S(1)} %stack.78.blocks, bf16[352,640]{1,0:T(8,128)(2,1)S(1)} %get-tuple-element.59.refs_0_.refs_1_, bf16[352,640]{1,0:T(8,128)(2,1)S(1)} %collective-permute-done.4.refs_1_.refs_4_, bf16[352,640]{1,0:T(8,128)(2,1)S(1)} %collective-permute-done.6.refs_2_.refs_7_, ...), custom_call_target="tpu_custom_call" | custom-call | flops 2306867200 | bytes 14909508 | tf_op jit(solution)/shard_map/logits/pallas_call | solution.py:23
  61.6 4.8 %collective-permute-done.17 = bf16[352,640]{1,0:T(8,128)(2,1)S(1)} collective-permute-done((bf16[352,640]{1,0:T(8,128)(2,1)S(1)}, bf16[352,640]{1,0:T(8,128)(2,1)S(1)}, u32[]{:S(2)}, u32[]{:S(2)}) %collective-permute-start.17) | collective-permute-done | bytes 450592 | tf_op jit(solution)/shard_map/ppermute | solution.py:506
  68.1 2.5 %exp_logits.4 = (f32[176,1280]{1,0:T(8,128)S(1)}, f32[176,1280]{1,0:T(8,128)S(1)}, f32[2,8,256]{2,1,0:T(8,128)S(1)}) custom-call(s32[17]{0:T(128)S(1)} %stack.78.blocks, bf16[352,640]{1,0:T(8,128)(2,1)S(1)} %broadcast_select_fusion.3.refs_0_.refs_14_.refs_20_, bf16[352,640]{1,0:T(8,128)(2,1)S(1)} %collective-permute-done.11.refs_1_.refs_26_.refs_32_, ...), custom_call_target="tpu_custom_call" | custom-call | flops 1153433600 | bytes 17629252 | tf_op jit(solution)/shard_map/exp_logits/pallas_call | solution.py:23
  70.6 4.1 %collective-permute-done.15 = bf16[352,640]{1,0:T(8,128)(2,1)S(1)} collective-permute-done((bf16[352,640]{1,0:T(8,128)(2,1)S(1)}, bf16[352,640]{1,0:T(8,128)(2,1)S(1)}, u32[]{:S(2)}, u32[]{:S(2)}) %collective-permute-start.15) | collective-permute-done | bytes 450592 | tf_op jit(solution)/shard_map/ppermute | solution.py:506
  76.8 3.2 %collective-permute-start.18 = (bf16[128,640]{1,0:T(8,128)(2,1)S(1)}, bf16[128,640]{1,0:T(8,128)(2,1)S(1)}, u32[]{:S(2)}, u32[]{:S(2)}) collective-permute-start(bf16[128,640]{1,0:T(8,128)(2,1)S(1)} %constant_dynamic-update-slice_fusion.refs_0_.refs_2_.refs_8_), channel_id=1, source_target_pairs={{0,4},{2,6},{4,0},{6,2},{8,12},{10,14},{12,8},{14,10},{1,5},{3,7},... | collective-permute-start | bytes 491528 | tf_op jit(solution)/shard_map/ppermute | solution.py:506
  83.9 2.5 %exp_logits.5 = (f32[176,1280]{1,0:T(8,128)S(1)}, f32[176,1280]{1,0:T(8,128)S(1)}, f32[2,8,256]{2,1,0:T(8,128)S(1)}) custom-call(s32[17]{0:T(128)S(1)} %stack.78.blocks, bf16[352,640]{1,0:T(8,128)(2,1)S(1)} %broadcast_select_fusion.1.refs_0_.refs_15_.refs_21_, bf16[352,640]{1,0:T(8,128)(2,1)S(1)} %collective-permute-done.16.refs_1_.refs_27_.refs_33_, ...), custom_call_target="tpu_custom_call" | custom-call | flops 1153433600 | bytes 17629252 | tf_op jit(solution)/shard_map/exp_logits/pallas_call | solution.py:23
  86.4 1.8 %logits.8 = (f32[64,1280]{1,0:T(8,128)S(1)}, f32[64,1280]{1,0:T(8,128)S(1)}) custom-call(s32[17]{0:T(128)S(1)} %stack.78.blocks, bf16[128,640]{1,0:T(8,128)(2,1)S(1)} %constant_dynamic-update-slice_fusion.refs_0_.refs_2_.refs_8_, bf16[128,640]{1,0:T(8,128)(2,1)S(1)} %collective-permute-done.18.refs_1_.refs_5_.refs_11_, bf16[4096,1280]{1,0:T(8,128)(2,1)S(1)} %copy-done, ...), custom_call_target="tpu_custom_call" | custom-call | flops 419430400 | bytes 13434948 | tf_op jit(solution)/shard_map/logits/pallas_call | solution.py:23
  88.2 2.5 %exp_logits.6 = (f32[176,1280]{1,0:T(8,128)S(1)}, f32[176,1280]{1,0:T(8,128)S(1)}, f32[2,8,256]{2,1,0:T(8,128)S(1)}) custom-call(s32[17]{0:T(128)S(1)} %stack.78.blocks, bf16[352,640]{1,0:T(8,128)(2,1)S(1)} %broadcast_select_fusion.refs_0_.refs_16_.refs_22_, bf16[352,640]{1,0:T(8,128)(2,1)S(1)} %collective-permute-done.19.refs_1_.refs_28_.refs_34_, ...), custom_call_target="tpu_custom_call" | custom-call | flops 1153433600 | bytes 17629252 | tf_op jit(solution)/shard_map/exp_logits/pallas_call | solution.py:23
  90.7 1.8 %logits.9 = (f32[64,1280]{1,0:T(8,128)S(1)}, f32[64,1280]{1,0:T(8,128)S(1)}) custom-call(s32[17]{0:T(128)S(1)} %stack.78.blocks, bf16[128,640]{1,0:T(8,128)(2,1)S(1)} %collective-permute-done.20.refs_0_.refs_12_.refs_19_.refs_24_.refs_31_, bf16[128,640]{1,0:T(8,128)(2,1)S(1)} %collective-permute-done.21.refs_1_.refs_13_.refs_18_.refs_25_.refs_30_, ...), custom_call_target="tpu_custom_call" | custom-call | flops 419430400 | bytes 14090308 | tf_op jit(solution)/shard_map/logits/pallas_call | solution.py:23
  92.6 2.0 %exp_logits.7 = (f32[240,1280]{1,0:T(8,128)S(1)}, f32[240,1280]{1,0:T(8,128)S(1)}, f32[2,8,256]{2,1,0:T(8,128)S(1)}) custom-call(s32[17]{0:T(128)S(1)} %stack.78.blocks, bf16[352,640]{1,0:T(8,128)(2,1)S(1)} %collective-permute-done.22.refs_0_.refs_29_.refs_35_, bf16[4096,1280]{1,0:T(8,128)(2,1)S(1)} %copy-done, ...), custom_call_target="tpu_custom_call" | custom-call | flops 576716800 | bytes 16031812 | tf_op jit(solution)/shard_map/exp_logits/pallas_call | solution.py:23
  95.5 2.9 %collective-permute-done.23 = f32[2,8,256]{2,1,0:T(8,128)S(1)} collective-permute-done((f32[2,8,256]{2,1,0:T(8,128)S(1)}, f32[2,8,256]{2,1,0:T(8,128)S(1)}, u32[]{:S(2)}, u32[]{:S(2)}) %collective-permute-start.23) | collective-permute-done | bytes 16416 | tf_op jit(solution)/shard_map/ppermute | solution.py:393
  98.4 2.3 %collective-permute-start.24 = (f32[2,8,256]{2,1,0:T(8,128)S(1)}, f32[2,8,256]{2,1,0:T(8,128)S(1)}, u32[]{:S(2)}, u32[]{:S(2)}) collective-permute-start(f32[2,8,256]{2,1,0:T(8,128)S(1)} %pad_maximum_fusion.4), channel_id=1, source_target_pairs={{0,4},{2,6},{4,0},{6,2},{8,12},{10,14},{12,8},{14,10},{1,5},{3,7},... | collective-permute-start | bytes 49160 | tf_op jit(solution)/shard_map/ppermute | solution.py:393
  102.5 2.2 %collective-permute-start.25 = (f32[2,8,256]{2,1,0:T(8,128)S(1)}, f32[2,8,256]{2,1,0:T(8,128)S(1)}, u32[]{:S(2)}, u32[]{:S(2)}) collective-permute-start(f32[2,8,256]{2,1,0:T(8,128)S(1)} %pad_maximum_fusion.5), channel_id=1, source_target_pairs={{0,8},{2,10},{4,12},{6,14},{8,0},{10,2},{12,4},{14,6},{1,9},{3,11}... | collective-permute-start | bytes 49160 | tf_op jit(solution)/shard_map/ppermute | solution.py:393
  104.6 2.6 %collective-permute-done.25 = f32[2,8,256]{2,1,0:T(8,128)S(1)} collective-permute-done((f32[2,8,256]{2,1,0:T(8,128)S(1)}, f32[2,8,256]{2,1,0:T(8,128)S(1)}, u32[]{:S(2)}, u32[]{:S(2)}) %collective-permute-start.25) | collective-permute-done | bytes 16416 | tf_op jit(solution)/shard_map/ppermute | solution.py:393
  107.2 2.9 %slopes.1 = (f32[768,1280]{1,0:T(8,128)S(1)}, f32[768,1280]{1,0:T(8,128)S(1)}, f32[8,256]{1,0:T(8,128)S(1)}) custom-call(f32[176,1280]{1,0:T(8,128)S(1)} %get-tuple-element.70.refs_0_, f32[176,1280]{1,0:T(8,128)S(1)} %get-tuple-element.81.refs_1_, f32[176,1280]{1,0:T(8,128)S(1)} %get-tuple-element.89.refs_2_, f32[240,1280]{1,0:T(8,128)S(1)} %get-tuple-element.99.refs_3_, ...), custom_call_target="tpu_custom_call" | custom-call | flops 11796480 | bytes 7897088 | tf_op jit(solution)/shard_map/slopes/pallas_call | solution.py:23
  110.8 3.0 %collective-permute-done.26 = f32[8,256]{1,0:T(8,128)S(1)} collective-permute-done((f32[8,256]{1,0:T(8,128)S(1)}, f32[8,256]{1,0:T(8,128)S(1)}, u32[]{:S(2)}, u32[]{:S(2)}) %collective-permute-start.26) | collective-permute-done | bytes 8224 | tf_op jit(solution)/shard_map/ppermute | solution.py:393
  113.8 2.0 %collective-permute-start.27 = (f32[8,256]{1,0:T(8,128)S(1)}, f32[8,256]{1,0:T(8,128)S(1)}, u32[]{:S(2)}, u32[]{:S(2)}) collective-permute-start(f32[8,256]{1,0:T(8,128)S(1)} %add.49), channel_id=1, source_target_pairs={{0,4},{2,6},{4,0},{6,2},{8,12},{10,14},{12,8},{14,10},{1,5},{3,7},... | collective-permute-start | bytes 24584 | tf_op jit(solution)/shard_map/ppermute | solution.py:393
  117.5 2.1 %collective-permute-start.28 = (f32[8,256]{1,0:T(8,128)S(1)}, f32[8,256]{1,0:T(8,128)S(1)}, u32[]{:S(2)}, u32[]{:S(2)}) collective-permute-start(f32[8,256]{1,0:T(8,128)S(1)} %add.50), channel_id=1, source_target_pairs={{0,8},{2,10},{4,12},{6,14},{8,0},{10,2},{12,4},{14,6},{1,9},{3,11}... | collective-permute-start | bytes 24584 | tf_op jit(solution)/shard_map/ppermute | solution.py:393
  (86 shorter events, 47.2 us)
Async XLA Ops:
  1.9 14.3 %collective-permute-start.1 = (bf16[352,640]{1,0:T(8,128)(2,1)S(1)}, bf16[352,640]{1,0:T(8,128)(2,1)S(1)}, u32[]{:S(2)}, u32[]{:S(2)}) collective-permute-start(bf16[352,640]{1,0:T(8,128)(2,1)S(1)} %get-tuple-element.57.refs_0_), channel_id=1, source_target_pairs={{0,4},{2,6},{4,0},{6,2},{8,12},{10,14},{12,8},{14,10},{1,5},{3,7},... | collective-permute-start | bytes 1351688 | tf_op jit(solution)/shard_map/ppermute | solution.py:506
  4.9 15.2 %collective-permute-start.2 = (bf16[352,640]{1,0:T(8,128)(2,1)S(1)}, bf16[352,640]{1,0:T(8,128)(2,1)S(1)}, u32[]{:S(2)}, u32[]{:S(2)}) collective-permute-start(bf16[352,640]{1,0:T(8,128)(2,1)S(1)} %get-tuple-element.57.refs_0_), channel_id=1, source_target_pairs={{0,2},{2,0},{4,6},{6,4},{8,10},{10,8},{12,14},{14,12},{1,3},{3,1},... | collective-permute-start | bytes 1351688 | tf_op jit(solution)/shard_map/ppermute | solution.py:506
  6.4 12.2 %collective-permute-start.3 = (bf16[64,640]{1,0:T(8,128)(2,1)S(1)}, bf16[64,640]{1,0:T(8,128)(2,1)}, u32[]{:S(2)}, u32[]{:S(2)}) collective-permute-start(bf16[64,640]{1,0:T(8,128)(2,1)S(1)} %get-tuple-element.58), channel_id=1, source_target_pairs={{0,2},{2,0},{4,6},{6,4},{8,10},{10,8},{12,14},{14,12},{1,3},{3,1},... | collective-permute-start | bytes 245768 | tf_op jit(solution)/shard_map/ppermute | solution.py:506
  7.0 18.0 %collective-permute-start.4 = (bf16[352,640]{1,0:T(8,128)(2,1)S(1)}, bf16[352,640]{1,0:T(8,128)(2,1)S(1)}, u32[]{:S(2)}, u32[]{:S(2)}) collective-permute-start(bf16[352,640]{1,0:T(8,128)(2,1)S(1)} %get-tuple-element.59.refs_0_.refs_1_), channel_id=1, source_target_pairs={{0,4},{2,6},{4,0},{6,2},{8,12},{10,14},{12,8},{14,10},{1,5},{3,7},... | collective-permute-start | bytes 1351688 | tf_op jit(solution)/shard_map/ppermute | solution.py:506
  7.1 27.1 %collective-permute-start = (bf16[448,1280]{1,0:T(8,128)(2,1)}, bf16[448,1280]{1,0:T(8,128)(2,1)}, u32[]{:S(2)}, u32[]{:S(2)}) collective-permute-start(bf16[448,1280]{1,0:T(8,128)(2,1)} %mine.1), channel_id=1, source_target_pairs={{0,1},{1,0},{2,3},{3,2},{4,5},{5,4},{6,7},{7,6},{8,9},{9,8},{10,11... | collective-permute-start | bytes 3440648 | tf_op jit(solution)/shard_map/ppermute | solution.py:506
  17.3 11.0 %collective-permute-start.7 = (bf16[352,640]{1,0:T(8,128)(2,1)S(1)}, bf16[352,640]{1,0:T(8,128)(2,1)S(1)}, u32[]{:S(2)}, u32[]{:S(2)}) collective-permute-start(bf16[352,640]{1,0:T(8,128)(2,1)S(1)} %pad_maximum_fusion), channel_id=1, source_target_pairs={{4,8},{8,4},{6,10},{10,6},{5,9},{9,5},{7,11},{11,7},{20,24},{24,20... | collective-permute-start | bytes 1351688 | tf_op jit(solution)/shard_map/ppermute | solution.py:506
  18.6 13.3 %collective-permute-start.6 = (bf16[352,640]{1,0:T(8,128)(2,1)S(1)}, bf16[352,640]{1,0:T(8,128)(2,1)S(1)}, u32[]{:S(2)}, u32[]{:S(2)}) collective-permute-start(bf16[352,640]{1,0:T(8,128)(2,1)S(1)} %get-tuple-element.59.refs_0_.refs_1_), channel_id=1, source_target_pairs={{0,2},{2,0},{4,6},{6,4},{8,10},{10,8},{12,14},{14,12},{1,3},{3,1},... | collective-permute-start | bytes 1351688 | tf_op jit(solution)/shard_map/ppermute | solution.py:506
  24.9 16.6 %collective-permute-start.5 = (bf16[352,640]{1,0:T(8,128)(2,1)S(1)}, bf16[352,640]{1,0:T(8,128)(2,1)S(1)}, u32[]{:S(2)}, u32[]{:S(2)}) collective-permute-start(bf16[352,640]{1,0:T(8,128)(2,1)S(1)} %collective-permute-done.1.refs_1_.refs_3_), channel_id=1, source_target_pairs={{0,2},{2,0},{4,6},{6,4},{8,10},{10,8},{12,14},{14,12},{1,3},{3,1},... | collective-permute-start | bytes 1351688 | tf_op jit(solution)/shard_map/ppermute | solution.py:506
  28.3 16.4 %collective-permute-start.9 = (bf16[352,640]{1,0:T(8,128)(2,1)S(1)}, bf16[352,640]{1,0:T(8,128)(2,1)S(1)}, u32[]{:S(2)}, u32[]{:S(2)}) collective-permute-start(bf16[352,640]{1,0:T(8,128)(2,1)S(1)} %collective-permute-done.7), channel_id=1, source_target_pairs={{4,0},{6,2},{8,12},{10,14},{5,1},{7,3},{9,13},{11,15},{20,16},{22,... | collective-permute-start | bytes 1351688 | tf_op jit(solution)/shard_map/ppermute | solution.py:506
  31.9 24.1 %collective-permute-start.8 = (bf16[352,640]{1,0:T(8,128)(2,1)S(1)}, bf16[352,640]{1,0:T(8,128)(2,1)S(1)}, u32[]{:S(2)}, u32[]{:S(2)}) collective-permute-start(bf16[352,640]{1,0:T(8,128)(2,1)S(1)} %collective-permute-done.4.refs_1_.refs_4_), channel_id=1, source_target_pairs={{0,2},{2,0},{4,6},{6,4},{8,10},{10,8},{12,14},{14,12},{1,3},{3,1},... | collective-permute-start | bytes 1351688 | tf_op jit(solution)/shard_map/ppermute | solution.py:506
  33.5 13.6 %collective-permute-start.13 = (bf16[352,640]{1,0:T(8,128)(2,1)S(1)}, bf16[352,640]{1,0:T(8,128)(2,1)S(1)}, u32[]{:S(2)}, u32[]{:S(2)}) collective-permute-start(bf16[352,640]{1,0:T(8,128)(2,1)S(1)} %pad_maximum_fusion.3), channel_id=1, source_target_pairs={{4,8},{8,4},{6,10},{10,6},{5,9},{9,5},{7,11},{11,7},{20,24},{24,20... | collective-permute-start | bytes 1351688 | tf_op jit(solution)/shard_map/ppermute | solution.py:506
  34.2 21.7 %collective-permute-start.14 = (bf16[352,640]{1,0:T(8,128)(2,1)S(1)}, bf16[352,640]{1,0:T(8,128)(2,1)S(1)}, u32[]{:S(2)}, u32[]{:S(2)}) collective-permute-start(bf16[352,640]{1,0:T(8,128)(2,1)S(1)} %collective-permute-done.10), channel_id=1, source_target_pairs={{4,0},{6,2},{8,12},{10,14},{5,1},{7,3},{9,13},{11,15},{20,16},{22,... | collective-permute-start | bytes 1351688 | tf_op jit(solution)/shard_map/ppermute | solution.py:506
  44.7 12.3 %collective-permute-start.12 = (bf16[352,640]{1,0:T(8,128)(2,1)S(1)}, bf16[352,640]{1,0:T(8,128)(2,1)S(1)}, u32[]{:S(2)}, u32[]{:S(2)}) collective-permute-start(bf16[352,640]{1,0:T(8,128)(2,1)S(1)} %pad_maximum_fusion.2), channel_id=1, source_target_pairs={{4,8},{8,4},{6,10},{10,6},{5,9},{9,5},{7,11},{11,7},{20,24},{24,20... | collective-permute-start | bytes 1351688 | tf_op jit(solution)/shard_map/ppermute | solution.py:506
  45.5 21.0 %collective-permute-start.11 = (bf16[352,640]{1,0:T(8,128)(2,1)S(1)}, bf16[352,640]{1,0:T(8,128)(2,1)S(1)}, u32[]{:S(2)}, u32[]{:S(2)}) collective-permute-start(bf16[352,640]{1,0:T(8,128)(2,1)S(1)} %broadcast_select_fusion.3.refs_0_.refs_14_.refs_20_), channel_id=1, source_target_pairs={{0,2},{2,0},{4,6},{6,4},{8,10},{10,8},{12,14},{14,12},{1,3},{3,1},... | collective-permute-start | bytes 1351688 | tf_op jit(solution)/shard_map/ppermute | solution.py:506
  47.1 19.3 %collective-permute-start.17 = (bf16[352,640]{1,0:T(8,128)(2,1)S(1)}, bf16[352,640]{1,0:T(8,128)(2,1)S(1)}, u32[]{:S(2)}, u32[]{:S(2)}) collective-permute-start(bf16[352,640]{1,0:T(8,128)(2,1)S(1)} %collective-permute-done.13), channel_id=1, source_target_pairs={{4,0},{6,2},{8,12},{10,14},{5,1},{7,3},{9,13},{11,15},{20,16},{22,... | collective-permute-start | bytes 1351688 | tf_op jit(solution)/shard_map/ppermute | solution.py:506
  56.0 18.8 %collective-permute-start.16 = (bf16[352,640]{1,0:T(8,128)(2,1)S(1)}, bf16[352,640]{1,0:T(8,128)(2,1)S(1)}, u32[]{:S(2)}, u32[]{:S(2)}) collective-permute-start(bf16[352,640]{1,0:T(8,128)(2,1)S(1)} %broadcast_select_fusion.1.refs_0_.refs_15_.refs_21_), channel_id=1, source_target_pairs={{0,2},{2,0},{4,6},{6,4},{8,10},{10,8},{12,14},{14,12},{1,3},{3,1},... | collective-permute-start | bytes 1351688 | tf_op jit(solution)/shard_map/ppermute | solution.py:506
  57.0 17.7 %collective-permute-start.15 = (bf16[352,640]{1,0:T(8,128)(2,1)S(1)}, bf16[352,640]{1,0:T(8,128)(2,1)S(1)}, u32[]{:S(2)}, u32[]{:S(2)}) collective-permute-start(bf16[352,640]{1,0:T(8,128)(2,1)S(1)} %collective-permute-done.12), channel_id=1, source_target_pairs={{4,0},{6,2},{8,12},{10,14},{5,1},{7,3},{9,13},{11,15},{20,16},{22,... | collective-permute-start | bytes 1351688 | tf_op jit(solution)/shard_map/ppermute | solution.py:506
  66.5 21.7 %collective-permute-start.19 = (bf16[352,640]{1,0:T(8,128)(2,1)S(1)}, bf16[352,640]{1,0:T(8,128)(2,1)S(1)}, u32[]{:S(2)}, u32[]{:S(2)}) collective-permute-start(bf16[352,640]{1,0:T(8,128)(2,1)S(1)} %broadcast_select_fusion.refs_0_.refs_16_.refs_22_), channel_id=1, source_target_pairs={{0,2},{2,0},{4,6},{6,4},{8,10},{10,8},{12,14},{14,12},{1,3},{3,1},... | collective-permute-start | bytes 1351688 | tf_op jit(solution)/shard_map/ppermute | solution.py:506
  74.8 17.8 %collective-permute-start.22 = (bf16[352,640]{1,0:T(8,128)(2,1)S(1)}, bf16[352,640]{1,0:T(8,128)(2,1)S(1)}, u32[]{:S(2)}, u32[]{:S(2)}) collective-permute-start(bf16[352,640]{1,0:T(8,128)(2,1)S(1)} %broadcast_select_fusion.2.refs_0_.refs_17_.refs_23_), channel_id=1, source_target_pairs={{0,2},{2,0},{4,6},{6,4},{8,10},{10,8},{12,14},{14,12},{1,3},{3,1},... | collective-permute-start | bytes 1351688 | tf_op jit(solution)/shard_map/ppermute | solution.py:506
  76.8 9.5 %collective-permute-start.18 = (bf16[128,640]{1,0:T(8,128)(2,1)S(1)}, bf16[128,640]{1,0:T(8,128)(2,1)S(1)}, u32[]{:S(2)}, u32[]{:S(2)}) collective-permute-start(bf16[128,640]{1,0:T(8,128)(2,1)S(1)} %constant_dynamic-update-slice_fusion.refs_0_.refs_2_.refs_8_), channel_id=1, source_target_pairs={{0,4},{2,6},{4,0},{6,2},{8,12},{10,14},{12,8},{14,10},{1,5},{3,7},... | collective-permute-start | bytes 491528 | tf_op jit(solution)/shard_map/ppermute | solution.py:506
  80.0 10.7 %collective-permute-start.20 = (bf16[128,640]{1,0:T(8,128)(2,1)S(1)}, bf16[128,640]{1,0:T(8,128)(2,1)S(1)}, u32[]{:S(2)}, u32[]{:S(2)}) collective-permute-start(bf16[128,640]{1,0:T(8,128)(2,1)S(1)} %constant_dynamic-update-slice_fusion.refs_0_.refs_2_.refs_8_), channel_id=1, source_target_pairs={{0,8},{2,10},{4,12},{6,14},{8,0},{10,2},{12,4},{14,6},{1,9},{3,11}... | collective-permute-start | bytes 491528 | tf_op jit(solution)/shard_map/ppermute | solution.py:506
  81.1 9.6 %collective-permute-start.21 = (bf16[128,640]{1,0:T(8,128)(2,1)S(1)}, bf16[128,640]{1,0:T(8,128)(2,1)S(1)}, u32[]{:S(2)}, u32[]{:S(2)}) collective-permute-start(bf16[128,640]{1,0:T(8,128)(2,1)S(1)} %constant_dynamic-update-slice_fusion.refs_0_.refs_2_.refs_8_), channel_id=1, source_target_pairs={{0,12},{2,14},{4,8},{6,10},{8,4},{10,6},{12,0},{14,2},{1,13},{3,15... | collective-permute-start | bytes 491528 | tf_op jit(solution)/shard_map/ppermute | solution.py:506
  102.5 4.7 %collective-permute-start.25 = (f32[2,8,256]{2,1,0:T(8,128)S(1)}, f32[2,8,256]{2,1,0:T(8,128)S(1)}, u32[]{:S(2)}, u32[]{:S(2)}) collective-permute-start(f32[2,8,256]{2,1,0:T(8,128)S(1)} %pad_maximum_fusion.5), channel_id=1, source_target_pairs={{0,8},{2,10},{4,12},{6,14},{8,0},{10,2},{12,4},{14,6},{1,9},{3,11}... | collective-permute-start | bytes 49160 | tf_op jit(solution)/shard_map/ppermute | solution.py:393
  117.5 4.5 %collective-permute-start.28 = (f32[8,256]{1,0:T(8,128)S(1)}, f32[8,256]{1,0:T(8,128)S(1)}, u32[]{:S(2)}, u32[]{:S(2)}) collective-permute-start(f32[8,256]{1,0:T(8,128)S(1)} %add.50), channel_id=1, source_target_pairs={{0,8},{2,10},{4,12},{6,14},{8,0},{10,2},{12,4},{14,6},{1,9},{3,11}... | collective-permute-start | bytes 24584 | tf_op jit(solution)/shard_map/ppermute | solution.py:393
  (9 other events, 78.9 us)
